TPU v7x, 256 devices: a whole 4x4x8 slice. The times are simulated.
256 devices in a mesh: batch: 8 (over y, z_lo), feat: 32 (over x, z_hi, core).
Axes of the slice: x: 4, y: 4, z: 8 (z_hi: 4, z_lo: 2; z = z_hi * 2 + z_lo), core: 2. Of those that a mesh axis runs over, the one named last changes fastest.
Arguments:
- view_a: bfloat16 [2560, 16384], P('batch', 'feat'), may hold values from -40 to 40
- view_b: bfloat16 [2560, 16384], P('batch', 'feat'), may hold values from -40 to 40
Outputs:
- loss: float32 [], replicated
- grad_a: float32 [2560, 16384], P('batch', 'feat')
- grad_b: float32 [2560, 16384], P('batch', 'feat')
All inputs are finite; a program needn't handle non-finite values.
Results may differ from a plain program's by a relative error of at most 0.003.
Values may be sent and summed in bfloat16 or wider, within the bound.
No kernel may reach another device: no remote copies, remote signals or barrier semaphores. Data moves between devices by JAX's collectives and lax.ppermute only.
A program may use at most 64 MiB of HBM per device.

v0:
```python
import functools

import jax
import jax.numpy as jnp
from jax import lax
from jax.experimental import pallas as pl
from jax.experimental.pallas import tpu as pltpu
from jax.sharding import Mesh, PartitionSpec as P

off_weight = 0.0051
norm_eps = 1e-05
f32, bf16 = jnp.float32, jnp.bfloat16
names = ("y", "zl", "x", "zh", "core")
sizes = (4, 2, 4, 4, 2)
batch = ("y", "zl")
like = jax.ShapeDtypeStruct
chunk = 80
low = 48


def from_axis(v, axis, k):
    return lax.ppermute(v, axis, [((i + k) % 4, i) for i in range(4)])


def from_pair(v, axis):
    return lax.ppermute(v, axis, [(1, 0), (0, 1)])


def inner(left, right):
    return lax.dot_general(left, right, (((1,), (1,)), ((), ())), preferred_element_type=f32)


def fold(v):
    return jnp.sum(v.reshape(v.shape[0] // 8, 8, v.shape[1]), 0)


def add_stats(block, shift, acc):
    def step(j, acc):
        d = block[pl.ds(pl.multiple_of(j * chunk, chunk), chunk), :].astype(f32) - shift
        return acc[0] + fold(d), acc[1] + fold(d * d)

    return lax.fori_loop(0, block.shape[0] // chunk, step, acc)


def stats_kernel(own, *refs):
    blocks, (st, known) = refs[:-2], refs[-2:]
    rows, full = own.shape

    def step(j, acc):
        return acc + fold(own[pl.ds(pl.multiple_of(j * chunk, chunk), chunk), :].astype(f32))

    total = lax.fori_loop(0, rows // chunk, step, jnp.zeros((8, full), f32))
    shift = jnp.sum(total, 0, keepdims=True) / rows
    acc = (jnp.zeros((8, full), f32), jnp.zeros((8, full), f32))
    start = 0
    for b in (own, *blocks):
        known[start : start + b.shape[0], :] = b[...]
        acc = add_stats(b, shift, acc)
        start += b.shape[0]
    st[0:8, :], st[8:16, :] = acc
    st[16:24, :] = jnp.broadcast_to(shift, (8, full))


def norm_kernel(images, idx, st, known, *refs):
    blocks, (n, no, inv_ref, p2lo, p2hi), (raw, sems) = refs[:-7], refs[-7:-2], refs[-2:]
    full = raw.shape[1]
    width, rows, first = full // 2, images // 8, known.shape[0]
    starts = [sum(b.shape[0] for b in blocks[:i]) for i in range(len(blocks))]
    copies = [
        pltpu.make_async_copy(b, raw.at[pl.ds(at, b.shape[0]), :], sems.at[i])
        for i, (b, at) in enumerate(zip(blocks, starts))
    ]
    for copy in copies:
        copy.start()
    shift = st[16:17, :]
    acc = (st[0:8, :], st[8:16, :])
    for b, at, copy in zip(blocks, starts, copies):
        copy.wait()
        acc = add_stats(raw.at[pl.ds(at, b.shape[0]), :], shift, acc)
    moved = jnp.sum(acc[0], 0, keepdims=True) / images
    inv = lax.rsqrt(jnp.sum(acc[1], 0, keepdims=True) / images - moved * moved + norm_eps)
    mean = shift + moved
    inv_ref[...] = jnp.broadcast_to(inv, (8, full))
    for src, start in ((known, 0), (raw, first)):

        def step(j, carry, src=src, start=start):
            v = src[pl.ds(pl.multiple_of(j * chunk, chunk), chunk), :].astype(f32)
            v = ((v - mean) * inv).astype(bf16)
            at = pl.ds(pl.multiple_of(start + j * chunk, chunk), chunk)
            n[at, :] = v
            no[at, :] = v[:, width:]
            return carry

        lax.fori_loop(0, src.shape[0] // chunk, step, 0)
    rx = rows // 4
    left = n[pl.ds(pl.multiple_of(lax.rem(idx[0] + 2, 4) * rx, rx), rx), :]
    for at in range(0, images, 640):
        cols = slice(at, at + 640)
        v = inner(left, n[cols, :]).astype(bf16)
        p2lo[:, cols] = v[:low, :]
        p2hi[:, cols] = v[low:, :]


def gram_kernel(idx, n, p0, p1lo, p1hi, p3lo, p3hi, part):
    rows, images = part.shape
    for at in range(0, images, 640):
        cols = slice(at, at + 640)
        part[:, cols] = inner(n[0:rows, :], n[cols, :]).astype(bf16)
    rx = rows // 4
    at = [pl.multiple_of(lax.rem(idx[0] + k, 4) * rx, rx) for k in range(4)]
    p0[...] = part[pl.ds(at[0], rx), :]
    for k, lo, hi in ((1, p1lo, p1hi), (3, p3lo, p3hi)):
        lo[...] = part[pl.ds(at[k], low), :]
        hi[...] = part[pl.ds(pl.multiple_of(at[k] + low, 16), rx - low), :]


def add_kernel(p1lo, a, p3hi, b, e, f):
    e[...] = (p1lo[...].astype(f32) + a[...].astype(f32)).astype(bf16)
    f[...] = (p3hi[...].astype(f32) + b[...].astype(f32)).astype(bf16)


def diag_kernel(images, n, o, inv_o, diag, my_own, o_own, inv_other):
    width = o.shape[1]
    zero = jnp.zeros((8, width), f32)

    def step(j, acc):
        at = pl.ds(pl.multiple_of(j * chunk, chunk), chunk)
        my, other = n[at, :width].astype(f32), o[at, :].astype(f32)
        return acc[0] + fold(my * other), acc[1] + fold(my), acc[2] + fold(other)

    acc = lax.fori_loop(0, images // chunk, step, (zero, zero, zero))
    sums = [jnp.sum(v, 0, keepdims=True) for v in acc]
    diag[...] = jnp.concatenate([sums[0] / images, *sums[1:], zero[0:5, :]], 0)
    my_own[...] = n[0 : my_own.shape[0], :width]
    o_own[...] = o[0 : o_own.shape[0], :]
    inv_other[...] = inv_o[...]


def sum_x_kernel(idx, p0, d, e, c, f, q0, q1, q2, q3, total):
    for k in range(4):
        cols = slice(k * 640, k * 640 + 640)
        up = p0[0:low, cols].astype(f32) + d[:, cols].astype(f32) + e[:, cols].astype(f32)
        down = p0[low:, cols].astype(f32) + c[:, cols].astype(f32) + f[:, cols].astype(f32)
        total[k, 0:low, :] = up.astype(bf16)
        total[k, low:, :] = down.astype(bf16)
    for k, q in enumerate((q0, q1, q2, q3)):
        q[...] = total[lax.rem(idx[1] + k, 4)]


def sum_z_kernel(q0, r1, r2, r3, mine):
    v = q0[...].astype(f32) + r1[...].astype(f32) + r2[...].astype(f32) + r3[...].astype(f32)
    mine[...] = v.astype(bf16)


def scalar_lanes(s, rows):
    hi = s.astype(bf16).astype(f32)
    mid = (s - hi).astype(bf16).astype(f32)
    lo = s - hi - mid
    lane = lax.broadcasted_iota(jnp.int32, (rows, 128), 1)
    return jnp.where(lane == 0, hi, jnp.where(lane == 1, mid, jnp.where(lane == 2, lo, 0.0))).astype(bf16)


def load_kernel(images, mine, theirs, diag, pay):
    rx, cw = theirs.shape
    off = jnp.sum(jnp.sum(mine[...].astype(f32) * theirs[...].astype(f32), 0, keepdims=True), 1, keepdims=True)
    c = diag[0:1, :]
    total = jnp.sum((1.0 - c) * (1.0 - c) - off_weight * c * c, 1, keepdims=True)
    part = total / 8 + 0.5 * off_weight * (off / (images * images))
    pay[:, :cw] = theirs[...]
    pay[:, cw:] = scalar_lanes(part, rx)


def lane_sum(ref, width):
    return jnp.sum(ref[0:8, width:].astype(f32)[0:1, :], 1, keepdims=True)


def join_kernel(idx, own, r1, r3, r2lo, r2hi, pay):
    rx, cw, low = own.shape[0], own.shape[1] - 128, r2lo.shape[0]
    part = jnp.zeros((1, 1), f32)
    at = [pl.multiple_of(lax.rem(idx[1] + k, 4) * cw, 128) for k in range(4)]
    for k, r in ((0, own), (3, r1), (1, r3)):
        pay[:, pl.ds(at[k], cw)] = r[:, :cw]
        part = part + lane_sum(r, cw)
    pay[0:low, pl.ds(at[2], cw)] = r2lo[:, :cw]
    pay[low:, pl.ds(at[2], cw)] = r2hi[:, :cw]
    part = part + lane_sum(r2lo, cw)
    pay[:, 4 * cw :] = scalar_lanes(part, rx)


def row_starts(idx, rx):
    return [pl.multiple_of(lax.rem(idx[0] + k, 4) * rx, rx) for k in range(4)]


def column_sums(v, n):
    return [jnp.sum(fold(v), 0, keepdims=True), jnp.sum(fold(v * n.astype(f32)), 0, keepdims=True)]


def first_product_kernel(idx, own, r1, r3, n, my, send, acc, gram):
    rx, images = own.shape[0], gram.shape[1]
    width = my.shape[1]
    starts = row_starts(idx, rx)
    part = jnp.zeros((1, 1), f32)
    for i, r in enumerate((own, r1, r3)):
        gram[i * rx : i * rx + rx, :] = r[:, :images]
        part = part + lane_sum(r, images)
    zero = jnp.zeros((1, width), f32)
    for out, cols in ((send, slice(width, 2 * width)), (my, slice(0, width))):
        out[...] = jnp.dot(gram[...], n[:, cols], preferred_element_type=f32)
        got = [zero, zero]
        for i, k in enumerate((0, 3, 1)):
            more = column_sums(out[i * rx : i * rx + rx, :], n[pl.ds(starts[k], rx), cols])
            got = [got[0] + more[0], got[1] + more[1]]
        acc[:, cols] = jnp.concatenate(got + [zero + part] + [zero] * 5, 0)


def last_product_kernel(idx, r2lo, r2hi, n, acc, my, send, sums, gram):
    (low, rx), images = (r2lo.shape[0], gram.shape[0]), gram.shape[1]
    width = my.shape[1]
    at = row_starts(idx, rx)[2]
    gram[0:low, :] = r2lo[:, :images]
    gram[low:, :] = r2hi[:, :images]
    part = lane_sum(r2lo, images)
    zero = jnp.zeros((1, width), f32)
    got = []
    for out, cols in ((send, slice(width, 2 * width)), (my, slice(0, width))):
        v = jnp.dot(gram[...], n[:, cols], preferred_element_type=f32)
        out[...] = v
        more = column_sums(v, n[pl.ds(at, rx), cols])
        got.append(acc[:, cols] + jnp.concatenate(more + [zero + part] + [zero] * 5, 0))
    to_even = jnp.where(idx[2] == 0, got[1], got[0])
    to_odd = jnp.where(idx[2] == 0, got[0], got[1])
    for i in range(0, sums.shape[0], 2):
        sums[i] = to_even
        sums[i + 1] = to_odd


def grad_kernel(images, idx, my3, my1, other3, other1, my_own, o_own, diag, sums, inv_my, inv_other, loss, *refs):
    grad_a, grad_b, out_my, out_other, sems = refs
    rx, width = my1.shape
    c = diag[0:1, :]
    scale, coef = 2.0 * off_weight / images, -2.0 * (1.0 - c) - 2.0 * off_weight * c
    even, odd = sums[0], sums[1]
    for i in range(2, sums.shape[0], 2):
        even, odd = even + sums[i], odd + sums[i + 1]
    loss[...] = even[2:3, 0:1] + odd[2:3, 0:1]
    mine = jnp.where(idx[2] == 0, even, odd)
    theirs = jnp.where(idx[2] == 0, odd, even)
    my_mean = (scale * mine[0:1, :] + coef * diag[2:3, :]) / images
    my_dot = scale * mine[1:2, :] / images + coef * c
    other_mean = (scale * theirs[0:1, :] + coef * diag[1:2, :]) / images
    other_dot = scale * theirs[1:2, :] / images + coef * c
    starts = row_starts(idx, rx)

    def write(my_ref, other_ref):
        copies = []
        for i, k in enumerate((0, 3, 1, 2)):
            at = pl.ds(starts[k], rx)
            rel = slice(i * rx, i * rx + rx)
            my, other = my_own[at, :].astype(f32), o_own[at, :].astype(f32)
            d_my = scale * (my3[rel, :] if i < 3 else my1[...]) + coef * other
            d_other = scale * (other3[rel, :] if i < 3 else other1[...]) + coef * my
            out_my[rel, :] = (d_my - my_mean - my * my_dot) * inv_my[0:1, :width]
            copies.append(pltpu.make_async_copy(out_my.at[rel, :], my_ref.at[at, :], sems.at[2 * i]))
            copies[-1].start()
            out_other[rel, :] = (d_other - other_mean - other * other_dot) * inv_other[0:1, :]
            copies.append(pltpu.make_async_copy(out_other.at[rel, :], other_ref.at[at, :], sems.at[2 * i + 1]))
            copies[-1].start()
        for copy in copies:
            copy.wait()

    @pl.when(idx[2] == 0)
    def _():
        write(grad_a, grad_b)

    @pl.when(idx[2] != 0)
    def _():
        write(grad_b, grad_a)


def call(kernel, outs, *args, scratch=(), limit=4, fetch=(), outside=0):
    spaces = [pltpu.SMEM if a.dtype == jnp.int32 else pltpu.VMEM for a in args] + [pl.ANY] * len(fetch)
    return pl.pallas_call(
        kernel,
        out_shape=outs,
        in_specs=[pl.BlockSpec(memory_space=s) for s in spaces],
        out_specs=[pl.BlockSpec(memory_space=pltpu.VMEM)] * (len(outs) - outside)
        + [pl.BlockSpec(memory_space=pl.ANY)] * outside,
        scratch_shapes=list(scratch),
        compiler_params=pltpu.CompilerParams(vmem_limit_bytes=limit * 2**20),
        cost_estimate=pl.CostEstimate(flops=0, bytes_accessed=0, transcendentals=0),
    )(*args, *fetch)


def per_device(view_a, view_b):
    rows, width = view_a.shape
    images, full, rx, cw = rows * 8, width * 2, rows // 4, rows * 2
    idx = jnp.stack([lax.axis_index("x"), lax.axis_index("zh"), lax.axis_index("core")]).astype(jnp.int32)
    first = lax.axis_index("core") == 0
    keep = jnp.where(first, view_a, view_b)
    give = jnp.where(first, view_b, view_a)
    own = jnp.concatenate([keep, from_pair(give, "core")], 1)

    half = rows // 2
    b10 = from_axis(own, "y", 1)
    b30 = from_axis(own, "y", 3)
    b01 = from_pair(own, "zl")
    b20 = (from_axis(b10[:half], "y", 1), from_axis(b30[half:], "y", 3))
    b11 = from_axis(b01, "y", 1)
    b31 = from_axis(b01, "y", 3)
    b21 = tuple(from_pair(b, "zl") for b in b20)

    known = (own, b01, b10, b30, *b20)
    st, known = call(
        stats_kernel, [like((24, full), f32), like((sum(b.shape[0] for b in known), full), bf16)], *known
    )
    def ring(v, axis):
        r1, r3 = from_axis(v, axis, 3), from_axis(v, axis, 1)
        return r1, r3, from_axis(r1[:low], axis, 3), from_axis(r3[low:], axis, 1)

    piece, shard = like((rx, images), bf16), like((rx, cw), bf16)
    up, down = like((low, images), bf16), like((rx - low, images), bf16)
    blocks = (b11, b31, *b21)
    n, no, inv, p2lo, p2hi = call(
        functools.partial(norm_kernel, images),
        [like((images, full), bf16), like((images, width), bf16), like((8, full), f32), up, down],
        *(idx, st, known),
        fetch=blocks,
        scratch=[pltpu.VMEM((images - known.shape[0], full), bf16), pltpu.SemaphoreType.DMA((len(blocks),))],
    )
    p0, p1lo, p1hi, p3lo, p3hi = call(
        gram_kernel, [piece, up, down, up, down], idx, n, scratch=[pltpu.VMEM((rows, images), bf16)], limit=8
    )
    a, b = from_axis(p2lo, "x", 3), from_axis(p2hi, "x", 1)
    c, d = from_axis(p1hi, "x", 3), from_axis(p3lo, "x", 1)
    e, f = call(add_kernel, [up, down], p1lo, a, p3hi, b)
    e, f = from_axis(e, "x", 3), from_axis(f, "x", 1)
    q0, q1, q2, q3 = call(sum_x_kernel, [shard] * 4, idx, p0, d, e, c, f, scratch=[pltpu.VMEM((4, rx, cw), bf16)])
    no, inv, q1 = lax.optimization_barrier((no, inv, q1))
    o = from_pair(no, "core")
    inv_other = from_pair(inv[:, width:], "core")
    diag, my_own, o_own, inv_other = call(
        functools.partial(diag_kernel, images),
        [like((8, width), f32), like((rows, width), bf16), like((rows, width), bf16), like((8, width), f32)],
        *(n, o, inv_other),
    )
    got = [from_axis(q, "zh", -k) for k, q in ((2, q2), (1, q1), (3, q3))]
    q0, _ = lax.optimization_barrier((q0, diag))
    (mine,) = call(sum_z_kernel, [shard], q0, *got)
    theirs = from_pair(mine, "core")
    (pay,) = call(functools.partial(load_kernel, images), [like((rx, cw + 128), bf16)], mine, theirs, diag)
    (pay,) = call(join_kernel, [like((rx, images + 128), bf16)], idx, pay, *ring(pay, "zh"))
    r1, r3, r2lo, r2hi = ring(pay, "x")
    wide, three, quarter = like((rows, width), f32), like((3 * rx, width), f32), like((rx, width), f32)
    my3, send3, acc = call(
        first_product_kernel,
        [three, three, like((8, full), f32)],
        *(idx, pay, r1, r3, n),
        scratch=[pltpu.VMEM((3 * rx, images), bf16)],
        limit=8,
    )
    other3 = from_pair(send3, "core")
    my1, send1, sums = call(
        last_product_kernel,
        [quarter, quarter, like((16, 8, width), f32)],
        *(idx, r2lo, r2hi, n, acc),
        scratch=[pltpu.VMEM((rx, images), bf16)],
    )
    other1 = from_pair(send1, "core")
    sums = lax.all_to_all(sums, batch + ("core",), split_axis=0, concat_axis=0, tiled=True)
    loss, grad_a, grad_b = call(
        functools.partial(grad_kernel, images),
        [like((1, 1), f32), wide, wide],
        *(idx, my3, my1, other3, other1, my_own, o_own, diag, sums, inv, inv_other),
        scratch=[pltpu.VMEM((rows, width), f32), pltpu.VMEM((rows, width), f32), pltpu.SemaphoreType.DMA((8,))],
        outside=2,
    )
    return (loss.reshape(()), grad_a, grad_b)


def solution(mesh):
    fine = Mesh(mesh.devices.reshape(sizes), names)
    spec = P(batch, ("x", "zh", "core"))
    return jax.shard_map(per_device, mesh=fine, in_specs=(spec, spec), out_specs=(P(), spec, spec), check_vma=False)
```

profile of v0, /device:TPU:1, one launch (start us, length us, event | category | flops | bytes accessed | tf_op | source)
XLA Modules:
  0.0 145.3 jit_solution(1213435457788535011)
XLA Ops:
  0.6 1.1 broadcast_select_fusion.1
  1.8 3.3 %collective-permute-start = (bf16[320,512]{1,0:T(8,128)(2,1)S(1)}, bf16[320,512]{1,0:T(8,128)(2,1)S(1)}, u32[]{:S(2)}, u32[]{:S(2)}) collective-permute-start(bf16[320,512]{1,0:T(8,128)(2,1)S(1)} %get-tuple-element.74), channel_id=1, source_target_pairs={{1,0},{0,1},{3,2},{2,3},{5,4},{4,5},{7,6},{6,7},{9,8},{8,9},{11,10... | collective-permute-start | bytes 983048 | tf_op jit(solution)/shard_map/ppermute | solution.py:26
  5.1 1.3 collective-permute-done
  6.3 0.1 pad_maximum_fusion.own
  6.4 0.1 collective-permute-start.3
  6.5 2.7 %collective-permute-start.2 = (bf16[320,1024]{1,0:T(8,128)(2,1)S(1)}, bf16[320,1024]{1,0:T(8,128)(2,1)S(1)}, u32[]{:S(2)}, u32[]{:S(2)}) collective-permute-start(bf16[320,1024]{1,0:T(8,128)(2,1)S(1)} %pad_maximum_fusion.own), channel_id=1, source_target_pairs={{64,0},{128,64},{192,128},{0,192},{65,1},{129,65},{193,129},{1,193... | collective-permute-start | bytes 1966088 | tf_op jit(solution)/shard_map/ppermute | solution.py:22
  9.2 14.4 %collective-permute-done.3.refs_2_ = bf16[320,1024]{1,0:T(8,128)(2,1)S(1)} collective-permute-done((bf16[320,1024]{1,0:T(8,128)(2,1)S(1)}, bf16[320,1024]{1,0:T(8,128)(2,1)S(1)}, u32[]{:S(2)}, u32[]{:S(2)}) %collective-permute-start.3) | collective-permute-done | bytes 655392 | tf_op jit(solution)/shard_map/ppermute | solution.py:22
  23.7 0.1 collective-permute-start.5
  23.8 2.7 %collective-permute-start.4 = (bf16[160,1024]{1,0:T(8,128)(2,1)S(1)}, bf16[160,1024]{1,0:T(8,128)(2,1)}, u32[]{:S(2)}, u32[]{:S(2)}) collective-permute-start(bf16[160,1024]{1,0:T(8,128)(2,1)S(1)} %slice.28), channel_id=1, source_target_pairs={{64,0},{128,64},{192,128},{0,192},{65,1},{129,65},{193,129},{1,193... | collective-permute-start | bytes 983048 | tf_op jit(solution)/shard_map/ppermute | solution.py:22
  26.6 2.7 %collective-permute-start.6 = (bf16[320,1024]{1,0:T(8,128)(2,1)S(1)}, bf16[320,1024]{1,0:T(8,128)(2,1)}, u32[]{:S(2)}, u32[]{:S(2)}) collective-permute-start(bf16[320,1024]{1,0:T(8,128)(2,1)S(1)} %collective-permute-done.1.refs_0_), channel_id=1, source_target_pairs={{64,0},{128,64},{192,128},{0,192},{65,1},{129,65},{193,129},{1,193... | collective-permute-start | bytes 1966088 | tf_op jit(solution)/shard_map/ppermute | solution.py:22
  29.2 3.9 %collective-permute-done.5.refs_4_ = bf16[160,1024]{1,0:T(8,128)(2,1)} collective-permute-done((bf16[160,1024]{1,0:T(8,128)(2,1)S(1)}, bf16[160,1024]{1,0:T(8,128)(2,1)}, u32[]{:S(2)}, u32[]{:S(2)}) %collective-permute-start.5) | collective-permute-done | bytes 327712 | tf_op jit(solution)/shard_map/ppermute | solution.py:22
  33.1 0.1 collective-permute-start.9
  33.2 1.4 collective-permute-start.8
  34.6 0.1 pad_add_fusion.idx
  34.6 2.9 %shard_map.49 = (f32[24,1024]{1,0:T(8,128)S(1)}, bf16[1600,1024]{1,0:T(8,128)(2,1)S(1)}) custom-call(bf16[320,1024]{1,0:T(8,128)(2,1)S(1)} %pad_maximum_fusion.own, bf16[320,1024]{1,0:T(8,128)(2,1)S(1)} %collective-permute-done.1.refs_0_, bf16[320,1024]{1,0:T(8,128)(2,1)S(1)} %collective-permute-done.2.refs_1_, ...), custom_call_target="tpu_custom_call" | custom-call | tf_op jit(solution)/shard_map/pallas_call | solution.py:282
  37.6 2.1 %collective-permute-done.9.refs_3_ = bf16[160,1024]{1,0:T(8,128)(2,1)} collective-permute-done((bf16[160,1024]{1,0:T(8,128)(2,1)}, bf16[160,1024]{1,0:T(8,128)(2,1)}, u32[]{:S(2)}, u32[]{:S(2)}) %collective-permute-start.9) | collective-permute-done | bytes 327712 | tf_op jit(solution)/shard_map/ppermute | solution.py:26
  39.6 6.2 %collective-permute-done.8.refs_2_ = bf16[160,1024]{1,0:T(8,128)(2,1)} collective-permute-done((bf16[160,1024]{1,0:T(8,128)(2,1)}, bf16[160,1024]{1,0:T(8,128)(2,1)}, u32[]{:S(2)}, u32[]{:S(2)}) %collective-permute-start.8) | collective-permute-done | bytes 327712 | tf_op jit(solution)/shard_map/ppermute | solution.py:26
  45.8 1.2 collective-permute-done.7.refs_1_
  47.0 5.6 %shard_map.50 = (bf16[2560,1024]{1,0:T(8,128)(2,1)S(1)}, bf16[2560,512]{1,0:T(8,128)(2,1)S(1)}, f32[8,1024]{1,0:T(8,128)S(1)}, bf16[48,2560]{1,0:T(8,128)(2,1)S(1)}, bf16[32,2560]{1,0:T(8,128)(2,1)S(1)}) custom-call(s32[3]{0:T(128)S(1)} %pad_add_fusion.idx, f32[24,1024]{1,0:T(8,128)S(1)} %get-tuple-element.38.st, ...), custom_call_target="tpu_custom_call" | custom-call | tf_op jit(solution)/shard_map/pallas_call | solution.py:282
  52.7 0.1 collective-permute-start.11
  52.7 2.7 %collective-permute-start.12 = (bf16[32,2560]{1,0:T(8,128)(2,1)S(1)}, bf16[32,2560]{1,0:T(8,128)(2,1)S(1)}, u32[]{:S(2)}, u32[]{:S(2)}) collective-permute-start(bf16[32,2560]{1,0:T(8,128)(2,1)S(1)} %get-tuple-element.46), channel_id=1, source_target_pairs={{8,0},{16,8},{24,16},{0,24},{9,1},{17,9},{25,17},{1,25},{10,2},{18... | collective-permute-start | bytes 491528 | tf_op jit(solution)/shard_map/ppermute | solution.py:22
  55.4 2.9 %shard_map.51 = (bf16[80,2560]{1,0:T(8,128)(2,1)S(1)}, bf16[48,2560]{1,0:T(8,128)(2,1)S(1)}, bf16[32,2560]{1,0:T(8,128)(2,1)S(1)}, bf16[48,2560]{1,0:T(8,128)(2,1)S(1)}, bf16[32,2560]{1,0:T(8,128)(2,1)S(1)}) custom-call(s32[3]{0:T(128)S(1)} %pad_add_fusion.idx, bf16[2560,1024]{1,0:T(8,128)(2,1)S(1)} %get-tuple-element.40.n), custom_call_target="tpu_custom_call" | custom-call | tf_op jit(solution)/shard_map/pallas_call | solution.py:282
  58.3 0.1 collective-permute-start.10
  58.4 0.6 collective-permute-done.11.a
  59.0 0.1 shard_map.52
  59.1 1.0 collective-permute-start.13
  60.1 0.1 collective-permute-start.14
  60.1 2.6 %collective-permute-start.15 = (bf16[32,2560]{1,0:T(8,128)(2,1)S(1)}, bf16[32,2560]{1,0:T(8,128)(2,1)S(1)}, u32[]{:S(2)}, u32[]{:S(2)}) collective-permute-start(bf16[32,2560]{1,0:T(8,128)(2,1)S(1)} %get-tuple-element.49), channel_id=1, source_target_pairs={{8,0},{16,8},{24,16},{0,24},{9,1},{17,9},{25,17},{1,25},{10,2},{18... | collective-permute-start | bytes 491528 | tf_op jit(solution)/shard_map/ppermute | solution.py:22
  62.7 4.6 %collective-permute-done.14.c = bf16[32,2560]{1,0:T(8,128)(2,1)S(1)} collective-permute-done((bf16[32,2560]{1,0:T(8,128)(2,1)S(1)}, bf16[32,2560]{1,0:T(8,128)(2,1)S(1)}, u32[]{:S(2)}, u32[]{:S(2)}) %collective-permute-start.14) | collective-permute-done | bytes 163872 | tf_op jit(solution)/shard_map/ppermute | solution.py:22
  67.4 0.7 shard_map.53
  68.1 6.2 %collective-permute-start.16 = (bf16[2560,512]{1,0:T(8,128)(2,1)S(1)}, bf16[2560,512]{1,0:T(8,128)(2,1)S(1)}, u32[]{:S(2)}, u32[]{:S(2)}) collective-permute-start(bf16[2560,512]{1,0:T(8,128)(2,1)S(1)} %get-tuple-element.54), channel_id=1, source_target_pairs={{1,0},{0,1},{3,2},{2,3},{5,4},{4,5},{7,6},{6,7},{9,8},{8,9},{11,10... | collective-permute-start | bytes 7864328 | tf_op jit(solution)/shard_map/ppermute | solution.py:26
  74.4 2.2 %collective-permute-start.19 = (bf16[80,640]{1,0:T(8,128)(2,1)S(1)}, bf16[80,640]{1,0:T(8,128)(2,1)S(1)}, u32[]{:S(2)}, u32[]{:S(2)}) collective-permute-start(bf16[80,640]{1,0:T(8,128)(2,1)S(1)} %get-tuple-element.59), channel_id=1, source_target_pairs={{6,0},{0,2},{2,4},{4,6},{7,1},{1,3},{3,5},{5,7},{14,8},{8,10},{10,... | collective-permute-start | bytes 307208 | tf_op jit(solution)/shard_map/ppermute | solution.py:22
  76.6 4.8 %collective-permute-start.18 = (bf16[80,640]{1,0:T(8,128)(2,1)S(1)}, bf16[80,640]{1,0:T(8,128)(2,1)S(1)}, u32[]{:S(2)}, u32[]{:S(2)}) collective-permute-start(bf16[80,640]{1,0:T(8,128)(2,1)S(1)} %get-tuple-element.58), channel_id=1, source_target_pairs={{4,0},{6,2},{0,4},{2,6},{5,1},{7,3},{1,5},{3,7},{12,8},{14,10},{8,... | collective-permute-start | bytes 307208 | tf_op jit(solution)/shard_map/ppermute | solution.py:22
  81.3 2.4 %collective-permute-start.20 = (bf16[80,640]{1,0:T(8,128)(2,1)S(1)}, bf16[80,640]{1,0:T(8,128)(2,1)S(1)}, u32[]{:S(2)}, u32[]{:S(2)}) collective-permute-start(bf16[80,640]{1,0:T(8,128)(2,1)S(1)} %get-tuple-element.60), channel_id=1, source_target_pairs={{2,0},{4,2},{6,4},{0,6},{3,1},{5,3},{7,5},{1,7},{10,8},{12,10},{14... | collective-permute-start | bytes 307208 | tf_op jit(solution)/shard_map/ppermute | solution.py:22
  83.7 0.9 collective-permute-start.17
  84.6 0.8 collective-permute-done.17.inv_o
  85.5 1.1 shard_map.54
  86.6 2.1 %collective-permute-done.18.r1 = bf16[80,640]{1,0:T(8,128)(2,1)S(1)} collective-permute-done((bf16[80,640]{1,0:T(8,128)(2,1)S(1)}, bf16[80,640]{1,0:T(8,128)(2,1)S(1)}, u32[]{:S(2)}, u32[]{:S(2)}) %collective-permute-start.18) | collective-permute-done | bytes 102432 | tf_op jit(solution)/shard_map/ppermute | solution.py:22
  88.7 3.0 %collective-permute-done.20.r3 = bf16[80,640]{1,0:T(8,128)(2,1)S(1)} collective-permute-done((bf16[80,640]{1,0:T(8,128)(2,1)S(1)}, bf16[80,640]{1,0:T(8,128)(2,1)S(1)}, u32[]{:S(2)}, u32[]{:S(2)}) %collective-permute-start.20) | collective-permute-done | bytes 102432 | tf_op jit(solution)/shard_map/ppermute | solution.py:22
  91.7 0.1 shard_map.55.mine
  91.7 0.6 collective-permute-start.21
  92.3 0.9 collective-permute-done.21.theirs
  93.3 0.1 shard_map.56.own
  93.4 1.5 %collective-permute-start.22 = (bf16[80,768]{1,0:T(8,128)(2,1)S(1)}, bf16[80,768]{1,0:T(8,128)(2,1)S(1)}, u32[]{:S(2)}, u32[]{:S(2)}) collective-permute-start(bf16[80,768]{1,0:T(8,128)(2,1)S(1)} %shard_map.56.own), channel_id=1, source_target_pairs={{6,0},{0,2},{2,4},{4,6},{7,1},{1,3},{3,5},{5,7},{14,8},{8,10},{10,... | collective-permute-start | bytes 368648 | tf_op jit(solution)/shard_map/ppermute | solution.py:22
  94.9 2.2 %collective-permute-start.23 = (bf16[80,768]{1,0:T(8,128)(2,1)S(1)}, bf16[80,768]{1,0:T(8,128)(2,1)S(1)}, u32[]{:S(2)}, u32[]{:S(2)}) collective-permute-start(bf16[80,768]{1,0:T(8,128)(2,1)S(1)} %shard_map.56.own), channel_id=1, source_target_pairs={{2,0},{4,2},{6,4},{0,6},{3,1},{5,3},{7,5},{1,7},{10,8},{12,10},{14... | collective-permute-start | bytes 368648 | tf_op jit(solution)/shard_map/ppermute | solution.py:22
  97.1 5.7 %collective-permute-done.22.r1 = bf16[80,768]{1,0:T(8,128)(2,1)S(1)} collective-permute-done((bf16[80,768]{1,0:T(8,128)(2,1)S(1)}, bf16[80,768]{1,0:T(8,128)(2,1)S(1)}, u32[]{:S(2)}, u32[]{:S(2)}) %collective-permute-start.22) | collective-permute-done | bytes 122912 | tf_op jit(solution)/shard_map/ppermute | solution.py:22
  102.7 0.3 collective-permute-start.24
  103.0 0.7 collective-permute-done.23.r3
  103.8 2.8 %collective-permute-start.25 = (bf16[32,768]{1,0:T(8,128)(2,1)S(1)}, bf16[32,768]{1,0:T(8,128)(2,1)S(1)}, u32[]{:S(2)}, u32[]{:S(2)}) collective-permute-start(bf16[32,768]{1,0:T(8,128)(2,1)S(1)} %slice.31), channel_id=1, source_target_pairs={{2,0},{4,2},{6,4},{0,6},{3,1},{5,3},{7,5},{1,7},{10,8},{12,10},{14... | collective-permute-start | bytes 147464 | tf_op jit(solution)/shard_map/ppermute | solution.py:22
  106.6 1.4 collective-permute-done.25.r2hi
  108.1 0.6 shard_map.57.own
  108.7 0.6 collective-permute-start.26
  109.3 2.2 %collective-permute-start.27 = (bf16[80,2688]{1,0:T(8,128)(2,1)S(1)}, bf16[80,2688]{1,0:T(8,128)(2,1)S(1)}, u32[]{:S(2)}, u32[]{:S(2)}) collective-permute-start(bf16[80,2688]{1,0:T(8,128)(2,1)S(1)} %shard_map.57.own), channel_id=1, source_target_pairs={{8,0},{16,8},{24,16},{0,24},{9,1},{17,9},{25,17},{1,25},{10,2},{18... | collective-permute-start | bytes 1290248 | tf_op jit(solution)/shard_map/ppermute | solution.py:22
  111.5 8.0 %collective-permute-done.26.r1 = bf16[80,2688]{1,0:T(8,128)(2,1)S(1)} collective-permute-done((bf16[80,2688]{1,0:T(8,128)(2,1)S(1)}, bf16[80,2688]{1,0:T(8,128)(2,1)S(1)}, u32[]{:S(2)}, u32[]{:S(2)}) %collective-permute-start.26) | collective-permute-done | bytes 430112 | tf_op jit(solution)/shard_map/ppermute | solution.py:22
  119.4 0.1 collective-permute-start.28
  119.5 2.7 %collective-permute-start.29 = (bf16[32,2688]{1,0:T(8,128)(2,1)S(1)}, bf16[32,2688]{1,0:T(8,128)(2,1)S(1)}, u32[]{:S(2)}, u32[]{:S(2)}) collective-permute-start(bf16[32,2688]{1,0:T(8,128)(2,1)S(1)} %slice.33), channel_id=1, source_target_pairs={{8,0},{16,8},{24,16},{0,24},{9,1},{17,9},{25,17},{1,25},{10,2},{18... | collective-permute-start | bytes 516104 | tf_op jit(solution)/shard_map/ppermute | solution.py:22
  122.3 2.1 %shard_map.58 = (f32[240,512]{1,0:T(8,128)S(1)}, f32[240,512]{1,0:T(8,128)S(1)}, f32[8,1024]{1,0:T(8,128)S(1)}) custom-call(s32[3]{0:T(128)S(1)} %pad_add_fusion.idx, bf16[80,2688]{1,0:T(8,128)(2,1)S(1)} %shard_map.57.own, bf16[80,2688]{1,0:T(8,128)(2,1)S(1)} %collective-permute-done.26.r1, bf16[80,2688]{1,0:T(8,128)(2,1)S(1)} %collective-permute-done.27.r3, ...), custom_call_target="tpu_custom_call" | custom-call | tf_op jit(solution)/shard_map/pallas_call | solution.py:282
  124.4 3.5 %collective-permute-start.30 = (f32[240,512]{1,0:T(8,128)S(1)}, f32[240,512]{1,0:T(8,128)S(1)}, u32[]{:S(2)}, u32[]{:S(2)}) collective-permute-start(f32[240,512]{1,0:T(8,128)S(1)} %get-tuple-element.64), channel_id=1, source_target_pairs={{1,0},{0,1},{3,2},{2,3},{5,4},{4,5},{7,6},{6,7},{9,8},{8,9},{11,10... | collective-permute-start | bytes 1474568 | tf_op jit(solution)/shard_map/ppermute | solution.py:26
  127.9 2.3 %shard_map.59 = (f32[80,512]{1,0:T(8,128)S(1)}, f32[80,512]{1,0:T(8,128)S(1)}, f32[16,8,512]{2,1,0:T(8,128)}) custom-call(s32[3]{0:T(128)S(1)} %pad_add_fusion.idx, bf16[48,2688]{1,0:T(8,128)(2,1)S(1)} %collective-permute-done.28.r2lo, bf16[32,2688]{1,0:T(8,128)(2,1)S(1)} %collective-permute-done.29.r2hi, bf16[2560,1024]{1,0:T(8,128)(2,1)S(1)} %get-tuple-element.40.n, ...), custom_call_target="tpu_custom_call" | custom-call | tf_op jit(solution)/shard_map/pallas_call | solution.py:282
  130.3 5.4 %all-to-all-start = ((f32[16,8,512]{2,1,0:T(8,128)}), f32[16,8,512]{2,1,0:T(8,128)S(1)}, u32[]{:S(2)}, u32[]{:S(2)}) async-start(f32[16,8,512]{2,1,0:T(8,128)} %get-tuple-element.68), calls=%async_computation | async-start | bytes 524288 | tf_op jit(solution)/shard_map/all_to_all | solution.py:369
  135.6 0.3 collective-permute-start.31
  135.9 1.1 collective-permute-done.31.other1
  137.0 5.8 %all-to-all-done.sums = f32[16,8,512]{2,1,0:T(8,128)S(1)} async-done(((f32[16,8,512]{2,1,0:T(8,128)}), f32[16,8,512]{2,1,0:T(8,128)S(1)}, u32[]{:S(2)}, u32[]{:S(2)}) %all-to-all-start) | async-done | bytes 262176 | tf_op jit(solution)/shard_map/all_to_all | solution.py:369
  142.8 2.2 %shard_map.60 = (f32[1,1]{1,0:T(1,128)}, f32[320,512]{1,0:T(8,128)}, f32[320,512]{1,0:T(8,128)}) custom-call(s32[3]{0:T(128)S(1)} %pad_add_fusion.idx, f32[240,512]{1,0:T(8,128)S(1)} %get-tuple-element.61.my3, f32[80,512]{1,0:T(8,128)S(1)} %get-tuple-element.63.my1, f32[240,512]{1,0:T(8,128)S(1)} %collective-permute-done.30.other3, ...), custom_call_target="tpu_custom_call" | custom-call | tf_op jit(solution)/shard_map/pallas_call | solution.py:282
  (24 shorter events, 0.2 us)
Async XLA Ops:
  1.8 4.6 %collective-permute-start = (bf16[320,512]{1,0:T(8,128)(2,1)S(1)}, bf16[320,512]{1,0:T(8,128)(2,1)S(1)}, u32[]{:S(2)}, u32[]{:S(2)}) collective-permute-start(bf16[320,512]{1,0:T(8,128)(2,1)S(1)} %get-tuple-element.74), channel_id=1, source_target_pairs={{1,0},{0,1},{3,2},{2,3},{5,4},{4,5},{7,6},{6,7},{9,8},{8,9},{11,10... | collective-permute-start | bytes 983048 | tf_op jit(solution)/shard_map/ppermute | solution.py:26
  6.4 17.2 %collective-permute-start.3 = (bf16[320,1024]{1,0:T(8,128)(2,1)S(1)}, bf16[320,1024]{1,0:T(8,128)(2,1)S(1)}, u32[]{:S(2)}, u32[]{:S(2)}) collective-permute-start(bf16[320,1024]{1,0:T(8,128)(2,1)S(1)} %pad_maximum_fusion.own), channel_id=1, source_target_pairs={{192,0},{0,64},{64,128},{128,192},{193,1},{1,65},{65,129},{129,193... | collective-permute-start | bytes 1966088 | tf_op jit(solution)/shard_map/ppermute | solution.py:22
  6.5 17.3 %collective-permute-start.2 = (bf16[320,1024]{1,0:T(8,128)(2,1)S(1)}, bf16[320,1024]{1,0:T(8,128)(2,1)S(1)}, u32[]{:S(2)}, u32[]{:S(2)}) collective-permute-start(bf16[320,1024]{1,0:T(8,128)(2,1)S(1)} %pad_maximum_fusion.own), channel_id=1, source_target_pairs={{64,0},{128,64},{192,128},{0,192},{65,1},{129,65},{193,129},{1,193... | collective-permute-start | bytes 1966088 | tf_op jit(solution)/shard_map/ppermute | solution.py:22
  9.2 17.4 %collective-permute-start.1 = (bf16[320,1024]{1,0:T(8,128)(2,1)S(1)}, bf16[320,1024]{1,0:T(8,128)(2,1)S(1)}, u32[]{:S(2)}, u32[]{:S(2)}) collective-permute-start(bf16[320,1024]{1,0:T(8,128)(2,1)S(1)} %pad_maximum_fusion.own), channel_id=1, source_target_pairs={{32,0},{0,32},{33,1},{1,33},{34,2},{2,34},{35,3},{3,35},{36,4},{4,... | collective-permute-start | bytes 1966088 | tf_op jit(solution)/shard_map/ppermute | solution.py:26
  23.7 9.4 %collective-permute-start.5 = (bf16[160,1024]{1,0:T(8,128)(2,1)S(1)}, bf16[160,1024]{1,0:T(8,128)(2,1)}, u32[]{:S(2)}, u32[]{:S(2)}) collective-permute-start(bf16[160,1024]{1,0:T(8,128)(2,1)S(1)} %slice.29), channel_id=1, source_target_pairs={{192,0},{0,64},{64,128},{128,192},{193,1},{1,65},{65,129},{129,193... | collective-permute-start | bytes 983048 | tf_op jit(solution)/shard_map/ppermute | solution.py:22
  23.8 9.4 %collective-permute-start.4 = (bf16[160,1024]{1,0:T(8,128)(2,1)S(1)}, bf16[160,1024]{1,0:T(8,128)(2,1)}, u32[]{:S(2)}, u32[]{:S(2)}) collective-permute-start(bf16[160,1024]{1,0:T(8,128)(2,1)S(1)} %slice.28), channel_id=1, source_target_pairs={{64,0},{128,64},{192,128},{0,192},{65,1},{129,65},{193,129},{1,193... | collective-permute-start | bytes 983048 | tf_op jit(solution)/shard_map/ppermute | solution.py:22
  26.6 20.5 %collective-permute-start.7 = (bf16[320,1024]{1,0:T(8,128)(2,1)S(1)}, bf16[320,1024]{1,0:T(8,128)(2,1)S(1)}, u32[]{:S(2)}, u32[]{:S(2)}) collective-permute-start(bf16[320,1024]{1,0:T(8,128)(2,1)S(1)} %collective-permute-done.1.refs_0_), channel_id=1, source_target_pairs={{192,0},{0,64},{64,128},{128,192},{193,1},{1,65},{65,129},{129,193... | collective-permute-start | bytes 1966088 | tf_op jit(solution)/shard_map/ppermute | solution.py:22
  26.6 20.5 %collective-permute-start.6 = (bf16[320,1024]{1,0:T(8,128)(2,1)S(1)}, bf16[320,1024]{1,0:T(8,128)(2,1)}, u32[]{:S(2)}, u32[]{:S(2)}) collective-permute-start(bf16[320,1024]{1,0:T(8,128)(2,1)S(1)} %collective-permute-done.1.refs_0_), channel_id=1, source_target_pairs={{64,0},{128,64},{192,128},{0,192},{65,1},{129,65},{193,129},{1,193... | collective-permute-start | bytes 1966088 | tf_op jit(solution)/shard_map/ppermute | solution.py:22
  33.1 6.5 %collective-permute-start.9 = (bf16[160,1024]{1,0:T(8,128)(2,1)}, bf16[160,1024]{1,0:T(8,128)(2,1)}, u32[]{:S(2)}, u32[]{:S(2)}) collective-permute-start(bf16[160,1024]{1,0:T(8,128)(2,1)} %collective-permute-done.5.refs_4_), channel_id=1, source_target_pairs={{32,0},{0,32},{33,1},{1,33},{34,2},{2,34},{35,3},{3,35},{36,4},{4,... | collective-permute-start | bytes 983048 | tf_op jit(solution)/shard_map/ppermute | solution.py:26
  33.2 12.6 %collective-permute-start.8 = (bf16[160,1024]{1,0:T(8,128)(2,1)}, bf16[160,1024]{1,0:T(8,128)(2,1)}, u32[]{:S(2)}, u32[]{:S(2)}) collective-permute-start(bf16[160,1024]{1,0:T(8,128)(2,1)} %collective-permute-done.4.refs_3_), channel_id=1, source_target_pairs={{32,0},{0,32},{33,1},{1,33},{34,2},{2,34},{35,3},{3,35},{36,4},{4,... | collective-permute-start | bytes 983048 | tf_op jit(solution)/shard_map/ppermute | solution.py:26
  52.7 6.3 %collective-permute-start.11 = (bf16[48,2560]{1,0:T(8,128)(2,1)S(1)}, bf16[48,2560]{1,0:T(8,128)(2,1)S(1)}, u32[]{:S(2)}, u32[]{:S(2)}) collective-permute-start(bf16[48,2560]{1,0:T(8,128)(2,1)S(1)} %get-tuple-element.44), channel_id=1, source_target_pairs={{24,0},{0,8},{8,16},{16,24},{25,1},{1,9},{9,17},{17,25},{26,2},{2,... | collective-permute-start | bytes 737288 | tf_op jit(solution)/shard_map/ppermute | solution.py:22
  52.7 5.7 %collective-permute-start.12 = (bf16[32,2560]{1,0:T(8,128)(2,1)S(1)}, bf16[32,2560]{1,0:T(8,128)(2,1)S(1)}, u32[]{:S(2)}, u32[]{:S(2)}) collective-permute-start(bf16[32,2560]{1,0:T(8,128)(2,1)S(1)} %get-tuple-element.46), channel_id=1, source_target_pairs={{8,0},{16,8},{24,16},{0,24},{9,1},{17,9},{25,17},{1,25},{10,2},{18... | collective-permute-start | bytes 491528 | tf_op jit(solution)/shard_map/ppermute | solution.py:22
  58.3 9.0 %collective-permute-start.10 = (bf16[48,2560]{1,0:T(8,128)(2,1)S(1)}, bf16[48,2560]{1,0:T(8,128)(2,1)S(1)}, u32[]{:S(2)}, u32[]{:S(2)}) collective-permute-start(bf16[48,2560]{1,0:T(8,128)(2,1)S(1)} %get-tuple-element.42), channel_id=1, source_target_pairs={{8,0},{16,8},{24,16},{0,24},{9,1},{17,9},{25,17},{1,25},{10,2},{18... | collective-permute-start | bytes 737288 | tf_op jit(solution)/shard_map/ppermute | solution.py:22
  59.1 8.3 %collective-permute-start.13 = (bf16[48,2560]{1,0:T(8,128)(2,1)S(1)}, bf16[48,2560]{1,0:T(8,128)(2,1)S(1)}, u32[]{:S(2)}, u32[]{:S(2)}) collective-permute-start(bf16[48,2560]{1,0:T(8,128)(2,1)S(1)} %get-tuple-element.47), channel_id=1, source_target_pairs={{24,0},{0,8},{8,16},{16,24},{25,1},{1,9},{9,17},{17,25},{26,2},{2,... | collective-permute-start | bytes 737288 | tf_op jit(solution)/shard_map/ppermute | solution.py:22
  60.1 7.3 %collective-permute-start.14 = (bf16[32,2560]{1,0:T(8,128)(2,1)S(1)}, bf16[32,2560]{1,0:T(8,128)(2,1)S(1)}, u32[]{:S(2)}, u32[]{:S(2)}) collective-permute-start(bf16[32,2560]{1,0:T(8,128)(2,1)S(1)} %get-tuple-element.48), channel_id=1, source_target_pairs={{24,0},{0,8},{8,16},{16,24},{25,1},{1,9},{9,17},{17,25},{26,2},{2,... | collective-permute-start | bytes 491528 | tf_op jit(solution)/shard_map/ppermute | solution.py:22
  60.1 7.2 %collective-permute-start.15 = (bf16[32,2560]{1,0:T(8,128)(2,1)S(1)}, bf16[32,2560]{1,0:T(8,128)(2,1)S(1)}, u32[]{:S(2)}, u32[]{:S(2)}) collective-permute-start(bf16[32,2560]{1,0:T(8,128)(2,1)S(1)} %get-tuple-element.49), channel_id=1, source_target_pairs={{8,0},{16,8},{24,16},{0,24},{9,1},{17,9},{25,17},{1,25},{10,2},{18... | collective-permute-start | bytes 491528 | tf_op jit(solution)/shard_map/ppermute | solution.py:22
  68.1 17.3 %collective-permute-start.16 = (bf16[2560,512]{1,0:T(8,128)(2,1)S(1)}, bf16[2560,512]{1,0:T(8,128)(2,1)S(1)}, u32[]{:S(2)}, u32[]{:S(2)}) collective-permute-start(bf16[2560,512]{1,0:T(8,128)(2,1)S(1)} %get-tuple-element.54), channel_id=1, source_target_pairs={{1,0},{0,1},{3,2},{2,3},{5,4},{4,5},{7,6},{6,7},{9,8},{8,9},{11,10... | collective-permute-start | bytes 7864328 | tf_op jit(solution)/shard_map/ppermute | solution.py:26
  74.4 12.2 %collective-permute-start.19 = (bf16[80,640]{1,0:T(8,128)(2,1)S(1)}, bf16[80,640]{1,0:T(8,128)(2,1)S(1)}, u32[]{:S(2)}, u32[]{:S(2)}) collective-permute-start(bf16[80,640]{1,0:T(8,128)(2,1)S(1)} %get-tuple-element.59), channel_id=1, source_target_pairs={{6,0},{0,2},{2,4},{4,6},{7,1},{1,3},{3,5},{5,7},{14,8},{8,10},{10,... | collective-permute-start | bytes 307208 | tf_op jit(solution)/shard_map/ppermute | solution.py:22
  76.6 12.2 %collective-permute-start.18 = (bf16[80,640]{1,0:T(8,128)(2,1)S(1)}, bf16[80,640]{1,0:T(8,128)(2,1)S(1)}, u32[]{:S(2)}, u32[]{:S(2)}) collective-permute-start(bf16[80,640]{1,0:T(8,128)(2,1)S(1)} %get-tuple-element.58), channel_id=1, source_target_pairs={{4,0},{6,2},{0,4},{2,6},{5,1},{7,3},{1,5},{3,7},{12,8},{14,10},{8,... | collective-permute-start | bytes 307208 | tf_op jit(solution)/shard_map/ppermute | solution.py:22
  81.3 10.4 %collective-permute-start.20 = (bf16[80,640]{1,0:T(8,128)(2,1)S(1)}, bf16[80,640]{1,0:T(8,128)(2,1)S(1)}, u32[]{:S(2)}, u32[]{:S(2)}) collective-permute-start(bf16[80,640]{1,0:T(8,128)(2,1)S(1)} %get-tuple-element.60), channel_id=1, source_target_pairs={{2,0},{4,2},{6,4},{0,6},{3,1},{5,3},{7,5},{1,7},{10,8},{12,10},{14... | collective-permute-start | bytes 307208 | tf_op jit(solution)/shard_map/ppermute | solution.py:22
  83.7 1.8 %collective-permute-start.17 = (f32[8,512]{1,0:T(8,128)S(1)}, f32[8,512]{1,0:T(8,128)S(1)}, u32[]{:S(2)}, u32[]{:S(2)}) collective-permute-start(f32[8,512]{1,0:T(8,128)S(1)} %slice.23), channel_id=1, source_target_pairs={{1,0},{0,1},{3,2},{2,3},{5,4},{4,5},{7,6},{6,7},{9,8},{8,9},{11,10... | collective-permute-start | bytes 49160 | tf_op jit(solution)/shard_map/ppermute | solution.py:26
  91.7 1.5 %collective-permute-start.21 = (bf16[80,640]{1,0:T(8,128)(2,1)S(1)}, bf16[80,640]{1,0:T(8,128)(2,1)S(1)}, u32[]{:S(2)}, u32[]{:S(2)}) collective-permute-start(bf16[80,640]{1,0:T(8,128)(2,1)S(1)} %shard_map.55.mine), channel_id=1, source_target_pairs={{1,0},{0,1},{3,2},{2,3},{5,4},{4,5},{7,6},{6,7},{9,8},{8,9},{11,10... | collective-permute-start | bytes 307208 | tf_op jit(solution)/shard_map/ppermute | solution.py:26
  93.4 9.3 %collective-permute-start.22 = (bf16[80,768]{1,0:T(8,128)(2,1)S(1)}, bf16[80,768]{1,0:T(8,128)(2,1)S(1)}, u32[]{:S(2)}, u32[]{:S(2)}) collective-permute-start(bf16[80,768]{1,0:T(8,128)(2,1)S(1)} %shard_map.56.own), channel_id=1, source_target_pairs={{6,0},{0,2},{2,4},{4,6},{7,1},{1,3},{3,5},{5,7},{14,8},{8,10},{10,... | collective-permute-start | bytes 368648 | tf_op jit(solution)/shard_map/ppermute | solution.py:22
  94.9 8.9 %collective-permute-start.23 = (bf16[80,768]{1,0:T(8,128)(2,1)S(1)}, bf16[80,768]{1,0:T(8,128)(2,1)S(1)}, u32[]{:S(2)}, u32[]{:S(2)}) collective-permute-start(bf16[80,768]{1,0:T(8,128)(2,1)S(1)} %shard_map.56.own), channel_id=1, source_target_pairs={{2,0},{4,2},{6,4},{0,6},{3,1},{5,3},{7,5},{1,7},{10,8},{12,10},{14... | collective-permute-start | bytes 368648 | tf_op jit(solution)/shard_map/ppermute | solution.py:22
  102.7 5.3 %collective-permute-start.24 = (bf16[48,768]{1,0:T(8,128)(2,1)S(1)}, bf16[48,768]{1,0:T(8,128)(2,1)S(1)}, u32[]{:S(2)}, u32[]{:S(2)}) collective-permute-start(bf16[48,768]{1,0:T(8,128)(2,1)S(1)} %slice.30), channel_id=1, source_target_pairs={{6,0},{0,2},{2,4},{4,6},{7,1},{1,3},{3,5},{5,7},{14,8},{8,10},{10,... | collective-permute-start | bytes 221192 | tf_op jit(solution)/shard_map/ppermute | solution.py:22
  103.8 4.3 %collective-permute-start.25 = (bf16[32,768]{1,0:T(8,128)(2,1)S(1)}, bf16[32,768]{1,0:T(8,128)(2,1)S(1)}, u32[]{:S(2)}, u32[]{:S(2)}) collective-permute-start(bf16[32,768]{1,0:T(8,128)(2,1)S(1)} %slice.31), channel_id=1, source_target_pairs={{2,0},{4,2},{6,4},{0,6},{3,1},{5,3},{7,5},{1,7},{10,8},{12,10},{14... | collective-permute-start | bytes 147464 | tf_op jit(solution)/shard_map/ppermute | solution.py:22
  108.7 10.7 %collective-permute-start.26 = (bf16[80,2688]{1,0:T(8,128)(2,1)S(1)}, bf16[80,2688]{1,0:T(8,128)(2,1)S(1)}, u32[]{:S(2)}, u32[]{:S(2)}) collective-permute-start(bf16[80,2688]{1,0:T(8,128)(2,1)S(1)} %shard_map.57.own), channel_id=1, source_target_pairs={{24,0},{0,8},{8,16},{16,24},{25,1},{1,9},{9,17},{17,25},{26,2},{2,... | collective-permute-start | bytes 1290248 | tf_op jit(solution)/shard_map/ppermute | solution.py:22
  109.3 10.3 %collective-permute-start.27 = (bf16[80,2688]{1,0:T(8,128)(2,1)S(1)}, bf16[80,2688]{1,0:T(8,128)(2,1)S(1)}, u32[]{:S(2)}, u32[]{:S(2)}) collective-permute-start(bf16[80,2688]{1,0:T(8,128)(2,1)S(1)} %shard_map.57.own), channel_id=1, source_target_pairs={{8,0},{16,8},{24,16},{0,24},{9,1},{17,9},{25,17},{1,25},{10,2},{18... | collective-permute-start | bytes 1290248 | tf_op jit(solution)/shard_map/ppermute | solution.py:22
  119.4 8.5 %collective-permute-start.28 = (bf16[48,2688]{1,0:T(8,128)(2,1)S(1)}, bf16[48,2688]{1,0:T(8,128)(2,1)S(1)}, u32[]{:S(2)}, u32[]{:S(2)}) collective-permute-start(bf16[48,2688]{1,0:T(8,128)(2,1)S(1)} %slice.32), channel_id=1, source_target_pairs={{24,0},{0,8},{8,16},{16,24},{25,1},{1,9},{9,17},{17,25},{26,2},{2,... | collective-permute-start | bytes 774152 | tf_op jit(solution)/shard_map/ppermute | solution.py:22
  119.5 8.4 %collective-permute-start.29 = (bf16[32,2688]{1,0:T(8,128)(2,1)S(1)}, bf16[32,2688]{1,0:T(8,128)(2,1)S(1)}, u32[]{:S(2)}, u32[]{:S(2)}) collective-permute-start(bf16[32,2688]{1,0:T(8,128)(2,1)S(1)} %slice.33), channel_id=1, source_target_pairs={{8,0},{16,8},{24,16},{0,24},{9,1},{17,9},{25,17},{1,25},{10,2},{18... | collective-permute-start | bytes 516104 | tf_op jit(solution)/shard_map/ppermute | solution.py:22
  124.4 12.7 %collective-permute-start.30 = (f32[240,512]{1,0:T(8,128)S(1)}, f32[240,512]{1,0:T(8,128)S(1)}, u32[]{:S(2)}, u32[]{:S(2)}) collective-permute-start(f32[240,512]{1,0:T(8,128)S(1)} %get-tuple-element.64), channel_id=1, source_target_pairs={{1,0},{0,1},{3,2},{2,3},{5,4},{4,5},{7,6},{6,7},{9,8},{8,9},{11,10... | collective-permute-start | bytes 1474568 | tf_op jit(solution)/shard_map/ppermute | solution.py:26
  130.3 12.6 %all-to-all-start = ((f32[16,8,512]{2,1,0:T(8,128)}), f32[16,8,512]{2,1,0:T(8,128)S(1)}, u32[]{:S(2)}, u32[]{:S(2)}) async-start(f32[16,8,512]{2,1,0:T(8,128)} %get-tuple-element.68), calls=%async_computation | async-start | bytes 524288 | tf_op jit(solution)/shard_map/all_to_all | solution.py:369
  135.6 1.4 collective-permute-start.31
where the time goes:
time: 146 us; the launch traced here: 145 us
  waiting for transfers between devices  63.8 us (44%)
  starting transfers between devices  58.2 us (40%)
  Pallas kernels  20.9 us (14%)
    ppermute x23, waiting for transfers between devices, from_axis(): return lax.ppermute(v, axis, [((i + k) % 4, i) for i in range(4)])  45.6 us
    ppermute x23, starting transfers between devices, from_axis(): return lax.ppermute(v, axis, [((i + k) % 4, i) for i in range(4)])  36.4 us
    pallas_call x12, Pallas kernels, call(): pl.pallas_call(kernel, out_shape=outs, in_specs=[pl.BlockSpec(memory_spac...  20.9 us
    ppermute x9, starting transfers between devices, from_pair(): return lax.ppermute(v, axis, [(1, 0), (0, 1)])  16.4 us
    ppermute x9, waiting for transfers between devices, from_pair(): return lax.ppermute(v, axis, [(1, 0), (0, 1)])  12.4 us
    all_to_all x1, waiting for transfers between devices, per_device(): lax.all_to_all(sums, batch + ('core',), split_axis=0, concat_axis=0, tile...  5.83 us
    all_to_all x1, starting transfers between devices, per_device(): lax.all_to_all(sums, batch + ('core',), split_axis=0, concat_axis=0, tile...  5.36 us
  transfers between devices with their start and end apart: 33, of which 18 were waited for; matrix products, arithmetic and copies ran while one was open for 0% of the time, Pallas kernels for 8%

commit v1 on v0

--- a/solution.py
+++ b/solution.py
@@ -61,7 +61,7 @@
     st[16:24, :] = jnp.broadcast_to(shift, (8, full))
 
 
-def norm_kernel(images, idx, st, known, *refs):
+def norm_kernel(images, st, known, *refs):
     blocks, (n, no, inv_ref, p2lo, p2hi), (raw, sems) = refs[:-7], refs[-7:-2], refs[-2:]
     full = raw.shape[1]
     width, rows, first = full // 2, images // 8, known.shape[0]
@@ -93,7 +93,7 @@
 
         lax.fori_loop(0, src.shape[0] // chunk, step, 0)
     rx = rows // 4
-    left = n[pl.ds(pl.multiple_of(lax.rem(idx[0] + 2, 4) * rx, rx), rx), :]
+    left = n[pl.ds(pl.multiple_of(lax.rem(lax.axis_index("x") + 2, 4) * rx, rx), rx), :]
     for at in range(0, images, 640):
         cols = slice(at, at + 640)
         v = inner(left, n[cols, :]).astype(bf16)
@@ -101,22 +101,23 @@
         p2hi[:, cols] = v[low:, :]
 
 
-def gram_kernel(idx, n, p0, p1lo, p1hi, p3lo, p3hi, part):
+def gram_kernel(n, p0, p1, p3, part):
     rows, images = part.shape
     for at in range(0, images, 640):
         cols = slice(at, at + 640)
         part[:, cols] = inner(n[0:rows, :], n[cols, :]).astype(bf16)
     rx = rows // 4
-    at = [pl.multiple_of(lax.rem(idx[0] + k, 4) * rx, rx) for k in range(4)]
+    at = [pl.multiple_of(lax.rem(lax.axis_index("x") + k, 4) * rx, rx) for k in range(4)]
     p0[...] = part[pl.ds(at[0], rx), :]
-    for k, lo, hi in ((1, p1lo, p1hi), (3, p3lo, p3hi)):
-        lo[...] = part[pl.ds(at[k], low), :]
-        hi[...] = part[pl.ds(pl.multiple_of(at[k] + low, 16), rx - low), :]
-
-
-def add_kernel(p1lo, a, p3hi, b, e, f):
-    e[...] = (p1lo[...].astype(f32) + a[...].astype(f32)).astype(bf16)
-    f[...] = (p3hi[...].astype(f32) + b[...].astype(f32)).astype(bf16)
+    p1[...] = part[pl.ds(at[1], rx), :]
+    p3[...] = part[pl.ds(at[3], rx), :]
+
+
+def add_kernel(p1, a, p3, b, e, f):
+    e[:low, :] = (p1[:low, :].astype(f32) + a[...].astype(f32)).astype(bf16)
+    e[low:, :] = p1[low:, :]
+    f[:low, :] = p3[:low, :]
+    f[low:, :] = (p3[low:, :].astype(f32) + b[...].astype(f32)).astype(bf16)
 
 
 def diag_kernel(images, n, o, inv_o, diag, my_own, o_own, inv_other):
@@ -136,15 +137,14 @@
     inv_other[...] = inv_o[...]
 
 
-def sum_x_kernel(idx, p0, d, e, c, f, q0, q1, q2, q3, total):
+def sum_x_kernel(p0, e, f, q0, q1, q2, q3, total):
+    cw = q0.shape[1]
     for k in range(4):
-        cols = slice(k * 640, k * 640 + 640)
-        up = p0[0:low, cols].astype(f32) + d[:, cols].astype(f32) + e[:, cols].astype(f32)
-        down = p0[low:, cols].astype(f32) + c[:, cols].astype(f32) + f[:, cols].astype(f32)
-        total[k, 0:low, :] = up.astype(bf16)
-        total[k, low:, :] = down.astype(bf16)
+        cols = slice(k * cw, k * cw + cw)
+        v = p0[:, cols].astype(f32) + e[:, cols].astype(f32) + f[:, cols].astype(f32)
+        total[k] = v.astype(bf16)
     for k, q in enumerate((q0, q1, q2, q3)):
-        q[...] = total[lax.rem(idx[1] + k, 4)]
+        q[...] = total[lax.rem(lax.axis_index("zh") + k, 4)]
 
 
 def sum_z_kernel(q0, r1, r2, r3, mine):
@@ -174,10 +174,10 @@
     return jnp.sum(ref[0:8, width:].astype(f32)[0:1, :], 1, keepdims=True)
 
 
-def join_kernel(idx, own, r1, r3, r2lo, r2hi, pay):
+def join_kernel(own, r1, r3, r2lo, r2hi, pay):
     rx, cw, low = own.shape[0], own.shape[1] - 128, r2lo.shape[0]
     part = jnp.zeros((1, 1), f32)
-    at = [pl.multiple_of(lax.rem(idx[1] + k, 4) * cw, 128) for k in range(4)]
+    at = [pl.multiple_of(lax.rem(lax.axis_index("zh") + k, 4) * cw, 128) for k in range(4)]
     for k, r in ((0, own), (3, r1), (1, r3)):
         pay[:, pl.ds(at[k], cw)] = r[:, :cw]
         part = part + lane_sum(r, cw)
@@ -187,18 +187,18 @@
     pay[:, 4 * cw :] = scalar_lanes(part, rx)
 
 
-def row_starts(idx, rx):
-    return [pl.multiple_of(lax.rem(idx[0] + k, 4) * rx, rx) for k in range(4)]
+def row_starts(rx):
+    return [pl.multiple_of(lax.rem(lax.axis_index("x") + k, 4) * rx, rx) for k in range(4)]
 
 
 def column_sums(v, n):
     return [jnp.sum(fold(v), 0, keepdims=True), jnp.sum(fold(v * n.astype(f32)), 0, keepdims=True)]
 
 
-def first_product_kernel(idx, own, r1, r3, n, my, send, acc, gram):
+def first_product_kernel(own, r1, r3, n, my, send, acc, gram):
     rx, images = own.shape[0], gram.shape[1]
     width = my.shape[1]
-    starts = row_starts(idx, rx)
+    starts = row_starts(rx)
     part = jnp.zeros((1, 1), f32)
     for i, r in enumerate((own, r1, r3)):
         gram[i * rx : i * rx + rx, :] = r[:, :images]
@@ -213,10 +213,10 @@
         acc[:, cols] = jnp.concatenate(got + [zero + part] + [zero] * 5, 0)
 
 
-def last_product_kernel(idx, r2lo, r2hi, n, acc, my, send, sums, gram):
+def last_product_kernel(r2lo, r2hi, n, acc, my, send, sums, gram):
     (low, rx), images = (r2lo.shape[0], gram.shape[0]), gram.shape[1]
     width = my.shape[1]
-    at = row_starts(idx, rx)[2]
+    at = row_starts(rx)[2]
     gram[0:low, :] = r2lo[:, :images]
     gram[low:, :] = r2hi[:, :images]
     part = lane_sum(r2lo, images)
@@ -227,14 +227,14 @@
         out[...] = v
         more = column_sums(v, n[pl.ds(at, rx), cols])
         got.append(acc[:, cols] + jnp.concatenate(more + [zero + part] + [zero] * 5, 0))
-    to_even = jnp.where(idx[2] == 0, got[1], got[0])
-    to_odd = jnp.where(idx[2] == 0, got[0], got[1])
+    to_even = jnp.where(lax.axis_index("core") == 0, got[1], got[0])
+    to_odd = jnp.where(lax.axis_index("core") == 0, got[0], got[1])
     for i in range(0, sums.shape[0], 2):
         sums[i] = to_even
         sums[i + 1] = to_odd
 
 
-def grad_kernel(images, idx, my3, my1, other3, other1, my_own, o_own, diag, sums, inv_my, inv_other, loss, *refs):
+def grad_kernel(images, my3, my1, other3, other1, my_own, o_own, diag, sums, inv_my, inv_other, loss, *refs):
     grad_a, grad_b, out_my, out_other, sems = refs
     rx, width = my1.shape
     c = diag[0:1, :]
@@ -243,13 +243,13 @@
     for i in range(2, sums.shape[0], 2):
         even, odd = even + sums[i], odd + sums[i + 1]
     loss[...] = even[2:3, 0:1] + odd[2:3, 0:1]
-    mine = jnp.where(idx[2] == 0, even, odd)
-    theirs = jnp.where(idx[2] == 0, odd, even)
+    mine = jnp.where(lax.axis_index("core") == 0, even, odd)
+    theirs = jnp.where(lax.axis_index("core") == 0, odd, even)
     my_mean = (scale * mine[0:1, :] + coef * diag[2:3, :]) / images
     my_dot = scale * mine[1:2, :] / images + coef * c
     other_mean = (scale * theirs[0:1, :] + coef * diag[1:2, :]) / images
     other_dot = scale * theirs[1:2, :] / images + coef * c
-    starts = row_starts(idx, rx)
+    starts = row_starts(rx)
 
     def write(my_ref, other_ref):
         copies = []
@@ -268,17 +268,17 @@
         for copy in copies:
             copy.wait()
 
-    @pl.when(idx[2] == 0)
+    @pl.when(lax.axis_index("core") == 0)
     def _():
         write(grad_a, grad_b)
 
-    @pl.when(idx[2] != 0)
+    @pl.when(lax.axis_index("core") != 0)
     def _():
         write(grad_b, grad_a)
 
 
 def call(kernel, outs, *args, scratch=(), limit=4, fetch=(), outside=0):
-    spaces = [pltpu.SMEM if a.dtype == jnp.int32 else pltpu.VMEM for a in args] + [pl.ANY] * len(fetch)
+    spaces = [pltpu.VMEM] * len(args) + [pl.ANY] * len(fetch)
     return pl.pallas_call(
         kernel,
         out_shape=outs,
@@ -294,7 +294,6 @@
 def per_device(view_a, view_b):
     rows, width = view_a.shape
     images, full, rx, cw = rows * 8, width * 2, rows // 4, rows * 2
-    idx = jnp.stack([lax.axis_index("x"), lax.axis_index("zh"), lax.axis_index("core")]).astype(jnp.int32)
     first = lax.axis_index("core") == 0
     keep = jnp.where(first, view_a, view_b)
     give = jnp.where(first, view_b, view_a)
@@ -323,18 +322,17 @@
     n, no, inv, p2lo, p2hi = call(
         functools.partial(norm_kernel, images),
         [like((images, full), bf16), like((images, width), bf16), like((8, full), f32), up, down],
-        *(idx, st, known),
+        *(st, known),
         fetch=blocks,
         scratch=[pltpu.VMEM((images - known.shape[0], full), bf16), pltpu.SemaphoreType.DMA((len(blocks),))],
     )
-    p0, p1lo, p1hi, p3lo, p3hi = call(
-        gram_kernel, [piece, up, down, up, down], idx, n, scratch=[pltpu.VMEM((rows, images), bf16)], limit=8
+    p0, p1, p3 = call(
+        gram_kernel, [piece] * 3, n, scratch=[pltpu.VMEM((rows, images), bf16)], limit=8
     )
     a, b = from_axis(p2lo, "x", 3), from_axis(p2hi, "x", 1)
-    c, d = from_axis(p1hi, "x", 3), from_axis(p3lo, "x", 1)
-    e, f = call(add_kernel, [up, down], p1lo, a, p3hi, b)
+    e, f = call(add_kernel, [piece] * 2, p1, a, p3, b)
     e, f = from_axis(e, "x", 3), from_axis(f, "x", 1)
-    q0, q1, q2, q3 = call(sum_x_kernel, [shard] * 4, idx, p0, d, e, c, f, scratch=[pltpu.VMEM((4, rx, cw), bf16)])
+    q0, q1, q2, q3 = call(sum_x_kernel, [shard] * 4, p0, e, f, scratch=[pltpu.VMEM((4, rx, cw), bf16)])
     no, inv, q1 = lax.optimization_barrier((no, inv, q1))
     o = from_pair(no, "core")
     inv_other = from_pair(inv[:, width:], "core")
@@ -348,13 +346,13 @@
     (mine,) = call(sum_z_kernel, [shard], q0, *got)
     theirs = from_pair(mine, "core")
     (pay,) = call(functools.partial(load_kernel, images), [like((rx, cw + 128), bf16)], mine, theirs, diag)
-    (pay,) = call(join_kernel, [like((rx, images + 128), bf16)], idx, pay, *ring(pay, "zh"))
+    (pay,) = call(join_kernel, [like((rx, images + 128), bf16)], pay, *ring(pay, "zh"))
     r1, r3, r2lo, r2hi = ring(pay, "x")
     wide, three, quarter = like((rows, width), f32), like((3 * rx, width), f32), like((rx, width), f32)
     my3, send3, acc = call(
         first_product_kernel,
         [three, three, like((8, full), f32)],
-        *(idx, pay, r1, r3, n),
+        *(pay, r1, r3, n),
         scratch=[pltpu.VMEM((3 * rx, images), bf16)],
         limit=8,
     )
@@ -362,7 +360,7 @@
     my1, send1, sums = call(
         last_product_kernel,
         [quarter, quarter, like((16, 8, width), f32)],
-        *(idx, r2lo, r2hi, n, acc),
+        *(r2lo, r2hi, n, acc),
         scratch=[pltpu.VMEM((rx, images), bf16)],
     )
     other1 = from_pair(send1, "core")
@@ -370,7 +368,7 @@
     loss, grad_a, grad_b = call(
         functools.partial(grad_kernel, images),
         [like((1, 1), f32), wide, wide],
-        *(idx, my3, my1, other3, other1, my_own, o_own, diag, sums, inv, inv_other),
+        *(my3, my1, other3, other1, my_own, o_own, diag, sums, inv, inv_other),
         scratch=[pltpu.VMEM((rows, width), f32), pltpu.VMEM((rows, width), f32), pltpu.SemaphoreType.DMA((8,))],
         outside=2,
     )

time: 146 us -> 142 us (0.973)
  Pallas kernels: 20.9 us -> 15.6 us
  waiting for transfers between devices: 63.8 us -> 66.7 us
  starting transfers between devices: 58.2 us -> 56.6 us
    pallas_call x12, Pallas kernels: 20.9 us -> 15.6 us  [call(): pl.pallas_call(kernel, out_shape=outs, in_specs=[pl.BlockSpec(memory_spac...]
    ppermute x23 -> x21, waiting for transfers between devices: 45.6 us -> 47.6 us  [from_axis(): return lax.ppermute(v, axis, [((i + k) % 4, i) for i in range(4)])]
    ppermute x23 -> x21, starting transfers between devices: 36.4 us -> 35.4 us  [from_axis(): return lax.ppermute(v, axis, [((i + k) % 4, i) for i in range(4)])]
  transfers between devices with their start and end apart: 33 -> 31, of which waited for: 18 -> 19; matrix products, arithmetic and copies ran while one was open for 0% -> 0% of each run, Pallas kernels for 8% -> 6%
where the time goes in v1:
time: 142 us; the launch traced here: 141 us
  waiting for transfers between devices  66.7 us (47%)
  starting transfers between devices  56.6 us (40%)
  Pallas kernels  15.6 us (11%)
    ppermute x21, waiting for transfers between devices, from_axis(): return lax.ppermute(v, axis, [((i + k) % 4, i) for i in range(4)])  47.6 us
    ppermute x21, starting transfers between devices, from_axis(): return lax.ppermute(v, axis, [((i + k) % 4, i) for i in range(4)])  35.4 us
    pallas_call x12, Pallas kernels, call(): pl.pallas_call(kernel, out_shape=outs, in_specs=[pl.BlockSpec(memory_spac...  15.6 us
    ppermute x9, starting transfers between devices, from_pair(): return lax.ppermute(v, axis, [(1, 0), (0, 1)])  15.2 us
    ppermute x9, waiting for transfers between devices, from_pair(): return lax.ppermute(v, axis, [(1, 0), (0, 1)])  13.3 us
    all_to_all x1, starting transfers between devices, per_device(): lax.all_to_all(sums, batch + ('core',), split_axis=0, concat_axis=0, tile...  6.01 us
    all_to_all x1, waiting for transfers between devices, per_device(): lax.all_to_all(sums, batch + ('core',), split_axis=0, concat_axis=0, tile...  5.77 us
  transfers between devices with their start and end apart: 31, of which 19 were waited for; matrix products, arithmetic and copies ran while one was open for 0% of the time, Pallas kernels for 6%

profile of v1, /device:TPU:1, one launch (start us, length us, event | category | flops | bytes accessed | tf_op | source)
XLA Modules:
  0.0 141.1 jit_solution(10000126014697672721)
XLA Ops:
  0.6 1.1 broadcast_select_fusion.1
  1.8 3.3 %collective-permute-start = (bf16[320,512]{1,0:T(8,128)(2,1)S(1)}, bf16[320,512]{1,0:T(8,128)(2,1)S(1)}, u32[]{:S(2)}, u32[]{:S(2)}) collective-permute-start(bf16[320,512]{1,0:T(8,128)(2,1)S(1)} %get-tuple-element.70), channel_id=1, source_target_pairs={{1,0},{0,1},{3,2},{2,3},{5,4},{4,5},{7,6},{6,7},{9,8},{8,9},{11,10... | collective-permute-start | bytes 983048 | tf_op jit(solution)/shard_map/ppermute | solution.py:26
  5.1 1.3 collective-permute-done
  6.3 0.1 pad_maximum_fusion.own
  6.4 0.1 collective-permute-start.3
  6.5 2.7 %collective-permute-start.2 = (bf16[320,1024]{1,0:T(8,128)(2,1)S(1)}, bf16[320,1024]{1,0:T(8,128)(2,1)S(1)}, u32[]{:S(2)}, u32[]{:S(2)}) collective-permute-start(bf16[320,1024]{1,0:T(8,128)(2,1)S(1)} %pad_maximum_fusion.own), channel_id=1, source_target_pairs={{64,0},{128,64},{192,128},{0,192},{65,1},{129,65},{193,129},{1,193... | collective-permute-start | bytes 1966088 | tf_op jit(solution)/shard_map/ppermute | solution.py:22
  9.2 0.0 collective-permute-start.1
  9.2 14.4 %collective-permute-done.3.refs_2_ = bf16[320,1024]{1,0:T(8,128)(2,1)S(1)} collective-permute-done((bf16[320,1024]{1,0:T(8,128)(2,1)S(1)}, bf16[320,1024]{1,0:T(8,128)(2,1)S(1)}, u32[]{:S(2)}, u32[]{:S(2)}) %collective-permute-start.3) | collective-permute-done | bytes 655392 | tf_op jit(solution)/shard_map/ppermute | solution.py:22
  23.7 0.1 collective-permute-start.5
  23.8 0.0 collective-permute-done.2.refs_1_
  23.8 2.7 %collective-permute-start.4 = (bf16[160,1024]{1,0:T(8,128)(2,1)S(1)}, bf16[160,1024]{1,0:T(8,128)(2,1)S(1)}, u32[]{:S(2)}, u32[]{:S(2)}) collective-permute-start(bf16[160,1024]{1,0:T(8,128)(2,1)S(1)} %slice.28), channel_id=1, source_target_pairs={{64,0},{128,64},{192,128},{0,192},{65,1},{129,65},{193,129},{1,193... | collective-permute-start | bytes 983048 | tf_op jit(solution)/shard_map/ppermute | solution.py:22
  26.6 2.7 %collective-permute-start.6 = (bf16[320,1024]{1,0:T(8,128)(2,1)S(1)}, bf16[320,1024]{1,0:T(8,128)(2,1)S(1)}, u32[]{:S(2)}, u32[]{:S(2)}) collective-permute-start(bf16[320,1024]{1,0:T(8,128)(2,1)S(1)} %collective-permute-done.1.refs_0_), channel_id=1, source_target_pairs={{64,0},{128,64},{192,128},{0,192},{65,1},{129,65},{193,129},{1,193... | collective-permute-start | bytes 1966088 | tf_op jit(solution)/shard_map/ppermute | solution.py:22
  29.2 3.7 %collective-permute-done.5.refs_4_ = bf16[160,1024]{1,0:T(8,128)(2,1)S(1)} collective-permute-done((bf16[160,1024]{1,0:T(8,128)(2,1)S(1)}, bf16[160,1024]{1,0:T(8,128)(2,1)S(1)}, u32[]{:S(2)}, u32[]{:S(2)}) %collective-permute-start.5) | collective-permute-done | bytes 327712 | tf_op jit(solution)/shard_map/ppermute | solution.py:22
  33.0 0.1 collective-permute-start.9
  33.1 1.4 collective-permute-start.8
  34.4 1.8 %shard_map.49 = (f32[24,1024]{1,0:T(8,128)S(1)}, bf16[1600,1024]{1,0:T(8,128)(2,1)S(1)}) custom-call(bf16[320,1024]{1,0:T(8,128)(2,1)S(1)} %pad_maximum_fusion.own, bf16[320,1024]{1,0:T(8,128)(2,1)S(1)} %collective-permute-done.1.refs_0_, bf16[320,1024]{1,0:T(8,128)(2,1)S(1)} %collective-permute-done.2.refs_1_, ...), custom_call_target="tpu_custom_call" | custom-call | tf_op jit(solution)/shard_map/pallas_call | solution.py:282
  36.3 2.9 %collective-permute-done.9.refs_3_ = bf16[160,1024]{1,0:T(8,128)(2,1)S(1)} collective-permute-done((bf16[160,1024]{1,0:T(8,128)(2,1)S(1)}, bf16[160,1024]{1,0:T(8,128)(2,1)S(1)}, u32[]{:S(2)}, u32[]{:S(2)}) %collective-permute-start.9) | collective-permute-done | bytes 327712 | tf_op jit(solution)/shard_map/ppermute | solution.py:26
  39.2 6.2 %collective-permute-done.8.refs_2_ = bf16[160,1024]{1,0:T(8,128)(2,1)S(1)} collective-permute-done((bf16[160,1024]{1,0:T(8,128)(2,1)S(1)}, bf16[160,1024]{1,0:T(8,128)(2,1)S(1)}, u32[]{:S(2)}, u32[]{:S(2)}) %collective-permute-start.8) | collective-permute-done | bytes 327712 | tf_op jit(solution)/shard_map/ppermute | solution.py:26
  45.4 1.7 %collective-permute-done.7.refs_1_ = bf16[320,1024]{1,0:T(8,128)(2,1)S(1)} collective-permute-done((bf16[320,1024]{1,0:T(8,128)(2,1)S(1)}, bf16[320,1024]{1,0:T(8,128)(2,1)S(1)}, u32[]{:S(2)}, u32[]{:S(2)}) %collective-permute-start.7) | collective-permute-done | bytes 655392 | tf_op jit(solution)/shard_map/ppermute | solution.py:22
  47.0 4.6 %shard_map.50 = (bf16[2560,1024]{1,0:T(8,128)(2,1)S(1)}, bf16[2560,512]{1,0:T(8,128)(2,1)S(1)}, f32[8,1024]{1,0:T(8,128)S(1)}, bf16[48,2560]{1,0:T(8,128)(2,1)S(1)}, bf16[32,2560]{1,0:T(8,128)(2,1)S(1)}) custom-call(f32[24,1024]{1,0:T(8,128)S(1)} %get-tuple-element.36.st, bf16[1600,1024]{1,0:T(8,128)(2,1)S(1)} %get-tuple-element.37.known, ...), custom_call_target="tpu_custom_call" | custom-call | tf_op jit(solution)/shard_map/pallas_call | solution.py:282
  51.6 0.1 collective-permute-start.10
  51.7 2.7 %collective-permute-start.11 = (bf16[32,2560]{1,0:T(8,128)(2,1)S(1)}, bf16[32,2560]{1,0:T(8,128)(2,1)S(1)}, u32[]{:S(2)}, u32[]{:S(2)}) collective-permute-start(bf16[32,2560]{1,0:T(8,128)(2,1)S(1)} %get-tuple-element.43), channel_id=1, source_target_pairs={{8,0},{16,8},{24,16},{0,24},{9,1},{17,9},{25,17},{1,25},{10,2},{18... | collective-permute-start | bytes 491528 | tf_op jit(solution)/shard_map/ppermute | solution.py:22
  54.4 2.4 %shard_map.51 = (bf16[80,2560]{1,0:T(8,128)(2,1)S(1)}, bf16[80,2560]{1,0:T(8,128)(2,1)S(1)}, bf16[80,2560]{1,0:T(8,128)(2,1)S(1)}) custom-call(bf16[2560,1024]{1,0:T(8,128)(2,1)S(1)} %get-tuple-element.38.n), custom_call_target="tpu_custom_call" | custom-call | tf_op jit(solution)/shard_map/pallas_call | solution.py:282
  56.8 1.2 collective-permute-done.10.a
  58.0 0.1 shard_map.52
  58.1 0.1 collective-permute-start.12
  58.2 2.7 %collective-permute-start.13 = (bf16[80,2560]{1,0:T(8,128)(2,1)S(1)}, bf16[80,2560]{1,0:T(8,128)(2,1)S(1)}, u32[]{:S(2)}, u32[]{:S(2)}) collective-permute-start(bf16[80,2560]{1,0:T(8,128)(2,1)S(1)} %get-tuple-element.45), channel_id=1, source_target_pairs={{8,0},{16,8},{24,16},{0,24},{9,1},{17,9},{25,17},{1,25},{10,2},{18... | collective-permute-start | bytes 1228808 | tf_op jit(solution)/shard_map/ppermute | solution.py:22
  60.8 5.3 %collective-permute-done.12.e = bf16[80,2560]{1,0:T(8,128)(2,1)S(1)} collective-permute-done((bf16[80,2560]{1,0:T(8,128)(2,1)S(1)}, bf16[80,2560]{1,0:T(8,128)(2,1)S(1)}, u32[]{:S(2)}, u32[]{:S(2)}) %collective-permute-start.12) | collective-permute-done | bytes 409632 | tf_op jit(solution)/shard_map/ppermute | solution.py:22
  66.2 0.2 shard_map.53
  66.4 5.5 %collective-permute-start.14 = (bf16[2560,512]{1,0:T(8,128)(2,1)S(1)}, bf16[2560,512]{1,0:T(8,128)(2,1)S(1)}, u32[]{:S(2)}, u32[]{:S(2)}) collective-permute-start(bf16[2560,512]{1,0:T(8,128)(2,1)S(1)} %get-tuple-element.50), channel_id=1, source_target_pairs={{1,0},{0,1},{3,2},{2,3},{5,4},{4,5},{7,6},{6,7},{9,8},{8,9},{11,10... | collective-permute-start | bytes 7864328 | tf_op jit(solution)/shard_map/ppermute | solution.py:26
  71.9 1.8 %collective-permute-start.17 = (bf16[80,640]{1,0:T(8,128)(2,1)S(1)}, bf16[80,640]{1,0:T(8,128)(2,1)S(1)}, u32[]{:S(2)}, u32[]{:S(2)}) collective-permute-start(bf16[80,640]{1,0:T(8,128)(2,1)S(1)} %get-tuple-element.55), channel_id=1, source_target_pairs={{6,0},{0,2},{2,4},{4,6},{7,1},{1,3},{3,5},{5,7},{14,8},{8,10},{10,... | collective-permute-start | bytes 307208 | tf_op jit(solution)/shard_map/ppermute | solution.py:22
  73.7 4.8 %collective-permute-start.16 = (bf16[80,640]{1,0:T(8,128)(2,1)S(1)}, bf16[80,640]{1,0:T(8,128)(2,1)S(1)}, u32[]{:S(2)}, u32[]{:S(2)}) collective-permute-start(bf16[80,640]{1,0:T(8,128)(2,1)S(1)} %get-tuple-element.54), channel_id=1, source_target_pairs={{4,0},{6,2},{0,4},{2,6},{5,1},{7,3},{1,5},{3,7},{12,8},{14,10},{8,... | collective-permute-start | bytes 307208 | tf_op jit(solution)/shard_map/ppermute | solution.py:22
  78.5 2.4 %collective-permute-start.18 = (bf16[80,640]{1,0:T(8,128)(2,1)S(1)}, bf16[80,640]{1,0:T(8,128)(2,1)S(1)}, u32[]{:S(2)}, u32[]{:S(2)}) collective-permute-start(bf16[80,640]{1,0:T(8,128)(2,1)S(1)} %get-tuple-element.56), channel_id=1, source_target_pairs={{2,0},{4,2},{6,4},{0,6},{3,1},{5,3},{7,5},{1,7},{10,8},{12,10},{14... | collective-permute-start | bytes 307208 | tf_op jit(solution)/shard_map/ppermute | solution.py:22
  80.9 0.9 collective-permute-start.15
  81.8 0.8 collective-permute-done.15.inv_o
  82.6 1.1 shard_map.54
  83.7 2.1 %collective-permute-done.16.r1 = bf16[80,640]{1,0:T(8,128)(2,1)S(1)} collective-permute-done((bf16[80,640]{1,0:T(8,128)(2,1)S(1)}, bf16[80,640]{1,0:T(8,128)(2,1)S(1)}, u32[]{:S(2)}, u32[]{:S(2)}) %collective-permute-start.16) | collective-permute-done | bytes 102432 | tf_op jit(solution)/shard_map/ppermute | solution.py:22
  85.9 3.0 %collective-permute-done.18.r3 = bf16[80,640]{1,0:T(8,128)(2,1)S(1)} collective-permute-done((bf16[80,640]{1,0:T(8,128)(2,1)S(1)}, bf16[80,640]{1,0:T(8,128)(2,1)S(1)}, u32[]{:S(2)}, u32[]{:S(2)}) %collective-permute-start.18) | collective-permute-done | bytes 102432 | tf_op jit(solution)/shard_map/ppermute | solution.py:22
  88.8 0.1 shard_map.55.mine
  88.9 0.6 collective-permute-start.19
  89.5 0.9 collective-permute-done.19.theirs
  90.4 0.1 shard_map.56.own
  90.6 1.5 %collective-permute-start.20 = (bf16[80,768]{1,0:T(8,128)(2,1)S(1)}, bf16[80,768]{1,0:T(8,128)(2,1)S(1)}, u32[]{:S(2)}, u32[]{:S(2)}) collective-permute-start(bf16[80,768]{1,0:T(8,128)(2,1)S(1)} %shard_map.56.own), channel_id=1, source_target_pairs={{6,0},{0,2},{2,4},{4,6},{7,1},{1,3},{3,5},{5,7},{14,8},{8,10},{10,... | collective-permute-start | bytes 368648 | tf_op jit(solution)/shard_map/ppermute | solution.py:22
  92.0 2.2 %collective-permute-start.21 = (bf16[80,768]{1,0:T(8,128)(2,1)S(1)}, bf16[80,768]{1,0:T(8,128)(2,1)S(1)}, u32[]{:S(2)}, u32[]{:S(2)}) collective-permute-start(bf16[80,768]{1,0:T(8,128)(2,1)S(1)} %shard_map.56.own), channel_id=1, source_target_pairs={{2,0},{4,2},{6,4},{0,6},{3,1},{5,3},{7,5},{1,7},{10,8},{12,10},{14... | collective-permute-start | bytes 368648 | tf_op jit(solution)/shard_map/ppermute | solution.py:22
  94.2 5.7 %collective-permute-done.20.r1 = bf16[80,768]{1,0:T(8,128)(2,1)S(1)} collective-permute-done((bf16[80,768]{1,0:T(8,128)(2,1)S(1)}, bf16[80,768]{1,0:T(8,128)(2,1)S(1)}, u32[]{:S(2)}, u32[]{:S(2)}) %collective-permute-start.20) | collective-permute-done | bytes 122912 | tf_op jit(solution)/shard_map/ppermute | solution.py:22
  99.9 0.3 collective-permute-start.22
  100.2 0.7 collective-permute-done.21.r3
  100.9 2.6 %collective-permute-start.23 = (bf16[32,768]{1,0:T(8,128)(2,1)S(1)}, bf16[32,768]{1,0:T(8,128)(2,1)S(1)}, u32[]{:S(2)}, u32[]{:S(2)}) collective-permute-start(bf16[32,768]{1,0:T(8,128)(2,1)S(1)} %slice.31), channel_id=1, source_target_pairs={{2,0},{4,2},{6,4},{0,6},{3,1},{5,3},{7,5},{1,7},{10,8},{12,10},{14... | collective-permute-start | bytes 147464 | tf_op jit(solution)/shard_map/ppermute | solution.py:22
  103.6 1.4 collective-permute-done.23.r2hi
  105.0 0.3 collective-permute-done.22.r2lo
  105.2 0.1 shard_map.57.own
  105.3 1.2 collective-permute-start.24
  106.5 2.1 %collective-permute-start.25 = (bf16[80,2688]{1,0:T(8,128)(2,1)S(1)}, bf16[80,2688]{1,0:T(8,128)(2,1)S(1)}, u32[]{:S(2)}, u32[]{:S(2)}) collective-permute-start(bf16[80,2688]{1,0:T(8,128)(2,1)S(1)} %shard_map.57.own), channel_id=1, source_target_pairs={{8,0},{16,8},{24,16},{0,24},{9,1},{17,9},{25,17},{1,25},{10,2},{18... | collective-permute-start | bytes 1290248 | tf_op jit(solution)/shard_map/ppermute | solution.py:22
  108.7 8.0 %collective-permute-done.24.r1 = bf16[80,2688]{1,0:T(8,128)(2,1)S(1)} collective-permute-done((bf16[80,2688]{1,0:T(8,128)(2,1)S(1)}, bf16[80,2688]{1,0:T(8,128)(2,1)S(1)}, u32[]{:S(2)}, u32[]{:S(2)}) %collective-permute-start.24) | collective-permute-done | bytes 430112 | tf_op jit(solution)/shard_map/ppermute | solution.py:22
  116.7 0.1 collective-permute-start.26
  116.8 2.7 %collective-permute-start.27 = (bf16[32,2688]{1,0:T(8,128)(2,1)S(1)}, bf16[32,2688]{1,0:T(8,128)(2,1)S(1)}, u32[]{:S(2)}, u32[]{:S(2)}) collective-permute-start(bf16[32,2688]{1,0:T(8,128)(2,1)S(1)} %slice.33), channel_id=1, source_target_pairs={{8,0},{16,8},{24,16},{0,24},{9,1},{17,9},{25,17},{1,25},{10,2},{18... | collective-permute-start | bytes 516104 | tf_op jit(solution)/shard_map/ppermute | solution.py:22
  119.5 1.5 %shard_map.58 = (f32[240,512]{1,0:T(8,128)S(1)}, f32[240,512]{1,0:T(8,128)S(1)}, f32[8,1024]{1,0:T(8,128)S(1)}) custom-call(bf16[80,2688]{1,0:T(8,128)(2,1)S(1)} %shard_map.57.own, bf16[80,2688]{1,0:T(8,128)(2,1)S(1)} %collective-permute-done.24.r1, bf16[80,2688]{1,0:T(8,128)(2,1)S(1)} %collective-permute-done.25.r3, bf16[2560,1024]{1,0:T(8,128)(2,1)S(1)} %get-tuple-element.38.n), custom_call_target="tpu_custom_call" | custom-call | tf_op jit(solution)/shard_map/pallas_call | solution.py:282
  121.1 3.2 %collective-permute-start.28 = (f32[240,512]{1,0:T(8,128)S(1)}, f32[240,512]{1,0:T(8,128)S(1)}, u32[]{:S(2)}, u32[]{:S(2)}) collective-permute-start(f32[240,512]{1,0:T(8,128)S(1)} %get-tuple-element.60), channel_id=1, source_target_pairs={{1,0},{0,1},{3,2},{2,3},{5,4},{4,5},{7,6},{6,7},{9,8},{8,9},{11,10... | collective-permute-start | bytes 1474568 | tf_op jit(solution)/shard_map/ppermute | solution.py:26
  124.3 1.8 %shard_map.59 = (f32[80,512]{1,0:T(8,128)S(1)}, f32[80,512]{1,0:T(8,128)S(1)}, f32[16,8,512]{2,1,0:T(8,128)}) custom-call(bf16[48,2688]{1,0:T(8,128)(2,1)S(1)} %collective-permute-done.26.r2lo, bf16[32,2688]{1,0:T(8,128)(2,1)S(1)} %collective-permute-done.27.r2hi, bf16[2560,1024]{1,0:T(8,128)(2,1)S(1)} %get-tuple-element.38.n, ...), custom_call_target="tpu_custom_call" | custom-call | tf_op jit(solution)/shard_map/pallas_call | solution.py:282
  126.1 6.0 %all-to-all-start = ((f32[16,8,512]{2,1,0:T(8,128)}), f32[16,8,512]{2,1,0:T(8,128)S(1)}, u32[]{:S(2)}, u32[]{:S(2)}) async-start(f32[16,8,512]{2,1,0:T(8,128)} %get-tuple-element.64), calls=%async_computation | async-start | bytes 524288 | tf_op jit(solution)/shard_map/all_to_all | solution.py:367
  132.1 0.2 collective-permute-start.29
  132.3 1.2 collective-permute-done.29.other1
  133.5 5.8 %all-to-all-done.sums = f32[16,8,512]{2,1,0:T(8,128)S(1)} async-done(((f32[16,8,512]{2,1,0:T(8,128)}), f32[16,8,512]{2,1,0:T(8,128)S(1)}, u32[]{:S(2)}, u32[]{:S(2)}) %all-to-all-start) | async-done | bytes 262176 | tf_op jit(solution)/shard_map/all_to_all | solution.py:367
  139.3 1.7 %shard_map.60 = (f32[1,1]{1,0:T(1,128)}, f32[320,512]{1,0:T(8,128)}, f32[320,512]{1,0:T(8,128)}) custom-call(f32[240,512]{1,0:T(8,128)S(1)} %get-tuple-element.57.my3, f32[80,512]{1,0:T(8,128)S(1)} %get-tuple-element.59.my1, f32[240,512]{1,0:T(8,128)S(1)} %collective-permute-done.28.other3, f32[80,512]{1,0:T(8,128)S(1)} %collective-permute-done.29.other1, ...), custom_call_target="tpu_custom_call" | custom-call | tf_op jit(solution)/shard_map/pallas_call | solution.py:282
  (19 shorter events, 0.1 us)
Async XLA Ops:
  1.8 4.6 %collective-permute-start = (bf16[320,512]{1,0:T(8,128)(2,1)S(1)}, bf16[320,512]{1,0:T(8,128)(2,1)S(1)}, u32[]{:S(2)}, u32[]{:S(2)}) collective-permute-start(bf16[320,512]{1,0:T(8,128)(2,1)S(1)} %get-tuple-element.70), channel_id=1, source_target_pairs={{1,0},{0,1},{3,2},{2,3},{5,4},{4,5},{7,6},{6,7},{9,8},{8,9},{11,10... | collective-permute-start | bytes 983048 | tf_op jit(solution)/shard_map/ppermute | solution.py:26
  6.4 17.2 %collective-permute-start.3 = (bf16[320,1024]{1,0:T(8,128)(2,1)S(1)}, bf16[320,1024]{1,0:T(8,128)(2,1)S(1)}, u32[]{:S(2)}, u32[]{:S(2)}) collective-permute-start(bf16[320,1024]{1,0:T(8,128)(2,1)S(1)} %pad_maximum_fusion.own), channel_id=1, source_target_pairs={{192,0},{0,64},{64,128},{128,192},{193,1},{1,65},{65,129},{129,193... | collective-permute-start | bytes 1966088 | tf_op jit(solution)/shard_map/ppermute | solution.py:22
  6.5 17.3 %collective-permute-start.2 = (bf16[320,1024]{1,0:T(8,128)(2,1)S(1)}, bf16[320,1024]{1,0:T(8,128)(2,1)S(1)}, u32[]{:S(2)}, u32[]{:S(2)}) collective-permute-start(bf16[320,1024]{1,0:T(8,128)(2,1)S(1)} %pad_maximum_fusion.own), channel_id=1, source_target_pairs={{64,0},{128,64},{192,128},{0,192},{65,1},{129,65},{193,129},{1,193... | collective-permute-start | bytes 1966088 | tf_op jit(solution)/shard_map/ppermute | solution.py:22
  9.2 17.4 %collective-permute-start.1 = (bf16[320,1024]{1,0:T(8,128)(2,1)S(1)}, bf16[320,1024]{1,0:T(8,128)(2,1)S(1)}, u32[]{:S(2)}, u32[]{:S(2)}) collective-permute-start(bf16[320,1024]{1,0:T(8,128)(2,1)S(1)} %pad_maximum_fusion.own), channel_id=1, source_target_pairs={{32,0},{0,32},{33,1},{1,33},{34,2},{2,34},{35,3},{3,35},{36,4},{4,... | collective-permute-start | bytes 1966088 | tf_op jit(solution)/shard_map/ppermute | solution.py:26
  23.7 9.3 %collective-permute-start.5 = (bf16[160,1024]{1,0:T(8,128)(2,1)S(1)}, bf16[160,1024]{1,0:T(8,128)(2,1)S(1)}, u32[]{:S(2)}, u32[]{:S(2)}) collective-permute-start(bf16[160,1024]{1,0:T(8,128)(2,1)S(1)} %slice.29), channel_id=1, source_target_pairs={{192,0},{0,64},{64,128},{128,192},{193,1},{1,65},{65,129},{129,193... | collective-permute-start | bytes 983048 | tf_op jit(solution)/shard_map/ppermute | solution.py:22
  23.8 9.3 %collective-permute-start.4 = (bf16[160,1024]{1,0:T(8,128)(2,1)S(1)}, bf16[160,1024]{1,0:T(8,128)(2,1)S(1)}, u32[]{:S(2)}, u32[]{:S(2)}) collective-permute-start(bf16[160,1024]{1,0:T(8,128)(2,1)S(1)} %slice.28), channel_id=1, source_target_pairs={{64,0},{128,64},{192,128},{0,192},{65,1},{129,65},{193,129},{1,193... | collective-permute-start | bytes 983048 | tf_op jit(solution)/shard_map/ppermute | solution.py:22
  26.5 20.5 %collective-permute-start.7 = (bf16[320,1024]{1,0:T(8,128)(2,1)S(1)}, bf16[320,1024]{1,0:T(8,128)(2,1)S(1)}, u32[]{:S(2)}, u32[]{:S(2)}) collective-permute-start(bf16[320,1024]{1,0:T(8,128)(2,1)S(1)} %collective-permute-done.1.refs_0_), channel_id=1, source_target_pairs={{192,0},{0,64},{64,128},{128,192},{193,1},{1,65},{65,129},{129,193... | collective-permute-start | bytes 1966088 | tf_op jit(solution)/shard_map/ppermute | solution.py:22
  26.6 20.5 %collective-permute-start.6 = (bf16[320,1024]{1,0:T(8,128)(2,1)S(1)}, bf16[320,1024]{1,0:T(8,128)(2,1)S(1)}, u32[]{:S(2)}, u32[]{:S(2)}) collective-permute-start(bf16[320,1024]{1,0:T(8,128)(2,1)S(1)} %collective-permute-done.1.refs_0_), channel_id=1, source_target_pairs={{64,0},{128,64},{192,128},{0,192},{65,1},{129,65},{193,129},{1,193... | collective-permute-start | bytes 1966088 | tf_op jit(solution)/shard_map/ppermute | solution.py:22
  33.0 6.2 %collective-permute-start.9 = (bf16[160,1024]{1,0:T(8,128)(2,1)S(1)}, bf16[160,1024]{1,0:T(8,128)(2,1)S(1)}, u32[]{:S(2)}, u32[]{:S(2)}) collective-permute-start(bf16[160,1024]{1,0:T(8,128)(2,1)S(1)} %collective-permute-done.5.refs_4_), channel_id=1, source_target_pairs={{32,0},{0,32},{33,1},{1,33},{34,2},{2,34},{35,3},{3,35},{36,4},{4,... | collective-permute-start | bytes 983048 | tf_op jit(solution)/shard_map/ppermute | solution.py:26
  33.1 12.3 %collective-permute-start.8 = (bf16[160,1024]{1,0:T(8,128)(2,1)S(1)}, bf16[160,1024]{1,0:T(8,128)(2,1)S(1)}, u32[]{:S(2)}, u32[]{:S(2)}) collective-permute-start(bf16[160,1024]{1,0:T(8,128)(2,1)S(1)} %collective-permute-done.4.refs_3_), channel_id=1, source_target_pairs={{32,0},{0,32},{33,1},{1,33},{34,2},{2,34},{35,3},{3,35},{36,4},{4,... | collective-permute-start | bytes 983048 | tf_op jit(solution)/shard_map/ppermute | solution.py:26
  51.6 6.3 %collective-permute-start.10 = (bf16[48,2560]{1,0:T(8,128)(2,1)S(1)}, bf16[48,2560]{1,0:T(8,128)(2,1)S(1)}, u32[]{:S(2)}, u32[]{:S(2)}) collective-permute-start(bf16[48,2560]{1,0:T(8,128)(2,1)S(1)} %get-tuple-element.41), channel_id=1, source_target_pairs={{24,0},{0,8},{8,16},{16,24},{25,1},{1,9},{9,17},{17,25},{26,2},{2,... | collective-permute-start | bytes 737288 | tf_op jit(solution)/shard_map/ppermute | solution.py:22
  51.7 5.0 %collective-permute-start.11 = (bf16[32,2560]{1,0:T(8,128)(2,1)S(1)}, bf16[32,2560]{1,0:T(8,128)(2,1)S(1)}, u32[]{:S(2)}, u32[]{:S(2)}) collective-permute-start(bf16[32,2560]{1,0:T(8,128)(2,1)S(1)} %get-tuple-element.43), channel_id=1, source_target_pairs={{8,0},{16,8},{24,16},{0,24},{9,1},{17,9},{25,17},{1,25},{10,2},{18... | collective-permute-start | bytes 491528 | tf_op jit(solution)/shard_map/ppermute | solution.py:22
  58.1 8.1 %collective-permute-start.12 = (bf16[80,2560]{1,0:T(8,128)(2,1)S(1)}, bf16[80,2560]{1,0:T(8,128)(2,1)S(1)}, u32[]{:S(2)}, u32[]{:S(2)}) collective-permute-start(bf16[80,2560]{1,0:T(8,128)(2,1)S(1)} %get-tuple-element.44), channel_id=1, source_target_pairs={{24,0},{0,8},{8,16},{16,24},{25,1},{1,9},{9,17},{17,25},{26,2},{2,... | collective-permute-start | bytes 1228808 | tf_op jit(solution)/shard_map/ppermute | solution.py:22
  58.2 8.0 %collective-permute-start.13 = (bf16[80,2560]{1,0:T(8,128)(2,1)S(1)}, bf16[80,2560]{1,0:T(8,128)(2,1)S(1)}, u32[]{:S(2)}, u32[]{:S(2)}) collective-permute-start(bf16[80,2560]{1,0:T(8,128)(2,1)S(1)} %get-tuple-element.45), channel_id=1, source_target_pairs={{8,0},{16,8},{24,16},{0,24},{9,1},{17,9},{25,17},{1,25},{10,2},{18... | collective-permute-start | bytes 1228808 | tf_op jit(solution)/shard_map/ppermute | solution.py:22
  66.4 16.2 %collective-permute-start.14 = (bf16[2560,512]{1,0:T(8,128)(2,1)S(1)}, bf16[2560,512]{1,0:T(8,128)(2,1)S(1)}, u32[]{:S(2)}, u32[]{:S(2)}) collective-permute-start(bf16[2560,512]{1,0:T(8,128)(2,1)S(1)} %get-tuple-element.50), channel_id=1, source_target_pairs={{1,0},{0,1},{3,2},{2,3},{5,4},{4,5},{7,6},{6,7},{9,8},{8,9},{11,10... | collective-permute-start | bytes 7864328 | tf_op jit(solution)/shard_map/ppermute | solution.py:26
  71.9 11.8 %collective-permute-start.17 = (bf16[80,640]{1,0:T(8,128)(2,1)S(1)}, bf16[80,640]{1,0:T(8,128)(2,1)S(1)}, u32[]{:S(2)}, u32[]{:S(2)}) collective-permute-start(bf16[80,640]{1,0:T(8,128)(2,1)S(1)} %get-tuple-element.55), channel_id=1, source_target_pairs={{6,0},{0,2},{2,4},{4,6},{7,1},{1,3},{3,5},{5,7},{14,8},{8,10},{10,... | collective-permute-start | bytes 307208 | tf_op jit(solution)/shard_map/ppermute | solution.py:22
  73.7 12.2 %collective-permute-start.16 = (bf16[80,640]{1,0:T(8,128)(2,1)S(1)}, bf16[80,640]{1,0:T(8,128)(2,1)S(1)}, u32[]{:S(2)}, u32[]{:S(2)}) collective-permute-start(bf16[80,640]{1,0:T(8,128)(2,1)S(1)} %get-tuple-element.54), channel_id=1, source_target_pairs={{4,0},{6,2},{0,4},{2,6},{5,1},{7,3},{1,5},{3,7},{12,8},{14,10},{8,... | collective-permute-start | bytes 307208 | tf_op jit(solution)/shard_map/ppermute | solution.py:22
  78.5 10.4 %collective-permute-start.18 = (bf16[80,640]{1,0:T(8,128)(2,1)S(1)}, bf16[80,640]{1,0:T(8,128)(2,1)S(1)}, u32[]{:S(2)}, u32[]{:S(2)}) collective-permute-start(bf16[80,640]{1,0:T(8,128)(2,1)S(1)} %get-tuple-element.56), channel_id=1, source_target_pairs={{2,0},{4,2},{6,4},{0,6},{3,1},{5,3},{7,5},{1,7},{10,8},{12,10},{14... | collective-permute-start | bytes 307208 | tf_op jit(solution)/shard_map/ppermute | solution.py:22
  80.9 1.8 %collective-permute-start.15 = (f32[8,512]{1,0:T(8,128)S(1)}, f32[8,512]{1,0:T(8,128)S(1)}, u32[]{:S(2)}, u32[]{:S(2)}) collective-permute-start(f32[8,512]{1,0:T(8,128)S(1)} %slice.23), channel_id=1, source_target_pairs={{1,0},{0,1},{3,2},{2,3},{5,4},{4,5},{7,6},{6,7},{9,8},{8,9},{11,10... | collective-permute-start | bytes 49160 | tf_op jit(solution)/shard_map/ppermute | solution.py:26
  88.9 1.5 %collective-permute-start.19 = (bf16[80,640]{1,0:T(8,128)(2,1)S(1)}, bf16[80,640]{1,0:T(8,128)(2,1)S(1)}, u32[]{:S(2)}, u32[]{:S(2)}) collective-permute-start(bf16[80,640]{1,0:T(8,128)(2,1)S(1)} %shard_map.55.mine), channel_id=1, source_target_pairs={{1,0},{0,1},{3,2},{2,3},{5,4},{4,5},{7,6},{6,7},{9,8},{8,9},{11,10... | collective-permute-start | bytes 307208 | tf_op jit(solution)/shard_map/ppermute | solution.py:26
  90.6 9.3 %collective-permute-start.20 = (bf16[80,768]{1,0:T(8,128)(2,1)S(1)}, bf16[80,768]{1,0:T(8,128)(2,1)S(1)}, u32[]{:S(2)}, u32[]{:S(2)}) collective-permute-start(bf16[80,768]{1,0:T(8,128)(2,1)S(1)} %shard_map.56.own), channel_id=1, source_target_pairs={{6,0},{0,2},{2,4},{4,6},{7,1},{1,3},{3,5},{5,7},{14,8},{8,10},{10,... | collective-permute-start | bytes 368648 | tf_op jit(solution)/shard_map/ppermute | solution.py:22
  92.0 8.9 %collective-permute-start.21 = (bf16[80,768]{1,0:T(8,128)(2,1)S(1)}, bf16[80,768]{1,0:T(8,128)(2,1)S(1)}, u32[]{:S(2)}, u32[]{:S(2)}) collective-permute-start(bf16[80,768]{1,0:T(8,128)(2,1)S(1)} %shard_map.56.own), channel_id=1, source_target_pairs={{2,0},{4,2},{6,4},{0,6},{3,1},{5,3},{7,5},{1,7},{10,8},{12,10},{14... | collective-permute-start | bytes 368648 | tf_op jit(solution)/shard_map/ppermute | solution.py:22
  99.9 5.3 %collective-permute-start.22 = (bf16[48,768]{1,0:T(8,128)(2,1)S(1)}, bf16[48,768]{1,0:T(8,128)(2,1)S(1)}, u32[]{:S(2)}, u32[]{:S(2)}) collective-permute-start(bf16[48,768]{1,0:T(8,128)(2,1)S(1)} %slice.30), channel_id=1, source_target_pairs={{6,0},{0,2},{2,4},{4,6},{7,1},{1,3},{3,5},{5,7},{14,8},{8,10},{10,... | collective-permute-start | bytes 221192 | tf_op jit(solution)/shard_map/ppermute | solution.py:22
  100.9 4.0 %collective-permute-start.23 = (bf16[32,768]{1,0:T(8,128)(2,1)S(1)}, bf16[32,768]{1,0:T(8,128)(2,1)S(1)}, u32[]{:S(2)}, u32[]{:S(2)}) collective-permute-start(bf16[32,768]{1,0:T(8,128)(2,1)S(1)} %slice.31), channel_id=1, source_target_pairs={{2,0},{4,2},{6,4},{0,6},{3,1},{5,3},{7,5},{1,7},{10,8},{12,10},{14... | collective-permute-start | bytes 147464 | tf_op jit(solution)/shard_map/ppermute | solution.py:22
  105.3 11.3 %collective-permute-start.24 = (bf16[80,2688]{1,0:T(8,128)(2,1)S(1)}, bf16[80,2688]{1,0:T(8,128)(2,1)S(1)}, u32[]{:S(2)}, u32[]{:S(2)}) collective-permute-start(bf16[80,2688]{1,0:T(8,128)(2,1)S(1)} %shard_map.57.own), channel_id=1, source_target_pairs={{24,0},{0,8},{8,16},{16,24},{25,1},{1,9},{9,17},{17,25},{26,2},{2,... | collective-permute-start | bytes 1290248 | tf_op jit(solution)/shard_map/ppermute | solution.py:22
  106.5 10.3 %collective-permute-start.25 = (bf16[80,2688]{1,0:T(8,128)(2,1)S(1)}, bf16[80,2688]{1,0:T(8,128)(2,1)S(1)}, u32[]{:S(2)}, u32[]{:S(2)}) collective-permute-start(bf16[80,2688]{1,0:T(8,128)(2,1)S(1)} %shard_map.57.own), channel_id=1, source_target_pairs={{8,0},{16,8},{24,16},{0,24},{9,1},{17,9},{25,17},{1,25},{10,2},{18... | collective-permute-start | bytes 1290248 | tf_op jit(solution)/shard_map/ppermute | solution.py:22
  116.7 7.6 %collective-permute-start.26 = (bf16[48,2688]{1,0:T(8,128)(2,1)S(1)}, bf16[48,2688]{1,0:T(8,128)(2,1)S(1)}, u32[]{:S(2)}, u32[]{:S(2)}) collective-permute-start(bf16[48,2688]{1,0:T(8,128)(2,1)S(1)} %slice.32), channel_id=1, source_target_pairs={{24,0},{0,8},{8,16},{16,24},{25,1},{1,9},{9,17},{17,25},{26,2},{2,... | collective-permute-start | bytes 774152 | tf_op jit(solution)/shard_map/ppermute | solution.py:22
  116.8 7.5 %collective-permute-start.27 = (bf16[32,2688]{1,0:T(8,128)(2,1)S(1)}, bf16[32,2688]{1,0:T(8,128)(2,1)S(1)}, u32[]{:S(2)}, u32[]{:S(2)}) collective-permute-start(bf16[32,2688]{1,0:T(8,128)(2,1)S(1)} %slice.33), channel_id=1, source_target_pairs={{8,0},{16,8},{24,16},{0,24},{9,1},{17,9},{25,17},{1,25},{10,2},{18... | collective-permute-start | bytes 516104 | tf_op jit(solution)/shard_map/ppermute | solution.py:22
  121.1 12.4 %collective-permute-start.28 = (f32[240,512]{1,0:T(8,128)S(1)}, f32[240,512]{1,0:T(8,128)S(1)}, u32[]{:S(2)}, u32[]{:S(2)}) collective-permute-start(f32[240,512]{1,0:T(8,128)S(1)} %get-tuple-element.60), channel_id=1, source_target_pairs={{1,0},{0,1},{3,2},{2,3},{5,4},{4,5},{7,6},{6,7},{9,8},{8,9},{11,10... | collective-permute-start | bytes 1474568 | tf_op jit(solution)/shard_map/ppermute | solution.py:26
  126.1 13.2 %all-to-all-start = ((f32[16,8,512]{2,1,0:T(8,128)}), f32[16,8,512]{2,1,0:T(8,128)S(1)}, u32[]{:S(2)}, u32[]{:S(2)}) async-start(f32[16,8,512]{2,1,0:T(8,128)} %get-tuple-element.64), calls=%async_computation | async-start | bytes 524288 | tf_op jit(solution)/shard_map/all_to_all | solution.py:367
  132.1 1.4 collective-permute-start.29

commit v2 on v1

--- a/solution.py
+++ b/solution.py
@@ -174,17 +174,20 @@
     return jnp.sum(ref[0:8, width:].astype(f32)[0:1, :], 1, keepdims=True)
 
 
-def join_kernel(own, r1, r3, r2lo, r2hi, pay):
-    rx, cw, low = own.shape[0], own.shape[1] - 128, r2lo.shape[0]
+def first_join_kernel(own, r1, r3, pay):
+    cw = pay.shape[1] // 3
+    for i, r in enumerate((own, r1, r3)):
+        pay[:, i * cw : i * cw + cw] = r[:, :cw]
+
+
+def last_join_kernel(own, r1, r3, r2lo, r2hi, pay):
+    (low, cw), rx = (r2lo.shape[0], r2lo.shape[1] - 128), pay.shape[0]
     part = jnp.zeros((1, 1), f32)
-    at = [pl.multiple_of(lax.rem(lax.axis_index("zh") + k, 4) * cw, 128) for k in range(4)]
-    for k, r in ((0, own), (3, r1), (1, r3)):
-        pay[:, pl.ds(at[k], cw)] = r[:, :cw]
+    for r in (own, r1, r3, r2lo):
         part = part + lane_sum(r, cw)
-    pay[0:low, pl.ds(at[2], cw)] = r2lo[:, :cw]
-    pay[low:, pl.ds(at[2], cw)] = r2hi[:, :cw]
-    part = part + lane_sum(r2lo, cw)
-    pay[:, 4 * cw :] = scalar_lanes(part, rx)
+    pay[0:low, :cw] = r2lo[:, :cw]
+    pay[low:, :cw] = r2hi[:, :cw]
+    pay[:, cw:] = scalar_lanes(part, rx)
 
 
 def row_starts(rx):
@@ -195,17 +198,28 @@
     return [jnp.sum(fold(v), 0, keepdims=True), jnp.sum(fold(v * n.astype(f32)), 0, keepdims=True)]
 
 
-def first_product_kernel(own, r1, r3, n, my, send, acc, gram):
-    rx, images = own.shape[0], gram.shape[1]
-    width = my.shape[1]
+def times(gram, n, cols):
+    cw = gram.shape[1] // 4
+    total = None
+    for i, k in enumerate((0, 3, 1, 2)):
+        at = pl.multiple_of(lax.rem(lax.axis_index("zh") + k, 4) * cw, cw)
+        v = jnp.dot(gram[:, i * cw : i * cw + cw], n[pl.ds(at, cw), cols], preferred_element_type=f32)
+        total = v if total is None else total + v
+    return total
+
+
+def first_product_kernel(own, r1, r3, own4, r14, r34, n, my, send, acc, gram):
+    rx, three = own.shape
+    width, cw = my.shape[1], three // 3
     starts = row_starts(rx)
     part = jnp.zeros((1, 1), f32)
-    for i, r in enumerate((own, r1, r3)):
-        gram[i * rx : i * rx + rx, :] = r[:, :images]
-        part = part + lane_sum(r, images)
+    for i, (r, r4) in enumerate(((own, own4), (r1, r14), (r3, r34))):
+        gram[i * rx : i * rx + rx, :three] = r[...]
+        gram[i * rx : i * rx + rx, three:] = r4[:, :cw]
+        part = part + lane_sum(r4, cw)
     zero = jnp.zeros((1, width), f32)
     for out, cols in ((send, slice(width, 2 * width)), (my, slice(0, width))):
-        out[...] = jnp.dot(gram[...], n[:, cols], preferred_element_type=f32)
+        out[...] = times(gram, n, cols)
         got = [zero, zero]
         for i, k in enumerate((0, 3, 1)):
             more = column_sums(out[i * rx : i * rx + rx, :], n[pl.ds(starts[k], rx), cols])
@@ -213,22 +227,25 @@
         acc[:, cols] = jnp.concatenate(got + [zero + part] + [zero] * 5, 0)
 
 
-def last_product_kernel(r2lo, r2hi, n, acc, my, send, sums, gram):
-    (low, rx), images = (r2lo.shape[0], gram.shape[0]), gram.shape[1]
-    width = my.shape[1]
+def last_product_kernel(r2lo, r2hi, r24lo, r24hi, n, acc, my, send, sums, gram):
+    low, three = r2lo.shape
+    rx, width, cw = gram.shape[0], my.shape[1], three // 3
     at = row_starts(rx)[2]
-    gram[0:low, :] = r2lo[:, :images]
-    gram[low:, :] = r2hi[:, :images]
-    part = lane_sum(r2lo, images)
+    gram[0:low, :three] = r2lo[...]
+    gram[low:, :three] = r2hi[...]
+    gram[0:low, three:] = r24lo[:, :cw]
+    gram[low:, three:] = r24hi[:, :cw]
+    part = lane_sum(r24lo, cw)
     zero = jnp.zeros((1, width), f32)
     got = []
     for out, cols in ((send, slice(width, 2 * width)), (my, slice(0, width))):
-        v = jnp.dot(gram[...], n[:, cols], preferred_element_type=f32)
+        v = times(gram, n, cols)
         out[...] = v
         more = column_sums(v, n[pl.ds(at, rx), cols])
         got.append(acc[:, cols] + jnp.concatenate(more + [zero + part] + [zero] * 5, 0))
-    to_even = jnp.where(lax.axis_index("core") == 0, got[1], got[0])
-    to_odd = jnp.where(lax.axis_index("core") == 0, got[0], got[1])
+    even = lax.axis_index("core") == 0
+    to_even = jnp.where(even, got[1], got[0])
+    to_odd = jnp.where(even, got[0], got[1])
     for i in range(0, sums.shape[0], 2):
         sums[i] = to_even
         sums[i + 1] = to_odd
@@ -346,13 +363,17 @@
     (mine,) = call(sum_z_kernel, [shard], q0, *got)
     theirs = from_pair(mine, "core")
     (pay,) = call(functools.partial(load_kernel, images), [like((rx, cw + 128), bf16)], mine, theirs, diag)
-    (pay,) = call(join_kernel, [like((rx, images + 128), bf16)], pay, *ring(pay, "zh"))
-    r1, r3, r2lo, r2hi = ring(pay, "x")
+    z1, z3 = from_axis(pay, "zh", 3), from_axis(pay, "zh", 1)
+    z2 = from_axis(z1[:low], "zh", 3), from_axis(z3[low:], "zh", 1)
+    (early,) = call(first_join_kernel, [like((rx, 3 * cw), bf16)], pay, z1, z3)
+    r1, r3, r2lo, r2hi = ring(early, "x")
+    (late,) = call(last_join_kernel, [like((rx, cw + 128), bf16)], pay, z1, z3, *z2)
+    r14, r34, r24lo, r24hi = ring(late, "x")
     wide, three, quarter = like((rows, width), f32), like((3 * rx, width), f32), like((rx, width), f32)
     my3, send3, acc = call(
         first_product_kernel,
         [three, three, like((8, full), f32)],
-        *(pay, r1, r3, n),
+        *(early, r1, r3, late, r14, r34, n),
         scratch=[pltpu.VMEM((3 * rx, images), bf16)],
         limit=8,
     )
@@ -360,7 +381,7 @@
     my1, send1, sums = call(
         last_product_kernel,
         [quarter, quarter, like((16, 8, width), f32)],
-        *(r2lo, r2hi, n, acc),
+        *(r2lo, r2hi, r24lo, r24hi, n, acc),
         scratch=[pltpu.VMEM((rx, images), bf16)],
     )
     other1 = from_pair(send1, "core")

time: 142 us -> 140 us (0.986)
  waiting for transfers between devices: 66.7 us -> 61.2 us
  starting transfers between devices: 56.6 us -> 59.8 us
    ppermute x21 -> x25, waiting for transfers between devices: 47.6 us -> 42.2 us  [from_axis(): return lax.ppermute(v, axis, [((i + k) % 4, i) for i in range(4)])]
    ppermute x21 -> x25, starting transfers between devices: 35.4 us -> 39.8 us  [from_axis(): return lax.ppermute(v, axis, [((i + k) % 4, i) for i in range(4)])]
    all_to_all x1, starting transfers between devices: 6.01 us -> 3.69 us  [per_device(): lax.all_to_all(sums, batch + ('core',), split_axis=0, concat_axis=0, tile...]
    pallas_call x12 -> x13, Pallas kernels: 15.6 us -> 15.9 us  [call(): pl.pallas_call(kernel, out_shape=outs, in_specs=[pl.BlockSpec(memory_spac...]
  transfers between devices with their start and end apart: 31 -> 35, of which waited for: 19 -> 21; matrix products, arithmetic and copies ran while one was open for 0% -> 0% of each run, Pallas kernels for 6% -> 6%
where the time goes in v2:
time: 140 us; the launch traced here: 139 us
  waiting for transfers between devices  61.2 us (44%)
  starting transfers between devices  59.8 us (43%)
  Pallas kernels  15.9 us (11%)
    ppermute x25, waiting for transfers between devices, from_axis(): return lax.ppermute(v, axis, [((i + k) % 4, i) for i in range(4)])  42.2 us
    ppermute x25, starting transfers between devices, from_axis(): return lax.ppermute(v, axis, [((i + k) % 4, i) for i in range(4)])  39.8 us
    ppermute x9, starting transfers between devices, from_pair(): return lax.ppermute(v, axis, [(1, 0), (0, 1)])  16.3 us
    pallas_call x13, Pallas kernels, call(): pl.pallas_call(kernel, out_shape=outs, in_specs=[pl.BlockSpec(memory_spac...  15.9 us
    ppermute x9, waiting for transfers between devices, from_pair(): return lax.ppermute(v, axis, [(1, 0), (0, 1)])  13.2 us
    all_to_all x1, waiting for transfers between devices, per_device(): lax.all_to_all(sums, batch + ('core',), split_axis=0, concat_axis=0, tile...  5.81 us
    all_to_all x1, starting transfers between devices, per_device(): lax.all_to_all(sums, batch + ('core',), split_axis=0, concat_axis=0, tile...  3.69 us
  transfers between devices with their start and end apart: 35, of which 21 were waited for; matrix products, arithmetic and copies ran while one was open for 0% of the time, Pallas kernels for 6%

profile of v2, /device:TPU:1, one launch (start us, length us, event | category | flops | bytes accessed | tf_op | source)
XLA Modules:
  0.0 139.2 jit_solution(15896493204770415982)
XLA Ops:
  0.6 1.1 broadcast_select_fusion.1
  1.8 3.3 %collective-permute-start = (bf16[320,512]{1,0:T(8,128)(2,1)S(1)}, bf16[320,512]{1,0:T(8,128)(2,1)S(1)}, u32[]{:S(2)}, u32[]{:S(2)}) collective-permute-start(bf16[320,512]{1,0:T(8,128)(2,1)S(1)} %get-tuple-element.70), channel_id=1, source_target_pairs={{1,0},{0,1},{3,2},{2,3},{5,4},{4,5},{7,6},{6,7},{9,8},{8,9},{11,10... | collective-permute-start | bytes 983048 | tf_op jit(solution)/shard_map/ppermute | solution.py:26
  5.1 1.3 collective-permute-done
  6.4 0.1 collective-permute-start.3
  6.5 2.7 %collective-permute-start.2 = (bf16[320,1024]{1,0:T(8,128)(2,1)S(1)}, bf16[320,1024]{1,0:T(8,128)(2,1)S(1)}, u32[]{:S(2)}, u32[]{:S(2)}) collective-permute-start(bf16[320,1024]{1,0:T(8,128)(2,1)S(1)} %pad_maximum_fusion.own), channel_id=1, source_target_pairs={{64,0},{128,64},{192,128},{0,192},{65,1},{129,65},{193,129},{1,193... | collective-permute-start | bytes 1966088 | tf_op jit(solution)/shard_map/ppermute | solution.py:22
  9.2 14.4 %collective-permute-done.3.refs_2_ = bf16[320,1024]{1,0:T(8,128)(2,1)S(1)} collective-permute-done((bf16[320,1024]{1,0:T(8,128)(2,1)S(1)}, bf16[320,1024]{1,0:T(8,128)(2,1)S(1)}, u32[]{:S(2)}, u32[]{:S(2)}) %collective-permute-start.3) | collective-permute-done | bytes 655392 | tf_op jit(solution)/shard_map/ppermute | solution.py:22
  23.7 0.1 collective-permute-start.5
  23.8 2.7 %collective-permute-start.4 = (bf16[160,1024]{1,0:T(8,128)(2,1)S(1)}, bf16[160,1024]{1,0:T(8,128)(2,1)S(1)}, u32[]{:S(2)}, u32[]{:S(2)}) collective-permute-start(bf16[160,1024]{1,0:T(8,128)(2,1)S(1)} %slice.36), channel_id=1, source_target_pairs={{64,0},{128,64},{192,128},{0,192},{65,1},{129,65},{193,129},{1,193... | collective-permute-start | bytes 983048 | tf_op jit(solution)/shard_map/ppermute | solution.py:22
  26.6 2.7 %collective-permute-start.6 = (bf16[320,1024]{1,0:T(8,128)(2,1)S(1)}, bf16[320,1024]{1,0:T(8,128)(2,1)S(1)}, u32[]{:S(2)}, u32[]{:S(2)}) collective-permute-start(bf16[320,1024]{1,0:T(8,128)(2,1)S(1)} %collective-permute-done.1.refs_0_), channel_id=1, source_target_pairs={{64,0},{128,64},{192,128},{0,192},{65,1},{129,65},{193,129},{1,193... | collective-permute-start | bytes 1966088 | tf_op jit(solution)/shard_map/ppermute | solution.py:22
  29.2 3.7 %collective-permute-done.5.refs_4_ = bf16[160,1024]{1,0:T(8,128)(2,1)S(1)} collective-permute-done((bf16[160,1024]{1,0:T(8,128)(2,1)S(1)}, bf16[160,1024]{1,0:T(8,128)(2,1)S(1)}, u32[]{:S(2)}, u32[]{:S(2)}) %collective-permute-start.5) | collective-permute-done | bytes 327712 | tf_op jit(solution)/shard_map/ppermute | solution.py:22
  33.0 0.1 collective-permute-start.9
  33.1 1.4 collective-permute-start.8
  34.4 1.8 %shard_map.49 = (f32[24,1024]{1,0:T(8,128)S(1)}, bf16[1600,1024]{1,0:T(8,128)(2,1)S(1)}) custom-call(bf16[320,1024]{1,0:T(8,128)(2,1)S(1)} %pad_maximum_fusion.own, bf16[320,1024]{1,0:T(8,128)(2,1)S(1)} %collective-permute-done.1.refs_0_, bf16[320,1024]{1,0:T(8,128)(2,1)S(1)} %collective-permute-done.2.refs_1_, ...), custom_call_target="tpu_custom_call" | custom-call | tf_op jit(solution)/shard_map/pallas_call | solution.py:299
  36.3 2.9 %collective-permute-done.9.refs_3_ = bf16[160,1024]{1,0:T(8,128)(2,1)S(1)} collective-permute-done((bf16[160,1024]{1,0:T(8,128)(2,1)S(1)}, bf16[160,1024]{1,0:T(8,128)(2,1)S(1)}, u32[]{:S(2)}, u32[]{:S(2)}) %collective-permute-start.9) | collective-permute-done | bytes 327712 | tf_op jit(solution)/shard_map/ppermute | solution.py:26
  39.2 6.2 %collective-permute-done.8.refs_2_ = bf16[160,1024]{1,0:T(8,128)(2,1)S(1)} collective-permute-done((bf16[160,1024]{1,0:T(8,128)(2,1)S(1)}, bf16[160,1024]{1,0:T(8,128)(2,1)S(1)}, u32[]{:S(2)}, u32[]{:S(2)}) %collective-permute-start.8) | collective-permute-done | bytes 327712 | tf_op jit(solution)/shard_map/ppermute | solution.py:26
  45.4 1.7 %collective-permute-done.7.refs_1_ = bf16[320,1024]{1,0:T(8,128)(2,1)S(1)} collective-permute-done((bf16[320,1024]{1,0:T(8,128)(2,1)S(1)}, bf16[320,1024]{1,0:T(8,128)(2,1)S(1)}, u32[]{:S(2)}, u32[]{:S(2)}) %collective-permute-start.7) | collective-permute-done | bytes 655392 | tf_op jit(solution)/shard_map/ppermute | solution.py:22
  47.0 4.6 %shard_map.50 = (bf16[2560,1024]{1,0:T(8,128)(2,1)S(1)}, bf16[2560,512]{1,0:T(8,128)(2,1)S(1)}, f32[8,1024]{1,0:T(8,128)S(1)}, bf16[48,2560]{1,0:T(8,128)(2,1)S(1)}, bf16[32,2560]{1,0:T(8,128)(2,1)S(1)}) custom-call(f32[24,1024]{1,0:T(8,128)S(1)} %get-tuple-element.36.st, bf16[1600,1024]{1,0:T(8,128)(2,1)S(1)} %get-tuple-element.37.known, ...), custom_call_target="tpu_custom_call" | custom-call | tf_op jit(solution)/shard_map/pallas_call | solution.py:299
  51.6 0.1 collective-permute-start.10
  51.7 2.7 %collective-permute-start.11 = (bf16[32,2560]{1,0:T(8,128)(2,1)S(1)}, bf16[32,2560]{1,0:T(8,128)(2,1)S(1)}, u32[]{:S(2)}, u32[]{:S(2)}) collective-permute-start(bf16[32,2560]{1,0:T(8,128)(2,1)S(1)} %get-tuple-element.43), channel_id=1, source_target_pairs={{8,0},{16,8},{24,16},{0,24},{9,1},{17,9},{25,17},{1,25},{10,2},{18... | collective-permute-start | bytes 491528 | tf_op jit(solution)/shard_map/ppermute | solution.py:22
  54.4 2.4 %shard_map.51 = (bf16[80,2560]{1,0:T(8,128)(2,1)S(1)}, bf16[80,2560]{1,0:T(8,128)(2,1)S(1)}, bf16[80,2560]{1,0:T(8,128)(2,1)S(1)}) custom-call(bf16[2560,1024]{1,0:T(8,128)(2,1)S(1)} %get-tuple-element.38.n), custom_call_target="tpu_custom_call" | custom-call | tf_op jit(solution)/shard_map/pallas_call | solution.py:299
  56.8 1.2 collective-permute-done.10.a
  58.0 0.1 shard_map.52
  58.1 0.1 collective-permute-start.12
  58.2 2.7 %collective-permute-start.13 = (bf16[80,2560]{1,0:T(8,128)(2,1)S(1)}, bf16[80,2560]{1,0:T(8,128)(2,1)S(1)}, u32[]{:S(2)}, u32[]{:S(2)}) collective-permute-start(bf16[80,2560]{1,0:T(8,128)(2,1)S(1)} %get-tuple-element.45), channel_id=1, source_target_pairs={{8,0},{16,8},{24,16},{0,24},{9,1},{17,9},{25,17},{1,25},{10,2},{18... | collective-permute-start | bytes 1228808 | tf_op jit(solution)/shard_map/ppermute | solution.py:22
  60.8 5.3 %collective-permute-done.12.e = bf16[80,2560]{1,0:T(8,128)(2,1)S(1)} collective-permute-done((bf16[80,2560]{1,0:T(8,128)(2,1)S(1)}, bf16[80,2560]{1,0:T(8,128)(2,1)S(1)}, u32[]{:S(2)}, u32[]{:S(2)}) %collective-permute-start.12) | collective-permute-done | bytes 409632 | tf_op jit(solution)/shard_map/ppermute | solution.py:22
  66.2 0.2 shard_map.53
  66.4 5.5 %collective-permute-start.14 = (bf16[2560,512]{1,0:T(8,128)(2,1)S(1)}, bf16[2560,512]{1,0:T(8,128)(2,1)S(1)}, u32[]{:S(2)}, u32[]{:S(2)}) collective-permute-start(bf16[2560,512]{1,0:T(8,128)(2,1)S(1)} %get-tuple-element.50), channel_id=1, source_target_pairs={{1,0},{0,1},{3,2},{2,3},{5,4},{4,5},{7,6},{6,7},{9,8},{8,9},{11,10... | collective-permute-start | bytes 7864328 | tf_op jit(solution)/shard_map/ppermute | solution.py:26
  71.9 1.8 %collective-permute-start.17 = (bf16[80,640]{1,0:T(8,128)(2,1)S(1)}, bf16[80,640]{1,0:T(8,128)(2,1)S(1)}, u32[]{:S(2)}, u32[]{:S(2)}) collective-permute-start(bf16[80,640]{1,0:T(8,128)(2,1)S(1)} %get-tuple-element.55), channel_id=1, source_target_pairs={{6,0},{0,2},{2,4},{4,6},{7,1},{1,3},{3,5},{5,7},{14,8},{8,10},{10,... | collective-permute-start | bytes 307208 | tf_op jit(solution)/shard_map/ppermute | solution.py:22
  73.7 4.8 %collective-permute-start.16 = (bf16[80,640]{1,0:T(8,128)(2,1)S(1)}, bf16[80,640]{1,0:T(8,128)(2,1)S(1)}, u32[]{:S(2)}, u32[]{:S(2)}) collective-permute-start(bf16[80,640]{1,0:T(8,128)(2,1)S(1)} %get-tuple-element.54), channel_id=1, source_target_pairs={{4,0},{6,2},{0,4},{2,6},{5,1},{7,3},{1,5},{3,7},{12,8},{14,10},{8,... | collective-permute-start | bytes 307208 | tf_op jit(solution)/shard_map/ppermute | solution.py:22
  78.5 2.4 %collective-permute-start.18 = (bf16[80,640]{1,0:T(8,128)(2,1)S(1)}, bf16[80,640]{1,0:T(8,128)(2,1)S(1)}, u32[]{:S(2)}, u32[]{:S(2)}) collective-permute-start(bf16[80,640]{1,0:T(8,128)(2,1)S(1)} %get-tuple-element.56), channel_id=1, source_target_pairs={{2,0},{4,2},{6,4},{0,6},{3,1},{5,3},{7,5},{1,7},{10,8},{12,10},{14... | collective-permute-start | bytes 307208 | tf_op jit(solution)/shard_map/ppermute | solution.py:22
  80.9 0.9 collective-permute-start.15
  81.8 0.8 collective-permute-done.15.inv_o
  82.6 1.1 shard_map.54
  83.7 2.1 %collective-permute-done.16.r1 = bf16[80,640]{1,0:T(8,128)(2,1)S(1)} collective-permute-done((bf16[80,640]{1,0:T(8,128)(2,1)S(1)}, bf16[80,640]{1,0:T(8,128)(2,1)S(1)}, u32[]{:S(2)}, u32[]{:S(2)}) %collective-permute-start.16) | collective-permute-done | bytes 102432 | tf_op jit(solution)/shard_map/ppermute | solution.py:22
  85.9 3.0 %collective-permute-done.18.r3 = bf16[80,640]{1,0:T(8,128)(2,1)S(1)} collective-permute-done((bf16[80,640]{1,0:T(8,128)(2,1)S(1)}, bf16[80,640]{1,0:T(8,128)(2,1)S(1)}, u32[]{:S(2)}, u32[]{:S(2)}) %collective-permute-start.18) | collective-permute-done | bytes 102432 | tf_op jit(solution)/shard_map/ppermute | solution.py:22
  88.9 0.6 collective-permute-start.19
  89.5 0.9 collective-permute-done.19.theirs
  90.4 0.1 shard_map.56.own
  90.6 3.4 %collective-permute-start.21 = (bf16[80,768]{1,0:T(8,128)(2,1)S(1)}, bf16[80,768]{1,0:T(8,128)(2,1)S(1)}, u32[]{:S(2)}, u32[]{:S(2)}) collective-permute-start(bf16[80,768]{1,0:T(8,128)(2,1)S(1)} %shard_map.56.own), channel_id=1, source_target_pairs={{2,0},{4,2},{6,4},{0,6},{3,1},{5,3},{7,5},{1,7},{10,8},{12,10},{14... | collective-permute-start | bytes 368648 | tf_op jit(solution)/shard_map/ppermute | solution.py:22
  94.0 4.7 %collective-permute-done.21.r3 = bf16[80,768]{1,0:T(8,128)(2,1)S(1)} collective-permute-done((bf16[80,768]{1,0:T(8,128)(2,1)S(1)}, bf16[80,768]{1,0:T(8,128)(2,1)S(1)}, u32[]{:S(2)}, u32[]{:S(2)}) %collective-permute-start.21) | collective-permute-done | bytes 122912 | tf_op jit(solution)/shard_map/ppermute | solution.py:22
  98.6 2.6 %collective-permute-done.20.r1 = bf16[80,768]{1,0:T(8,128)(2,1)S(1)} collective-permute-done((bf16[80,768]{1,0:T(8,128)(2,1)S(1)}, bf16[80,768]{1,0:T(8,128)(2,1)S(1)}, u32[]{:S(2)}, u32[]{:S(2)}) %collective-permute-start.20) | collective-permute-done | bytes 122912 | tf_op jit(solution)/shard_map/ppermute | solution.py:22
  101.2 1.2 collective-permute-start.22
  102.4 1.9 %collective-permute-start.23 = (bf16[80,1920]{1,0:T(8,128)(2,1)S(1)}, bf16[80,1920]{1,0:T(8,128)(2,1)S(1)}, u32[]{:S(2)}, u32[]{:S(2)}) collective-permute-start(bf16[80,1920]{1,0:T(8,128)(2,1)S(1)} %shard_map.57.own), channel_id=1, source_target_pairs={{8,0},{16,8},{24,16},{0,24},{9,1},{17,9},{25,17},{1,25},{10,2},{18... | collective-permute-start | bytes 921608 | tf_op jit(solution)/shard_map/ppermute | solution.py:22
  104.4 0.8 collective-permute-start.24
  105.2 2.7 %collective-permute-start.25 = (bf16[32,768]{1,0:T(8,128)(2,1)S(1)}, bf16[32,768]{1,0:T(8,128)(2,1)S(1)}, u32[]{:S(2)}, u32[]{:S(2)}) collective-permute-start(bf16[32,768]{1,0:T(8,128)(2,1)S(1)} %slice.39), channel_id=1, source_target_pairs={{2,0},{4,2},{6,4},{0,6},{3,1},{5,3},{7,5},{1,7},{10,8},{12,10},{14... | collective-permute-start | bytes 147464 | tf_op jit(solution)/shard_map/ppermute | solution.py:22
  107.9 1.9 %collective-permute-done.25.r2hi = bf16[32,768]{1,0:T(8,128)(2,1)S(1)} collective-permute-done((bf16[32,768]{1,0:T(8,128)(2,1)S(1)}, bf16[32,768]{1,0:T(8,128)(2,1)S(1)}, u32[]{:S(2)}, u32[]{:S(2)}) %collective-permute-start.25) | collective-permute-done | bytes 49184 | tf_op jit(solution)/shard_map/ppermute | solution.py:22
  109.9 0.4 collective-permute-done.24.r2lo
  110.2 0.1 shard_map.58.own4
  110.3 0.1 collective-permute-start.26
  110.4 0.4 collective-permute-done.22.r1
  110.9 0.5 collective-permute-start.28
  111.3 2.3 %collective-permute-start.27 = (bf16[80,768]{1,0:T(8,128)(2,1)S(1)}, bf16[80,768]{1,0:T(8,128)(2,1)S(1)}, u32[]{:S(2)}, u32[]{:S(2)}) collective-permute-start(bf16[80,768]{1,0:T(8,128)(2,1)S(1)} %shard_map.58.own4), channel_id=1, source_target_pairs={{8,0},{16,8},{24,16},{0,24},{9,1},{17,9},{25,17},{1,25},{10,2},{18... | collective-permute-start | bytes 368648 | tf_op jit(solution)/shard_map/ppermute | solution.py:22
  113.6 1.1 collective-permute-start.29
  114.7 0.6 collective-permute-done.26.r14
  115.4 0.1 collective-permute-done.27.r34
  115.5 3.1 %collective-permute-start.31 = (bf16[32,768]{1,0:T(8,128)(2,1)S(1)}, bf16[32,768]{1,0:T(8,128)(2,1)S(1)}, u32[]{:S(2)}, u32[]{:S(2)}) collective-permute-start(bf16[32,768]{1,0:T(8,128)(2,1)S(1)} %slice.43), channel_id=1, source_target_pairs={{8,0},{16,8},{24,16},{0,24},{9,1},{17,9},{25,17},{1,25},{10,2},{18... | collective-permute-start | bytes 147464 | tf_op jit(solution)/shard_map/ppermute | solution.py:22
  118.6 1.8 %shard_map.59 = (f32[240,512]{1,0:T(8,128)S(1)}, f32[240,512]{1,0:T(8,128)S(1)}, f32[8,1024]{1,0:T(8,128)S(1)}) custom-call(bf16[80,1920]{1,0:T(8,128)(2,1)S(1)} %shard_map.57.own, bf16[80,1920]{1,0:T(8,128)(2,1)S(1)} %collective-permute-done.22.r1, bf16[80,1920]{1,0:T(8,128)(2,1)S(1)} %collective-permute-done.23.r3, bf16[80,768]{1,0:T(8,128)(2,1)S(1)} %shard_map.58.own4, ...), custom_call_target="tpu_custom_call" | custom-call | tf_op jit(solution)/shard_map/pallas_call | solution.py:299
  120.3 4.2 %collective-permute-start.32 = (f32[240,512]{1,0:T(8,128)S(1)}, f32[240,512]{1,0:T(8,128)S(1)}, u32[]{:S(2)}, u32[]{:S(2)}) collective-permute-start(f32[240,512]{1,0:T(8,128)S(1)} %get-tuple-element.60), channel_id=1, source_target_pairs={{1,0},{0,1},{3,2},{2,3},{5,4},{4,5},{7,6},{6,7},{9,8},{8,9},{11,10... | collective-permute-start | bytes 1474568 | tf_op jit(solution)/shard_map/ppermute | solution.py:26
  124.5 1.8 %shard_map.60 = (f32[80,512]{1,0:T(8,128)S(1)}, f32[80,512]{1,0:T(8,128)S(1)}, f32[16,8,512]{2,1,0:T(8,128)}) custom-call(bf16[48,1920]{1,0:T(8,128)(2,1)S(1)} %collective-permute-done.28.r2lo, bf16[32,1920]{1,0:T(8,128)(2,1)S(1)} %collective-permute-done.29.r2hi, bf16[48,768]{1,0:T(8,128)(2,1)S(1)} %collective-permute-done.30.r24lo, ...), custom_call_target="tpu_custom_call" | custom-call | tf_op jit(solution)/shard_map/pallas_call | solution.py:299
  126.4 3.7 %all-to-all-start = ((f32[16,8,512]{2,1,0:T(8,128)}), f32[16,8,512]{2,1,0:T(8,128)S(1)}, u32[]{:S(2)}, u32[]{:S(2)}) async-start(f32[16,8,512]{2,1,0:T(8,128)} %get-tuple-element.64), calls=%async_computation | async-start | bytes 524288 | tf_op jit(solution)/shard_map/all_to_all | solution.py:388
  130.1 0.3 collective-permute-start.33
  130.4 1.1 collective-permute-done.33.other1
  131.5 5.8 %all-to-all-done.sums = f32[16,8,512]{2,1,0:T(8,128)S(1)} async-done(((f32[16,8,512]{2,1,0:T(8,128)}), f32[16,8,512]{2,1,0:T(8,128)S(1)}, u32[]{:S(2)}, u32[]{:S(2)}) %all-to-all-start) | async-done | bytes 262176 | tf_op jit(solution)/shard_map/all_to_all | solution.py:388
  137.3 1.7 %shard_map.61 = (f32[1,1]{1,0:T(1,128)}, f32[320,512]{1,0:T(8,128)}, f32[320,512]{1,0:T(8,128)}) custom-call(f32[240,512]{1,0:T(8,128)S(1)} %get-tuple-element.57.my3, f32[80,512]{1,0:T(8,128)S(1)} %get-tuple-element.59.my1, f32[240,512]{1,0:T(8,128)S(1)} %collective-permute-done.32.other3, f32[80,512]{1,0:T(8,128)S(1)} %collective-permute-done.33.other1, ...), custom_call_target="tpu_custom_call" | custom-call | tf_op jit(solution)/shard_map/pallas_call | solution.py:299
  (30 shorter events, 0.3 us)
Async XLA Ops:
  1.8 4.6 %collective-permute-start = (bf16[320,512]{1,0:T(8,128)(2,1)S(1)}, bf16[320,512]{1,0:T(8,128)(2,1)S(1)}, u32[]{:S(2)}, u32[]{:S(2)}) collective-permute-start(bf16[320,512]{1,0:T(8,128)(2,1)S(1)} %get-tuple-element.70), channel_id=1, source_target_pairs={{1,0},{0,1},{3,2},{2,3},{5,4},{4,5},{7,6},{6,7},{9,8},{8,9},{11,10... | collective-permute-start | bytes 983048 | tf_op jit(solution)/shard_map/ppermute | solution.py:26
  6.4 17.2 %collective-permute-start.3 = (bf16[320,1024]{1,0:T(8,128)(2,1)S(1)}, bf16[320,1024]{1,0:T(8,128)(2,1)S(1)}, u32[]{:S(2)}, u32[]{:S(2)}) collective-permute-start(bf16[320,1024]{1,0:T(8,128)(2,1)S(1)} %pad_maximum_fusion.own), channel_id=1, source_target_pairs={{192,0},{0,64},{64,128},{128,192},{193,1},{1,65},{65,129},{129,193... | collective-permute-start | bytes 1966088 | tf_op jit(solution)/shard_map/ppermute | solution.py:22
  6.5 17.3 %collective-permute-start.2 = (bf16[320,1024]{1,0:T(8,128)(2,1)S(1)}, bf16[320,1024]{1,0:T(8,128)(2,1)S(1)}, u32[]{:S(2)}, u32[]{:S(2)}) collective-permute-start(bf16[320,1024]{1,0:T(8,128)(2,1)S(1)} %pad_maximum_fusion.own), channel_id=1, source_target_pairs={{64,0},{128,64},{192,128},{0,192},{65,1},{129,65},{193,129},{1,193... | collective-permute-start | bytes 1966088 | tf_op jit(solution)/shard_map/ppermute | solution.py:22
  9.2 17.4 %collective-permute-start.1 = (bf16[320,1024]{1,0:T(8,128)(2,1)S(1)}, bf16[320,1024]{1,0:T(8,128)(2,1)S(1)}, u32[]{:S(2)}, u32[]{:S(2)}) collective-permute-start(bf16[320,1024]{1,0:T(8,128)(2,1)S(1)} %pad_maximum_fusion.own), channel_id=1, source_target_pairs={{32,0},{0,32},{33,1},{1,33},{34,2},{2,34},{35,3},{3,35},{36,4},{4,... | collective-permute-start | bytes 1966088 | tf_op jit(solution)/shard_map/ppermute | solution.py:26
  23.7 9.3 %collective-permute-start.5 = (bf16[160,1024]{1,0:T(8,128)(2,1)S(1)}, bf16[160,1024]{1,0:T(8,128)(2,1)S(1)}, u32[]{:S(2)}, u32[]{:S(2)}) collective-permute-start(bf16[160,1024]{1,0:T(8,128)(2,1)S(1)} %slice.37), channel_id=1, source_target_pairs={{192,0},{0,64},{64,128},{128,192},{193,1},{1,65},{65,129},{129,193... | collective-permute-start | bytes 983048 | tf_op jit(solution)/shard_map/ppermute | solution.py:22
  23.8 9.3 %collective-permute-start.4 = (bf16[160,1024]{1,0:T(8,128)(2,1)S(1)}, bf16[160,1024]{1,0:T(8,128)(2,1)S(1)}, u32[]{:S(2)}, u32[]{:S(2)}) collective-permute-start(bf16[160,1024]{1,0:T(8,128)(2,1)S(1)} %slice.36), channel_id=1, source_target_pairs={{64,0},{128,64},{192,128},{0,192},{65,1},{129,65},{193,129},{1,193... | collective-permute-start | bytes 983048 | tf_op jit(solution)/shard_map/ppermute | solution.py:22
  26.5 20.5 %collective-permute-start.7 = (bf16[320,1024]{1,0:T(8,128)(2,1)S(1)}, bf16[320,1024]{1,0:T(8,128)(2,1)S(1)}, u32[]{:S(2)}, u32[]{:S(2)}) collective-permute-start(bf16[320,1024]{1,0:T(8,128)(2,1)S(1)} %collective-permute-done.1.refs_0_), channel_id=1, source_target_pairs={{192,0},{0,64},{64,128},{128,192},{193,1},{1,65},{65,129},{129,193... | collective-permute-start | bytes 1966088 | tf_op jit(solution)/shard_map/ppermute | solution.py:22
  26.6 20.5 %collective-permute-start.6 = (bf16[320,1024]{1,0:T(8,128)(2,1)S(1)}, bf16[320,1024]{1,0:T(8,128)(2,1)S(1)}, u32[]{:S(2)}, u32[]{:S(2)}) collective-permute-start(bf16[320,1024]{1,0:T(8,128)(2,1)S(1)} %collective-permute-done.1.refs_0_), channel_id=1, source_target_pairs={{64,0},{128,64},{192,128},{0,192},{65,1},{129,65},{193,129},{1,193... | collective-permute-start | bytes 1966088 | tf_op jit(solution)/shard_map/ppermute | solution.py:22
  33.0 6.2 %collective-permute-start.9 = (bf16[160,1024]{1,0:T(8,128)(2,1)S(1)}, bf16[160,1024]{1,0:T(8,128)(2,1)S(1)}, u32[]{:S(2)}, u32[]{:S(2)}) collective-permute-start(bf16[160,1024]{1,0:T(8,128)(2,1)S(1)} %collective-permute-done.5.refs_4_), channel_id=1, source_target_pairs={{32,0},{0,32},{33,1},{1,33},{34,2},{2,34},{35,3},{3,35},{36,4},{4,... | collective-permute-start | bytes 983048 | tf_op jit(solution)/shard_map/ppermute | solution.py:26
  33.1 12.3 %collective-permute-start.8 = (bf16[160,1024]{1,0:T(8,128)(2,1)S(1)}, bf16[160,1024]{1,0:T(8,128)(2,1)S(1)}, u32[]{:S(2)}, u32[]{:S(2)}) collective-permute-start(bf16[160,1024]{1,0:T(8,128)(2,1)S(1)} %collective-permute-done.4.refs_3_), channel_id=1, source_target_pairs={{32,0},{0,32},{33,1},{1,33},{34,2},{2,34},{35,3},{3,35},{36,4},{4,... | collective-permute-start | bytes 983048 | tf_op jit(solution)/shard_map/ppermute | solution.py:26
  51.6 6.3 %collective-permute-start.10 = (bf16[48,2560]{1,0:T(8,128)(2,1)S(1)}, bf16[48,2560]{1,0:T(8,128)(2,1)S(1)}, u32[]{:S(2)}, u32[]{:S(2)}) collective-permute-start(bf16[48,2560]{1,0:T(8,128)(2,1)S(1)} %get-tuple-element.41), channel_id=1, source_target_pairs={{24,0},{0,8},{8,16},{16,24},{25,1},{1,9},{9,17},{17,25},{26,2},{2,... | collective-permute-start | bytes 737288 | tf_op jit(solution)/shard_map/ppermute | solution.py:22
  51.7 5.0 %collective-permute-start.11 = (bf16[32,2560]{1,0:T(8,128)(2,1)S(1)}, bf16[32,2560]{1,0:T(8,128)(2,1)S(1)}, u32[]{:S(2)}, u32[]{:S(2)}) collective-permute-start(bf16[32,2560]{1,0:T(8,128)(2,1)S(1)} %get-tuple-element.43), channel_id=1, source_target_pairs={{8,0},{16,8},{24,16},{0,24},{9,1},{17,9},{25,17},{1,25},{10,2},{18... | collective-permute-start | bytes 491528 | tf_op jit(solution)/shard_map/ppermute | solution.py:22
  58.1 8.1 %collective-permute-start.12 = (bf16[80,2560]{1,0:T(8,128)(2,1)S(1)}, bf16[80,2560]{1,0:T(8,128)(2,1)S(1)}, u32[]{:S(2)}, u32[]{:S(2)}) collective-permute-start(bf16[80,2560]{1,0:T(8,128)(2,1)S(1)} %get-tuple-element.44), channel_id=1, source_target_pairs={{24,0},{0,8},{8,16},{16,24},{25,1},{1,9},{9,17},{17,25},{26,2},{2,... | collective-permute-start | bytes 1228808 | tf_op jit(solution)/shard_map/ppermute | solution.py:22
  58.2 8.0 %collective-permute-start.13 = (bf16[80,2560]{1,0:T(8,128)(2,1)S(1)}, bf16[80,2560]{1,0:T(8,128)(2,1)S(1)}, u32[]{:S(2)}, u32[]{:S(2)}) collective-permute-start(bf16[80,2560]{1,0:T(8,128)(2,1)S(1)} %get-tuple-element.45), channel_id=1, source_target_pairs={{8,0},{16,8},{24,16},{0,24},{9,1},{17,9},{25,17},{1,25},{10,2},{18... | collective-permute-start | bytes 1228808 | tf_op jit(solution)/shard_map/ppermute | solution.py:22
  66.4 16.2 %collective-permute-start.14 = (bf16[2560,512]{1,0:T(8,128)(2,1)S(1)}, bf16[2560,512]{1,0:T(8,128)(2,1)S(1)}, u32[]{:S(2)}, u32[]{:S(2)}) collective-permute-start(bf16[2560,512]{1,0:T(8,128)(2,1)S(1)} %get-tuple-element.50), channel_id=1, source_target_pairs={{1,0},{0,1},{3,2},{2,3},{5,4},{4,5},{7,6},{6,7},{9,8},{8,9},{11,10... | collective-permute-start | bytes 7864328 | tf_op jit(solution)/shard_map/ppermute | solution.py:26
  71.9 11.8 %collective-permute-start.17 = (bf16[80,640]{1,0:T(8,128)(2,1)S(1)}, bf16[80,640]{1,0:T(8,128)(2,1)S(1)}, u32[]{:S(2)}, u32[]{:S(2)}) collective-permute-start(bf16[80,640]{1,0:T(8,128)(2,1)S(1)} %get-tuple-element.55), channel_id=1, source_target_pairs={{6,0},{0,2},{2,4},{4,6},{7,1},{1,3},{3,5},{5,7},{14,8},{8,10},{10,... | collective-permute-start | bytes 307208 | tf_op jit(solution)/shard_map/ppermute | solution.py:22
  73.7 12.2 %collective-permute-start.16 = (bf16[80,640]{1,0:T(8,128)(2,1)S(1)}, bf16[80,640]{1,0:T(8,128)(2,1)S(1)}, u32[]{:S(2)}, u32[]{:S(2)}) collective-permute-start(bf16[80,640]{1,0:T(8,128)(2,1)S(1)} %get-tuple-element.54), channel_id=1, source_target_pairs={{4,0},{6,2},{0,4},{2,6},{5,1},{7,3},{1,5},{3,7},{12,8},{14,10},{8,... | collective-permute-start | bytes 307208 | tf_op jit(solution)/shard_map/ppermute | solution.py:22
  78.5 10.4 %collective-permute-start.18 = (bf16[80,640]{1,0:T(8,128)(2,1)S(1)}, bf16[80,640]{1,0:T(8,128)(2,1)S(1)}, u32[]{:S(2)}, u32[]{:S(2)}) collective-permute-start(bf16[80,640]{1,0:T(8,128)(2,1)S(1)} %get-tuple-element.56), channel_id=1, source_target_pairs={{2,0},{4,2},{6,4},{0,6},{3,1},{5,3},{7,5},{1,7},{10,8},{12,10},{14... | collective-permute-start | bytes 307208 | tf_op jit(solution)/shard_map/ppermute | solution.py:22
  80.9 1.8 %collective-permute-start.15 = (f32[8,512]{1,0:T(8,128)S(1)}, f32[8,512]{1,0:T(8,128)S(1)}, u32[]{:S(2)}, u32[]{:S(2)}) collective-permute-start(f32[8,512]{1,0:T(8,128)S(1)} %slice.29), channel_id=1, source_target_pairs={{1,0},{0,1},{3,2},{2,3},{5,4},{4,5},{7,6},{6,7},{9,8},{8,9},{11,10... | collective-permute-start | bytes 49160 | tf_op jit(solution)/shard_map/ppermute | solution.py:26
  88.9 1.5 %collective-permute-start.19 = (bf16[80,640]{1,0:T(8,128)(2,1)S(1)}, bf16[80,640]{1,0:T(8,128)(2,1)S(1)}, u32[]{:S(2)}, u32[]{:S(2)}) collective-permute-start(bf16[80,640]{1,0:T(8,128)(2,1)S(1)} %shard_map.55.mine), channel_id=1, source_target_pairs={{1,0},{0,1},{3,2},{2,3},{5,4},{4,5},{7,6},{6,7},{9,8},{8,9},{11,10... | collective-permute-start | bytes 307208 | tf_op jit(solution)/shard_map/ppermute | solution.py:26
  90.6 8.1 %collective-permute-start.21 = (bf16[80,768]{1,0:T(8,128)(2,1)S(1)}, bf16[80,768]{1,0:T(8,128)(2,1)S(1)}, u32[]{:S(2)}, u32[]{:S(2)}) collective-permute-start(bf16[80,768]{1,0:T(8,128)(2,1)S(1)} %shard_map.56.own), channel_id=1, source_target_pairs={{2,0},{4,2},{6,4},{0,6},{3,1},{5,3},{7,5},{1,7},{10,8},{12,10},{14... | collective-permute-start | bytes 368648 | tf_op jit(solution)/shard_map/ppermute | solution.py:22
  93.9 7.3 %collective-permute-start.20 = (bf16[80,768]{1,0:T(8,128)(2,1)S(1)}, bf16[80,768]{1,0:T(8,128)(2,1)S(1)}, u32[]{:S(2)}, u32[]{:S(2)}) collective-permute-start(bf16[80,768]{1,0:T(8,128)(2,1)S(1)} %shard_map.56.own), channel_id=1, source_target_pairs={{6,0},{0,2},{2,4},{4,6},{7,1},{1,3},{3,5},{5,7},{14,8},{8,10},{10,... | collective-permute-start | bytes 368648 | tf_op jit(solution)/shard_map/ppermute | solution.py:22
  101.2 9.6 %collective-permute-start.22 = (bf16[80,1920]{1,0:T(8,128)(2,1)S(1)}, bf16[80,1920]{1,0:T(8,128)(2,1)S(1)}, u32[]{:S(2)}, u32[]{:S(2)}) collective-permute-start(bf16[80,1920]{1,0:T(8,128)(2,1)S(1)} %shard_map.57.own), channel_id=1, source_target_pairs={{24,0},{0,8},{8,16},{16,24},{25,1},{1,9},{9,17},{17,25},{26,2},{2,... | collective-permute-start | bytes 921608 | tf_op jit(solution)/shard_map/ppermute | solution.py:22
  102.4 11.2 %collective-permute-start.23 = (bf16[80,1920]{1,0:T(8,128)(2,1)S(1)}, bf16[80,1920]{1,0:T(8,128)(2,1)S(1)}, u32[]{:S(2)}, u32[]{:S(2)}) collective-permute-start(bf16[80,1920]{1,0:T(8,128)(2,1)S(1)} %shard_map.57.own), channel_id=1, source_target_pairs={{8,0},{16,8},{24,16},{0,24},{9,1},{17,9},{25,17},{1,25},{10,2},{18... | collective-permute-start | bytes 921608 | tf_op jit(solution)/shard_map/ppermute | solution.py:22
  104.4 5.9 %collective-permute-start.24 = (bf16[48,768]{1,0:T(8,128)(2,1)S(1)}, bf16[48,768]{1,0:T(8,128)(2,1)S(1)}, u32[]{:S(2)}, u32[]{:S(2)}) collective-permute-start(bf16[48,768]{1,0:T(8,128)(2,1)S(1)} %slice.38), channel_id=1, source_target_pairs={{6,0},{0,2},{2,4},{4,6},{7,1},{1,3},{3,5},{5,7},{14,8},{8,10},{10,... | collective-permute-start | bytes 221192 | tf_op jit(solution)/shard_map/ppermute | solution.py:22
  105.2 4.7 %collective-permute-start.25 = (bf16[32,768]{1,0:T(8,128)(2,1)S(1)}, bf16[32,768]{1,0:T(8,128)(2,1)S(1)}, u32[]{:S(2)}, u32[]{:S(2)}) collective-permute-start(bf16[32,768]{1,0:T(8,128)(2,1)S(1)} %slice.39), channel_id=1, source_target_pairs={{2,0},{4,2},{6,4},{0,6},{3,1},{5,3},{7,5},{1,7},{10,8},{12,10},{14... | collective-permute-start | bytes 147464 | tf_op jit(solution)/shard_map/ppermute | solution.py:22
  110.3 5.0 %collective-permute-start.26 = (bf16[80,768]{1,0:T(8,128)(2,1)S(1)}, bf16[80,768]{1,0:T(8,128)(2,1)S(1)}, u32[]{:S(2)}, u32[]{:S(2)}) collective-permute-start(bf16[80,768]{1,0:T(8,128)(2,1)S(1)} %shard_map.58.own4), channel_id=1, source_target_pairs={{24,0},{0,8},{8,16},{16,24},{25,1},{1,9},{9,17},{17,25},{26,2},{2,... | collective-permute-start | bytes 368648 | tf_op jit(solution)/shard_map/ppermute | solution.py:22
  110.9 13.6 %collective-permute-start.28 = (bf16[48,1920]{1,0:T(8,128)(2,1)S(1)}, bf16[48,1920]{1,0:T(8,128)(2,1)S(1)}, u32[]{:S(2)}, u32[]{:S(2)}) collective-permute-start(bf16[48,1920]{1,0:T(8,128)(2,1)S(1)} %slice.40), channel_id=1, source_target_pairs={{24,0},{0,8},{8,16},{16,24},{25,1},{1,9},{9,17},{17,25},{26,2},{2,... | collective-permute-start | bytes 552968 | tf_op jit(solution)/shard_map/ppermute | solution.py:22
  111.3 4.1 %collective-permute-start.27 = (bf16[80,768]{1,0:T(8,128)(2,1)S(1)}, bf16[80,768]{1,0:T(8,128)(2,1)S(1)}, u32[]{:S(2)}, u32[]{:S(2)}) collective-permute-start(bf16[80,768]{1,0:T(8,128)(2,1)S(1)} %shard_map.58.own4), channel_id=1, source_target_pairs={{8,0},{16,8},{24,16},{0,24},{9,1},{17,9},{25,17},{1,25},{10,2},{18... | collective-permute-start | bytes 368648 | tf_op jit(solution)/shard_map/ppermute | solution.py:22
  113.6 10.9 %collective-permute-start.29 = (bf16[32,1920]{1,0:T(8,128)(2,1)S(1)}, bf16[32,1920]{1,0:T(8,128)(2,1)S(1)}, u32[]{:S(2)}, u32[]{:S(2)}) collective-permute-start(bf16[32,1920]{1,0:T(8,128)(2,1)S(1)} %slice.41), channel_id=1, source_target_pairs={{8,0},{16,8},{24,16},{0,24},{9,1},{17,9},{25,17},{1,25},{10,2},{18... | collective-permute-start | bytes 368648 | tf_op jit(solution)/shard_map/ppermute | solution.py:22
  115.3 9.2 %collective-permute-start.30 = (bf16[48,768]{1,0:T(8,128)(2,1)S(1)}, bf16[48,768]{1,0:T(8,128)(2,1)S(1)}, u32[]{:S(2)}, u32[]{:S(2)}) collective-permute-start(bf16[48,768]{1,0:T(8,128)(2,1)S(1)} %slice.42), channel_id=1, source_target_pairs={{24,0},{0,8},{8,16},{16,24},{25,1},{1,9},{9,17},{17,25},{26,2},{2,... | collective-permute-start | bytes 221192 | tf_op jit(solution)/shard_map/ppermute | solution.py:22
  115.5 9.0 %collective-permute-start.31 = (bf16[32,768]{1,0:T(8,128)(2,1)S(1)}, bf16[32,768]{1,0:T(8,128)(2,1)S(1)}, u32[]{:S(2)}, u32[]{:S(2)}) collective-permute-start(bf16[32,768]{1,0:T(8,128)(2,1)S(1)} %slice.43), channel_id=1, source_target_pairs={{8,0},{16,8},{24,16},{0,24},{9,1},{17,9},{25,17},{1,25},{10,2},{18... | collective-permute-start | bytes 147464 | tf_op jit(solution)/shard_map/ppermute | solution.py:22
  120.3 11.1 %collective-permute-start.32 = (f32[240,512]{1,0:T(8,128)S(1)}, f32[240,512]{1,0:T(8,128)S(1)}, u32[]{:S(2)}, u32[]{:S(2)}) collective-permute-start(f32[240,512]{1,0:T(8,128)S(1)} %get-tuple-element.60), channel_id=1, source_target_pairs={{1,0},{0,1},{3,2},{2,3},{5,4},{4,5},{7,6},{6,7},{9,8},{8,9},{11,10... | collective-permute-start | bytes 1474568 | tf_op jit(solution)/shard_map/ppermute | solution.py:26
  126.4 10.9 %all-to-all-start = ((f32[16,8,512]{2,1,0:T(8,128)}), f32[16,8,512]{2,1,0:T(8,128)S(1)}, u32[]{:S(2)}, u32[]{:S(2)}) async-start(f32[16,8,512]{2,1,0:T(8,128)} %get-tuple-element.64), calls=%async_computation | async-start | bytes 524288 | tf_op jit(solution)/shard_map/all_to_all | solution.py:388
  130.1 1.4 %collective-permute-start.33 = (f32[80,512]{1,0:T(8,128)S(1)}, f32[80,512]{1,0:T(8,128)S(1)}, u32[]{:S(2)}, u32[]{:S(2)}) collective-permute-start(f32[80,512]{1,0:T(8,128)S(1)} %get-tuple-element.61), channel_id=1, source_target_pairs={{1,0},{0,1},{3,2},{2,3},{5,4},{4,5},{7,6},{6,7},{9,8},{8,9},{11,10... | collective-permute-start | bytes 491528 | tf_op jit(solution)/shard_map/ppermute | solution.py:26

commit v3 on v2

--- a/solution.py
+++ b/solution.py
@@ -227,15 +227,14 @@
         acc[:, cols] = jnp.concatenate(got + [zero + part] + [zero] * 5, 0)
 
 
-def last_product_kernel(r2lo, r2hi, r24lo, r24hi, n, acc, my, send, sums, gram):
+def last_product_kernel(r2lo, r2hi, r24, n, acc, my, send, sums, gram):
     low, three = r2lo.shape
     rx, width, cw = gram.shape[0], my.shape[1], three // 3
     at = row_starts(rx)[2]
     gram[0:low, :three] = r2lo[...]
     gram[low:, :three] = r2hi[...]
-    gram[0:low, three:] = r24lo[:, :cw]
-    gram[low:, three:] = r24hi[:, :cw]
-    part = lane_sum(r24lo, cw)
+    gram[:, three:] = r24[:, :cw]
+    part = lane_sum(r24, cw)
     zero = jnp.zeros((1, width), f32)
     got = []
     for out, cols in ((send, slice(width, 2 * width)), (my, slice(0, width))):
@@ -368,7 +367,7 @@
     (early,) = call(first_join_kernel, [like((rx, 3 * cw), bf16)], pay, z1, z3)
     r1, r3, r2lo, r2hi = ring(early, "x")
     (late,) = call(last_join_kernel, [like((rx, cw + 128), bf16)], pay, z1, z3, *z2)
-    r14, r34, r24lo, r24hi = ring(late, "x")
+    r24, r14, r34 = (from_axis(late, "x", k) for k in (2, 3, 1))
     wide, three, quarter = like((rows, width), f32), like((3 * rx, width), f32), like((rx, width), f32)
     my3, send3, acc = call(
         first_product_kernel,
@@ -381,7 +380,7 @@
     my1, send1, sums = call(
         last_product_kernel,
         [quarter, quarter, like((16, 8, width), f32)],
-        *(r2lo, r2hi, r24lo, r24hi, n, acc),
+        *(r2lo, r2hi, r24, n, acc),
         scratch=[pltpu.VMEM((rx, images), bf16)],
     )
     other1 = from_pair(send1, "core")

time: 140 us -> 145 us (1.036)
  waiting for transfers between devices: 61.2 us -> 70 us
  starting transfers between devices: 59.8 us -> 56.8 us
    ppermute x25 -> x24, waiting for transfers between devices: 42.2 us -> 50.9 us  [from_axis(): return lax.ppermute(v, axis, [((i + k) % 4, i) for i in range(4)])]
    ppermute x25 -> x24, starting transfers between devices: 39.8 us -> 37 us  [from_axis(): return lax.ppermute(v, axis, [((i + k) % 4, i) for i in range(4)])]
  transfers between devices with their start and end apart: 35 -> 34, of which waited for: 21 -> 19; matrix products, arithmetic and copies ran while one was open for 0% -> 0% of each run, Pallas kernels for 6% -> 6%
where the time goes in v3:
time: 145 us
  waiting for transfers between devices  70 us (48%)
  starting transfers between devices  56.8 us (39%)
  Pallas kernels  15.9 us (11%)
    ppermute x24, waiting for transfers between devices, from_axis(): return lax.ppermute(v, axis, [((i + k) % 4, i) for i in range(4)])  50.9 us
    ppermute x24, starting transfers between devices, from_axis(): return lax.ppermute(v, axis, [((i + k) % 4, i) for i in range(4)])  37 us
    ppermute x9, starting transfers between devices, from_pair(): return lax.ppermute(v, axis, [(1, 0), (0, 1)])  16.3 us
    pallas_call x13, Pallas kernels, call(): pl.pallas_call(kernel, out_shape=outs, in_specs=[pl.BlockSpec(memory_spac...  15.9 us
    ppermute x9, waiting for transfers between devices, from_pair(): return lax.ppermute(v, axis, [(1, 0), (0, 1)])  13.4 us
    all_to_all x1, waiting for transfers between devices, per_device(): lax.all_to_all(sums, batch + ('core',), split_axis=0, concat_axis=0, tile...  5.72 us
    all_to_all x1, starting transfers between devices, per_device(): lax.all_to_all(sums, batch + ('core',), split_axis=0, concat_axis=0, tile...  3.55 us
  transfers between devices with their start and end apart: 34, of which 19 were waited for; matrix products, arithmetic and copies ran while one was open for 0% of the time, Pallas kernels for 6%

profile of v3, /device:TPU:1, one launch (start us, length us, event | category | flops | bytes accessed | tf_op | source)
XLA Modules:
  0.0 145.0 jit_solution(15947918722108541524)
XLA Ops:
  0.6 1.1 broadcast_select_fusion.1
  1.8 3.3 %collective-permute-start = (bf16[320,512]{1,0:T(8,128)(2,1)S(1)}, bf16[320,512]{1,0:T(8,128)(2,1)S(1)}, u32[]{:S(2)}, u32[]{:S(2)}) collective-permute-start(bf16[320,512]{1,0:T(8,128)(2,1)S(1)} %get-tuple-element.70), channel_id=1, source_target_pairs={{1,0},{0,1},{3,2},{2,3},{5,4},{4,5},{7,6},{6,7},{9,8},{8,9},{11,10... | collective-permute-start | bytes 983048 | tf_op jit(solution)/shard_map/ppermute | solution.py:26
  5.1 1.3 collective-permute-done
  6.3 0.1 pad_maximum_fusion.own
  6.4 0.1 collective-permute-start.3
  6.5 2.7 %collective-permute-start.2 = (bf16[320,1024]{1,0:T(8,128)(2,1)S(1)}, bf16[320,1024]{1,0:T(8,128)(2,1)S(1)}, u32[]{:S(2)}, u32[]{:S(2)}) collective-permute-start(bf16[320,1024]{1,0:T(8,128)(2,1)S(1)} %pad_maximum_fusion.own), channel_id=1, source_target_pairs={{64,0},{128,64},{192,128},{0,192},{65,1},{129,65},{193,129},{1,193... | collective-permute-start | bytes 1966088 | tf_op jit(solution)/shard_map/ppermute | solution.py:22
  9.2 0.0 collective-permute-start.1
  9.2 14.4 %collective-permute-done.3.refs_2_ = bf16[320,1024]{1,0:T(8,128)(2,1)S(1)} collective-permute-done((bf16[320,1024]{1,0:T(8,128)(2,1)S(1)}, bf16[320,1024]{1,0:T(8,128)(2,1)S(1)}, u32[]{:S(2)}, u32[]{:S(2)}) %collective-permute-start.3) | collective-permute-done | bytes 655392 | tf_op jit(solution)/shard_map/ppermute | solution.py:22
  23.7 0.1 collective-permute-start.5
  23.8 2.7 %collective-permute-start.4 = (bf16[160,1024]{1,0:T(8,128)(2,1)S(1)}, bf16[160,1024]{1,0:T(8,128)(2,1)S(1)}, u32[]{:S(2)}, u32[]{:S(2)}) collective-permute-start(bf16[160,1024]{1,0:T(8,128)(2,1)S(1)} %slice.28), channel_id=1, source_target_pairs={{64,0},{128,64},{192,128},{0,192},{65,1},{129,65},{193,129},{1,193... | collective-permute-start | bytes 983048 | tf_op jit(solution)/shard_map/ppermute | solution.py:22
  26.6 2.7 %collective-permute-start.6 = (bf16[320,1024]{1,0:T(8,128)(2,1)S(1)}, bf16[320,1024]{1,0:T(8,128)(2,1)S(1)}, u32[]{:S(2)}, u32[]{:S(2)}) collective-permute-start(bf16[320,1024]{1,0:T(8,128)(2,1)S(1)} %collective-permute-done.1.refs_0_), channel_id=1, source_target_pairs={{64,0},{128,64},{192,128},{0,192},{65,1},{129,65},{193,129},{1,193... | collective-permute-start | bytes 1966088 | tf_op jit(solution)/shard_map/ppermute | solution.py:22
  29.2 3.7 %collective-permute-done.5.refs_4_ = bf16[160,1024]{1,0:T(8,128)(2,1)S(1)} collective-permute-done((bf16[160,1024]{1,0:T(8,128)(2,1)S(1)}, bf16[160,1024]{1,0:T(8,128)(2,1)S(1)}, u32[]{:S(2)}, u32[]{:S(2)}) %collective-permute-start.5) | collective-permute-done | bytes 327712 | tf_op jit(solution)/shard_map/ppermute | solution.py:22
  33.0 0.1 collective-permute-start.9
  33.1 1.4 collective-permute-start.8
  34.4 1.8 %shard_map.49 = (f32[24,1024]{1,0:T(8,128)S(1)}, bf16[1600,1024]{1,0:T(8,128)(2,1)S(1)}) custom-call(bf16[320,1024]{1,0:T(8,128)(2,1)S(1)} %pad_maximum_fusion.own, bf16[320,1024]{1,0:T(8,128)(2,1)S(1)} %collective-permute-done.1.refs_0_, bf16[320,1024]{1,0:T(8,128)(2,1)S(1)} %collective-permute-done.2.refs_1_, ...), custom_call_target="tpu_custom_call" | custom-call | tf_op jit(solution)/shard_map/pallas_call | solution.py:298
  36.3 2.9 %collective-permute-done.9.refs_3_ = bf16[160,1024]{1,0:T(8,128)(2,1)S(1)} collective-permute-done((bf16[160,1024]{1,0:T(8,128)(2,1)S(1)}, bf16[160,1024]{1,0:T(8,128)(2,1)S(1)}, u32[]{:S(2)}, u32[]{:S(2)}) %collective-permute-start.9) | collective-permute-done | bytes 327712 | tf_op jit(solution)/shard_map/ppermute | solution.py:26
  39.2 6.2 %collective-permute-done.8.refs_2_ = bf16[160,1024]{1,0:T(8,128)(2,1)S(1)} collective-permute-done((bf16[160,1024]{1,0:T(8,128)(2,1)S(1)}, bf16[160,1024]{1,0:T(8,128)(2,1)S(1)}, u32[]{:S(2)}, u32[]{:S(2)}) %collective-permute-start.8) | collective-permute-done | bytes 327712 | tf_op jit(solution)/shard_map/ppermute | solution.py:26
  45.4 1.7 %collective-permute-done.7.refs_1_ = bf16[320,1024]{1,0:T(8,128)(2,1)S(1)} collective-permute-done((bf16[320,1024]{1,0:T(8,128)(2,1)S(1)}, bf16[320,1024]{1,0:T(8,128)(2,1)S(1)}, u32[]{:S(2)}, u32[]{:S(2)}) %collective-permute-start.7) | collective-permute-done | bytes 655392 | tf_op jit(solution)/shard_map/ppermute | solution.py:22
  47.0 4.6 %shard_map.50 = (bf16[2560,1024]{1,0:T(8,128)(2,1)S(1)}, bf16[2560,512]{1,0:T(8,128)(2,1)S(1)}, f32[8,1024]{1,0:T(8,128)S(1)}, bf16[48,2560]{1,0:T(8,128)(2,1)S(1)}, bf16[32,2560]{1,0:T(8,128)(2,1)S(1)}) custom-call(f32[24,1024]{1,0:T(8,128)S(1)} %get-tuple-element.36.st, bf16[1600,1024]{1,0:T(8,128)(2,1)S(1)} %get-tuple-element.37.known, ...), custom_call_target="tpu_custom_call" | custom-call | tf_op jit(solution)/shard_map/pallas_call | solution.py:298
  51.6 0.1 collective-permute-start.10
  51.7 2.7 %collective-permute-start.11 = (bf16[32,2560]{1,0:T(8,128)(2,1)S(1)}, bf16[32,2560]{1,0:T(8,128)(2,1)S(1)}, u32[]{:S(2)}, u32[]{:S(2)}) collective-permute-start(bf16[32,2560]{1,0:T(8,128)(2,1)S(1)} %get-tuple-element.43), channel_id=1, source_target_pairs={{8,0},{16,8},{24,16},{0,24},{9,1},{17,9},{25,17},{1,25},{10,2},{18... | collective-permute-start | bytes 491528 | tf_op jit(solution)/shard_map/ppermute | solution.py:22
  54.4 2.4 %shard_map.51 = (bf16[80,2560]{1,0:T(8,128)(2,1)S(1)}, bf16[80,2560]{1,0:T(8,128)(2,1)S(1)}, bf16[80,2560]{1,0:T(8,128)(2,1)S(1)}) custom-call(bf16[2560,1024]{1,0:T(8,128)(2,1)S(1)} %get-tuple-element.38.n), custom_call_target="tpu_custom_call" | custom-call | tf_op jit(solution)/shard_map/pallas_call | solution.py:298
  56.8 1.2 collective-permute-done.10.a
  58.0 0.1 shard_map.52
  58.1 0.1 collective-permute-start.12
  58.2 2.7 %collective-permute-start.13 = (bf16[80,2560]{1,0:T(8,128)(2,1)S(1)}, bf16[80,2560]{1,0:T(8,128)(2,1)S(1)}, u32[]{:S(2)}, u32[]{:S(2)}) collective-permute-start(bf16[80,2560]{1,0:T(8,128)(2,1)S(1)} %get-tuple-element.45), channel_id=1, source_target_pairs={{8,0},{16,8},{24,16},{0,24},{9,1},{17,9},{25,17},{1,25},{10,2},{18... | collective-permute-start | bytes 1228808 | tf_op jit(solution)/shard_map/ppermute | solution.py:22
  60.8 5.3 %collective-permute-done.12.e = bf16[80,2560]{1,0:T(8,128)(2,1)S(1)} collective-permute-done((bf16[80,2560]{1,0:T(8,128)(2,1)S(1)}, bf16[80,2560]{1,0:T(8,128)(2,1)S(1)}, u32[]{:S(2)}, u32[]{:S(2)}) %collective-permute-start.12) | collective-permute-done | bytes 409632 | tf_op jit(solution)/shard_map/ppermute | solution.py:22
  66.2 0.2 shard_map.53
  66.4 5.5 %collective-permute-start.14 = (bf16[2560,512]{1,0:T(8,128)(2,1)S(1)}, bf16[2560,512]{1,0:T(8,128)(2,1)S(1)}, u32[]{:S(2)}, u32[]{:S(2)}) collective-permute-start(bf16[2560,512]{1,0:T(8,128)(2,1)S(1)} %get-tuple-element.50), channel_id=1, source_target_pairs={{1,0},{0,1},{3,2},{2,3},{5,4},{4,5},{7,6},{6,7},{9,8},{8,9},{11,10... | collective-permute-start | bytes 7864328 | tf_op jit(solution)/shard_map/ppermute | solution.py:26
  71.9 1.8 %collective-permute-start.17 = (bf16[80,640]{1,0:T(8,128)(2,1)S(1)}, bf16[80,640]{1,0:T(8,128)(2,1)S(1)}, u32[]{:S(2)}, u32[]{:S(2)}) collective-permute-start(bf16[80,640]{1,0:T(8,128)(2,1)S(1)} %get-tuple-element.55), channel_id=1, source_target_pairs={{6,0},{0,2},{2,4},{4,6},{7,1},{1,3},{3,5},{5,7},{14,8},{8,10},{10,... | collective-permute-start | bytes 307208 | tf_op jit(solution)/shard_map/ppermute | solution.py:22
  73.7 4.8 %collective-permute-start.16 = (bf16[80,640]{1,0:T(8,128)(2,1)S(1)}, bf16[80,640]{1,0:T(8,128)(2,1)S(1)}, u32[]{:S(2)}, u32[]{:S(2)}) collective-permute-start(bf16[80,640]{1,0:T(8,128)(2,1)S(1)} %get-tuple-element.54), channel_id=1, source_target_pairs={{4,0},{6,2},{0,4},{2,6},{5,1},{7,3},{1,5},{3,7},{12,8},{14,10},{8,... | collective-permute-start | bytes 307208 | tf_op jit(solution)/shard_map/ppermute | solution.py:22
  78.5 2.4 %collective-permute-start.18 = (bf16[80,640]{1,0:T(8,128)(2,1)S(1)}, bf16[80,640]{1,0:T(8,128)(2,1)S(1)}, u32[]{:S(2)}, u32[]{:S(2)}) collective-permute-start(bf16[80,640]{1,0:T(8,128)(2,1)S(1)} %get-tuple-element.56), channel_id=1, source_target_pairs={{2,0},{4,2},{6,4},{0,6},{3,1},{5,3},{7,5},{1,7},{10,8},{12,10},{14... | collective-permute-start | bytes 307208 | tf_op jit(solution)/shard_map/ppermute | solution.py:22
  80.9 0.9 collective-permute-start.15
  81.8 0.8 collective-permute-done.15.inv_o
  82.6 1.1 shard_map.54
  83.7 2.1 %collective-permute-done.16.r1 = bf16[80,640]{1,0:T(8,128)(2,1)S(1)} collective-permute-done((bf16[80,640]{1,0:T(8,128)(2,1)S(1)}, bf16[80,640]{1,0:T(8,128)(2,1)S(1)}, u32[]{:S(2)}, u32[]{:S(2)}) %collective-permute-start.16) | collective-permute-done | bytes 102432 | tf_op jit(solution)/shard_map/ppermute | solution.py:22
  85.9 3.0 %collective-permute-done.18.r3 = bf16[80,640]{1,0:T(8,128)(2,1)S(1)} collective-permute-done((bf16[80,640]{1,0:T(8,128)(2,1)S(1)}, bf16[80,640]{1,0:T(8,128)(2,1)S(1)}, u32[]{:S(2)}, u32[]{:S(2)}) %collective-permute-start.18) | collective-permute-done | bytes 102432 | tf_op jit(solution)/shard_map/ppermute | solution.py:22
  88.8 0.1 shard_map.55.mine
  88.9 0.6 collective-permute-start.19
  89.5 0.9 collective-permute-done.19.theirs
  90.4 0.1 shard_map.56.own
  90.6 3.4 %collective-permute-start.21 = (bf16[80,768]{1,0:T(8,128)(2,1)S(1)}, bf16[80,768]{1,0:T(8,128)(2,1)S(1)}, u32[]{:S(2)}, u32[]{:S(2)}) collective-permute-start(bf16[80,768]{1,0:T(8,128)(2,1)S(1)} %shard_map.56.own), channel_id=1, source_target_pairs={{2,0},{4,2},{6,4},{0,6},{3,1},{5,3},{7,5},{1,7},{10,8},{12,10},{14... | collective-permute-start | bytes 368648 | tf_op jit(solution)/shard_map/ppermute | solution.py:22
  94.0 4.7 %collective-permute-done.21.r3 = bf16[80,768]{1,0:T(8,128)(2,1)S(1)} collective-permute-done((bf16[80,768]{1,0:T(8,128)(2,1)S(1)}, bf16[80,768]{1,0:T(8,128)(2,1)S(1)}, u32[]{:S(2)}, u32[]{:S(2)}) %collective-permute-start.21) | collective-permute-done | bytes 122912 | tf_op jit(solution)/shard_map/ppermute | solution.py:22
  98.6 2.6 %collective-permute-done.20.r1 = bf16[80,768]{1,0:T(8,128)(2,1)S(1)} collective-permute-done((bf16[80,768]{1,0:T(8,128)(2,1)S(1)}, bf16[80,768]{1,0:T(8,128)(2,1)S(1)}, u32[]{:S(2)}, u32[]{:S(2)}) %collective-permute-start.20) | collective-permute-done | bytes 122912 | tf_op jit(solution)/shard_map/ppermute | solution.py:22
  101.2 1.2 collective-permute-start.22
  102.4 1.9 %collective-permute-start.23 = (bf16[80,1920]{1,0:T(8,128)(2,1)S(1)}, bf16[80,1920]{1,0:T(8,128)(2,1)S(1)}, u32[]{:S(2)}, u32[]{:S(2)}) collective-permute-start(bf16[80,1920]{1,0:T(8,128)(2,1)S(1)} %shard_map.57.own), channel_id=1, source_target_pairs={{8,0},{16,8},{24,16},{0,24},{9,1},{17,9},{25,17},{1,25},{10,2},{18... | collective-permute-start | bytes 921608 | tf_op jit(solution)/shard_map/ppermute | solution.py:22
  104.4 0.8 collective-permute-start.24
  105.2 5.6 %collective-permute-done.22.r1 = bf16[80,1920]{1,0:T(8,128)(2,1)S(1)} collective-permute-done((bf16[80,1920]{1,0:T(8,128)(2,1)S(1)}, bf16[80,1920]{1,0:T(8,128)(2,1)S(1)}, u32[]{:S(2)}, u32[]{:S(2)}) %collective-permute-start.22) | collective-permute-done | bytes 307232 | tf_op jit(solution)/shard_map/ppermute | solution.py:22
  110.9 0.3 collective-permute-start.28
  111.2 1.0 collective-permute-start.25
  112.2 3.0 %collective-permute-done.25.r2hi = bf16[32,768]{1,0:T(8,128)(2,1)S(1)} collective-permute-done((bf16[32,768]{1,0:T(8,128)(2,1)S(1)}, bf16[32,768]{1,0:T(8,128)(2,1)S(1)}, u32[]{:S(2)}, u32[]{:S(2)}) %collective-permute-start.25) | collective-permute-done | bytes 49184 | tf_op jit(solution)/shard_map/ppermute | solution.py:22
  115.3 0.1 shard_map.58.own4
  115.4 2.8 %collective-permute-start.27 = (bf16[80,768]{1,0:T(8,128)(2,1)S(1)}, bf16[80,768]{1,0:T(8,128)(2,1)S(1)}, u32[]{:S(2)}, u32[]{:S(2)}) collective-permute-start(bf16[80,768]{1,0:T(8,128)(2,1)S(1)} %shard_map.58.own4), channel_id=1, source_target_pairs={{8,0},{16,8},{24,16},{0,24},{9,1},{17,9},{25,17},{1,25},{10,2},{18... | collective-permute-start | bytes 368648 | tf_op jit(solution)/shard_map/ppermute | solution.py:22
  118.2 1.3 collective-permute-start.30
  119.5 1.4 collective-permute-start.29
  121.0 3.5 %collective-permute-done.26.r14 = bf16[80,768]{1,0:T(8,128)(2,1)S(1)} collective-permute-done((bf16[80,768]{1,0:T(8,128)(2,1)S(1)}, bf16[80,768]{1,0:T(8,128)(2,1)S(1)}, u32[]{:S(2)}, u32[]{:S(2)}) %collective-permute-start.26) | collective-permute-done | bytes 122912 | tf_op jit(solution)/shard_map/ppermute | solution.py:22
  124.4 1.8 %shard_map.59 = (f32[240,512]{1,0:T(8,128)S(1)}, f32[240,512]{1,0:T(8,128)S(1)}, f32[8,1024]{1,0:T(8,128)S(1)}) custom-call(bf16[80,1920]{1,0:T(8,128)(2,1)S(1)} %shard_map.57.own, bf16[80,1920]{1,0:T(8,128)(2,1)S(1)} %collective-permute-done.22.r1, bf16[80,1920]{1,0:T(8,128)(2,1)S(1)} %collective-permute-done.23.r3, bf16[80,768]{1,0:T(8,128)(2,1)S(1)} %shard_map.58.own4, ...), custom_call_target="tpu_custom_call" | custom-call | tf_op jit(solution)/shard_map/pallas_call | solution.py:298
  126.2 4.3 %collective-permute-start.31 = (f32[240,512]{1,0:T(8,128)S(1)}, f32[240,512]{1,0:T(8,128)S(1)}, u32[]{:S(2)}, u32[]{:S(2)}) collective-permute-start(f32[240,512]{1,0:T(8,128)S(1)} %get-tuple-element.60), channel_id=1, source_target_pairs={{1,0},{0,1},{3,2},{2,3},{5,4},{4,5},{7,6},{6,7},{9,8},{8,9},{11,10... | collective-permute-start | bytes 1474568 | tf_op jit(solution)/shard_map/ppermute | solution.py:26
  130.5 1.8 %shard_map.60 = (f32[80,512]{1,0:T(8,128)S(1)}, f32[80,512]{1,0:T(8,128)S(1)}, f32[16,8,512]{2,1,0:T(8,128)}) custom-call(bf16[48,1920]{1,0:T(8,128)(2,1)S(1)} %collective-permute-done.28.r2lo, bf16[32,1920]{1,0:T(8,128)(2,1)S(1)} %collective-permute-done.29.r2hi, bf16[80,768]{1,0:T(8,128)(2,1)S(1)} %collective-permute-done.30.r24, ...), custom_call_target="tpu_custom_call" | custom-call | tf_op jit(solution)/shard_map/pallas_call | solution.py:298
  132.3 3.6 %all-to-all-start = ((f32[16,8,512]{2,1,0:T(8,128)}), f32[16,8,512]{2,1,0:T(8,128)S(1)}, u32[]{:S(2)}, u32[]{:S(2)}) async-start(f32[16,8,512]{2,1,0:T(8,128)} %get-tuple-element.64), calls=%async_computation | async-start | bytes 524288 | tf_op jit(solution)/shard_map/all_to_all | solution.py:387
  135.9 0.2 collective-permute-start.32
  136.1 1.3 collective-permute-done.32.other1
  137.3 5.7 %all-to-all-done.sums = f32[16,8,512]{2,1,0:T(8,128)S(1)} async-done(((f32[16,8,512]{2,1,0:T(8,128)}), f32[16,8,512]{2,1,0:T(8,128)S(1)}, u32[]{:S(2)}, u32[]{:S(2)}) %all-to-all-start) | async-done | bytes 262176 | tf_op jit(solution)/shard_map/all_to_all | solution.py:387
  143.1 1.7 %shard_map.61 = (f32[1,1]{1,0:T(1,128)}, f32[320,512]{1,0:T(8,128)}, f32[320,512]{1,0:T(8,128)}) custom-call(f32[240,512]{1,0:T(8,128)S(1)} %get-tuple-element.57.my3, f32[80,512]{1,0:T(8,128)S(1)} %get-tuple-element.59.my1, f32[240,512]{1,0:T(8,128)S(1)} %collective-permute-done.31.other3, f32[80,512]{1,0:T(8,128)S(1)} %collective-permute-done.32.other1, ...), custom_call_target="tpu_custom_call" | custom-call | tf_op jit(solution)/shard_map/pallas_call | solution.py:298
  (26 shorter events, 0.2 us)
Async XLA Ops:
  1.8 4.6 %collective-permute-start = (bf16[320,512]{1,0:T(8,128)(2,1)S(1)}, bf16[320,512]{1,0:T(8,128)(2,1)S(1)}, u32[]{:S(2)}, u32[]{:S(2)}) collective-permute-start(bf16[320,512]{1,0:T(8,128)(2,1)S(1)} %get-tuple-element.70), channel_id=1, source_target_pairs={{1,0},{0,1},{3,2},{2,3},{5,4},{4,5},{7,6},{6,7},{9,8},{8,9},{11,10... | collective-permute-start | bytes 983048 | tf_op jit(solution)/shard_map/ppermute | solution.py:26
  6.4 17.2 %collective-permute-start.3 = (bf16[320,1024]{1,0:T(8,128)(2,1)S(1)}, bf16[320,1024]{1,0:T(8,128)(2,1)S(1)}, u32[]{:S(2)}, u32[]{:S(2)}) collective-permute-start(bf16[320,1024]{1,0:T(8,128)(2,1)S(1)} %pad_maximum_fusion.own), channel_id=1, source_target_pairs={{192,0},{0,64},{64,128},{128,192},{193,1},{1,65},{65,129},{129,193... | collective-permute-start | bytes 1966088 | tf_op jit(solution)/shard_map/ppermute | solution.py:22
  6.5 17.3 %collective-permute-start.2 = (bf16[320,1024]{1,0:T(8,128)(2,1)S(1)}, bf16[320,1024]{1,0:T(8,128)(2,1)S(1)}, u32[]{:S(2)}, u32[]{:S(2)}) collective-permute-start(bf16[320,1024]{1,0:T(8,128)(2,1)S(1)} %pad_maximum_fusion.own), channel_id=1, source_target_pairs={{64,0},{128,64},{192,128},{0,192},{65,1},{129,65},{193,129},{1,193... | collective-permute-start | bytes 1966088 | tf_op jit(solution)/shard_map/ppermute | solution.py:22
  9.2 17.4 %collective-permute-start.1 = (bf16[320,1024]{1,0:T(8,128)(2,1)S(1)}, bf16[320,1024]{1,0:T(8,128)(2,1)S(1)}, u32[]{:S(2)}, u32[]{:S(2)}) collective-permute-start(bf16[320,1024]{1,0:T(8,128)(2,1)S(1)} %pad_maximum_fusion.own), channel_id=1, source_target_pairs={{32,0},{0,32},{33,1},{1,33},{34,2},{2,34},{35,3},{3,35},{36,4},{4,... | collective-permute-start | bytes 1966088 | tf_op jit(solution)/shard_map/ppermute | solution.py:26
  23.7 9.3 %collective-permute-start.5 = (bf16[160,1024]{1,0:T(8,128)(2,1)S(1)}, bf16[160,1024]{1,0:T(8,128)(2,1)S(1)}, u32[]{:S(2)}, u32[]{:S(2)}) collective-permute-start(bf16[160,1024]{1,0:T(8,128)(2,1)S(1)} %slice.29), channel_id=1, source_target_pairs={{192,0},{0,64},{64,128},{128,192},{193,1},{1,65},{65,129},{129,193... | collective-permute-start | bytes 983048 | tf_op jit(solution)/shard_map/ppermute | solution.py:22
  23.8 9.3 %collective-permute-start.4 = (bf16[160,1024]{1,0:T(8,128)(2,1)S(1)}, bf16[160,1024]{1,0:T(8,128)(2,1)S(1)}, u32[]{:S(2)}, u32[]{:S(2)}) collective-permute-start(bf16[160,1024]{1,0:T(8,128)(2,1)S(1)} %slice.28), channel_id=1, source_target_pairs={{64,0},{128,64},{192,128},{0,192},{65,1},{129,65},{193,129},{1,193... | collective-permute-start | bytes 983048 | tf_op jit(solution)/shard_map/ppermute | solution.py:22
  26.5 20.5 %collective-permute-start.7 = (bf16[320,1024]{1,0:T(8,128)(2,1)S(1)}, bf16[320,1024]{1,0:T(8,128)(2,1)S(1)}, u32[]{:S(2)}, u32[]{:S(2)}) collective-permute-start(bf16[320,1024]{1,0:T(8,128)(2,1)S(1)} %collective-permute-done.1.refs_0_), channel_id=1, source_target_pairs={{192,0},{0,64},{64,128},{128,192},{193,1},{1,65},{65,129},{129,193... | collective-permute-start | bytes 1966088 | tf_op jit(solution)/shard_map/ppermute | solution.py:22
  26.6 20.5 %collective-permute-start.6 = (bf16[320,1024]{1,0:T(8,128)(2,1)S(1)}, bf16[320,1024]{1,0:T(8,128)(2,1)S(1)}, u32[]{:S(2)}, u32[]{:S(2)}) collective-permute-start(bf16[320,1024]{1,0:T(8,128)(2,1)S(1)} %collective-permute-done.1.refs_0_), channel_id=1, source_target_pairs={{64,0},{128,64},{192,128},{0,192},{65,1},{129,65},{193,129},{1,193... | collective-permute-start | bytes 1966088 | tf_op jit(solution)/shard_map/ppermute | solution.py:22
  33.0 6.2 %collective-permute-start.9 = (bf16[160,1024]{1,0:T(8,128)(2,1)S(1)}, bf16[160,1024]{1,0:T(8,128)(2,1)S(1)}, u32[]{:S(2)}, u32[]{:S(2)}) collective-permute-start(bf16[160,1024]{1,0:T(8,128)(2,1)S(1)} %collective-permute-done.5.refs_4_), channel_id=1, source_target_pairs={{32,0},{0,32},{33,1},{1,33},{34,2},{2,34},{35,3},{3,35},{36,4},{4,... | collective-permute-start | bytes 983048 | tf_op jit(solution)/shard_map/ppermute | solution.py:26
  33.1 12.3 %collective-permute-start.8 = (bf16[160,1024]{1,0:T(8,128)(2,1)S(1)}, bf16[160,1024]{1,0:T(8,128)(2,1)S(1)}, u32[]{:S(2)}, u32[]{:S(2)}) collective-permute-start(bf16[160,1024]{1,0:T(8,128)(2,1)S(1)} %collective-permute-done.4.refs_3_), channel_id=1, source_target_pairs={{32,0},{0,32},{33,1},{1,33},{34,2},{2,34},{35,3},{3,35},{36,4},{4,... | collective-permute-start | bytes 983048 | tf_op jit(solution)/shard_map/ppermute | solution.py:26
  51.6 6.3 %collective-permute-start.10 = (bf16[48,2560]{1,0:T(8,128)(2,1)S(1)}, bf16[48,2560]{1,0:T(8,128)(2,1)S(1)}, u32[]{:S(2)}, u32[]{:S(2)}) collective-permute-start(bf16[48,2560]{1,0:T(8,128)(2,1)S(1)} %get-tuple-element.41), channel_id=1, source_target_pairs={{24,0},{0,8},{8,16},{16,24},{25,1},{1,9},{9,17},{17,25},{26,2},{2,... | collective-permute-start | bytes 737288 | tf_op jit(solution)/shard_map/ppermute | solution.py:22
  51.7 5.0 %collective-permute-start.11 = (bf16[32,2560]{1,0:T(8,128)(2,1)S(1)}, bf16[32,2560]{1,0:T(8,128)(2,1)S(1)}, u32[]{:S(2)}, u32[]{:S(2)}) collective-permute-start(bf16[32,2560]{1,0:T(8,128)(2,1)S(1)} %get-tuple-element.43), channel_id=1, source_target_pairs={{8,0},{16,8},{24,16},{0,24},{9,1},{17,9},{25,17},{1,25},{10,2},{18... | collective-permute-start | bytes 491528 | tf_op jit(solution)/shard_map/ppermute | solution.py:22
  58.1 8.1 %collective-permute-start.12 = (bf16[80,2560]{1,0:T(8,128)(2,1)S(1)}, bf16[80,2560]{1,0:T(8,128)(2,1)S(1)}, u32[]{:S(2)}, u32[]{:S(2)}) collective-permute-start(bf16[80,2560]{1,0:T(8,128)(2,1)S(1)} %get-tuple-element.44), channel_id=1, source_target_pairs={{24,0},{0,8},{8,16},{16,24},{25,1},{1,9},{9,17},{17,25},{26,2},{2,... | collective-permute-start | bytes 1228808 | tf_op jit(solution)/shard_map/ppermute | solution.py:22
  58.2 8.0 %collective-permute-start.13 = (bf16[80,2560]{1,0:T(8,128)(2,1)S(1)}, bf16[80,2560]{1,0:T(8,128)(2,1)S(1)}, u32[]{:S(2)}, u32[]{:S(2)}) collective-permute-start(bf16[80,2560]{1,0:T(8,128)(2,1)S(1)} %get-tuple-element.45), channel_id=1, source_target_pairs={{8,0},{16,8},{24,16},{0,24},{9,1},{17,9},{25,17},{1,25},{10,2},{18... | collective-permute-start | bytes 1228808 | tf_op jit(solution)/shard_map/ppermute | solution.py:22
  66.4 16.2 %collective-permute-start.14 = (bf16[2560,512]{1,0:T(8,128)(2,1)S(1)}, bf16[2560,512]{1,0:T(8,128)(2,1)S(1)}, u32[]{:S(2)}, u32[]{:S(2)}) collective-permute-start(bf16[2560,512]{1,0:T(8,128)(2,1)S(1)} %get-tuple-element.50), channel_id=1, source_target_pairs={{1,0},{0,1},{3,2},{2,3},{5,4},{4,5},{7,6},{6,7},{9,8},{8,9},{11,10... | collective-permute-start | bytes 7864328 | tf_op jit(solution)/shard_map/ppermute | solution.py:26
  71.9 11.8 %collective-permute-start.17 = (bf16[80,640]{1,0:T(8,128)(2,1)S(1)}, bf16[80,640]{1,0:T(8,128)(2,1)S(1)}, u32[]{:S(2)}, u32[]{:S(2)}) collective-permute-start(bf16[80,640]{1,0:T(8,128)(2,1)S(1)} %get-tuple-element.55), channel_id=1, source_target_pairs={{6,0},{0,2},{2,4},{4,6},{7,1},{1,3},{3,5},{5,7},{14,8},{8,10},{10,... | collective-permute-start | bytes 307208 | tf_op jit(solution)/shard_map/ppermute | solution.py:22
  73.7 12.2 %collective-permute-start.16 = (bf16[80,640]{1,0:T(8,128)(2,1)S(1)}, bf16[80,640]{1,0:T(8,128)(2,1)S(1)}, u32[]{:S(2)}, u32[]{:S(2)}) collective-permute-start(bf16[80,640]{1,0:T(8,128)(2,1)S(1)} %get-tuple-element.54), channel_id=1, source_target_pairs={{4,0},{6,2},{0,4},{2,6},{5,1},{7,3},{1,5},{3,7},{12,8},{14,10},{8,... | collective-permute-start | bytes 307208 | tf_op jit(solution)/shard_map/ppermute | solution.py:22
  78.5 10.4 %collective-permute-start.18 = (bf16[80,640]{1,0:T(8,128)(2,1)S(1)}, bf16[80,640]{1,0:T(8,128)(2,1)S(1)}, u32[]{:S(2)}, u32[]{:S(2)}) collective-permute-start(bf16[80,640]{1,0:T(8,128)(2,1)S(1)} %get-tuple-element.56), channel_id=1, source_target_pairs={{2,0},{4,2},{6,4},{0,6},{3,1},{5,3},{7,5},{1,7},{10,8},{12,10},{14... | collective-permute-start | bytes 307208 | tf_op jit(solution)/shard_map/ppermute | solution.py:22
  80.9 1.8 %collective-permute-start.15 = (f32[8,512]{1,0:T(8,128)S(1)}, f32[8,512]{1,0:T(8,128)S(1)}, u32[]{:S(2)}, u32[]{:S(2)}) collective-permute-start(f32[8,512]{1,0:T(8,128)S(1)} %slice.23), channel_id=1, source_target_pairs={{1,0},{0,1},{3,2},{2,3},{5,4},{4,5},{7,6},{6,7},{9,8},{8,9},{11,10... | collective-permute-start | bytes 49160 | tf_op jit(solution)/shard_map/ppermute | solution.py:26
  88.9 1.5 %collective-permute-start.19 = (bf16[80,640]{1,0:T(8,128)(2,1)S(1)}, bf16[80,640]{1,0:T(8,128)(2,1)S(1)}, u32[]{:S(2)}, u32[]{:S(2)}) collective-permute-start(bf16[80,640]{1,0:T(8,128)(2,1)S(1)} %shard_map.55.mine), channel_id=1, source_target_pairs={{1,0},{0,1},{3,2},{2,3},{5,4},{4,5},{7,6},{6,7},{9,8},{8,9},{11,10... | collective-permute-start | bytes 307208 | tf_op jit(solution)/shard_map/ppermute | solution.py:26
  90.6 8.1 %collective-permute-start.21 = (bf16[80,768]{1,0:T(8,128)(2,1)S(1)}, bf16[80,768]{1,0:T(8,128)(2,1)S(1)}, u32[]{:S(2)}, u32[]{:S(2)}) collective-permute-start(bf16[80,768]{1,0:T(8,128)(2,1)S(1)} %shard_map.56.own), channel_id=1, source_target_pairs={{2,0},{4,2},{6,4},{0,6},{3,1},{5,3},{7,5},{1,7},{10,8},{12,10},{14... | collective-permute-start | bytes 368648 | tf_op jit(solution)/shard_map/ppermute | solution.py:22
  93.9 7.3 %collective-permute-start.20 = (bf16[80,768]{1,0:T(8,128)(2,1)S(1)}, bf16[80,768]{1,0:T(8,128)(2,1)S(1)}, u32[]{:S(2)}, u32[]{:S(2)}) collective-permute-start(bf16[80,768]{1,0:T(8,128)(2,1)S(1)} %shard_map.56.own), channel_id=1, source_target_pairs={{6,0},{0,2},{2,4},{4,6},{7,1},{1,3},{3,5},{5,7},{14,8},{8,10},{10,... | collective-permute-start | bytes 368648 | tf_op jit(solution)/shard_map/ppermute | solution.py:22
  101.2 9.6 %collective-permute-start.22 = (bf16[80,1920]{1,0:T(8,128)(2,1)S(1)}, bf16[80,1920]{1,0:T(8,128)(2,1)S(1)}, u32[]{:S(2)}, u32[]{:S(2)}) collective-permute-start(bf16[80,1920]{1,0:T(8,128)(2,1)S(1)} %shard_map.57.own), channel_id=1, source_target_pairs={{24,0},{0,8},{8,16},{16,24},{25,1},{1,9},{9,17},{17,25},{26,2},{2,... | collective-permute-start | bytes 921608 | tf_op jit(solution)/shard_map/ppermute | solution.py:22
  102.4 17.1 %collective-permute-start.23 = (bf16[80,1920]{1,0:T(8,128)(2,1)S(1)}, bf16[80,1920]{1,0:T(8,128)(2,1)S(1)}, u32[]{:S(2)}, u32[]{:S(2)}) collective-permute-start(bf16[80,1920]{1,0:T(8,128)(2,1)S(1)} %shard_map.57.own), channel_id=1, source_target_pairs={{8,0},{16,8},{24,16},{0,24},{9,1},{17,9},{25,17},{1,25},{10,2},{18... | collective-permute-start | bytes 921608 | tf_op jit(solution)/shard_map/ppermute | solution.py:22
  104.4 10.9 %collective-permute-start.24 = (bf16[48,768]{1,0:T(8,128)(2,1)S(1)}, bf16[48,768]{1,0:T(8,128)(2,1)S(1)}, u32[]{:S(2)}, u32[]{:S(2)}) collective-permute-start(bf16[48,768]{1,0:T(8,128)(2,1)S(1)} %slice.30), channel_id=1, source_target_pairs={{6,0},{0,2},{2,4},{4,6},{7,1},{1,3},{3,5},{5,7},{14,8},{8,10},{10,... | collective-permute-start | bytes 221192 | tf_op jit(solution)/shard_map/ppermute | solution.py:22
  110.9 19.6 %collective-permute-start.28 = (bf16[48,1920]{1,0:T(8,128)(2,1)S(1)}, bf16[48,1920]{1,0:T(8,128)(2,1)S(1)}, u32[]{:S(2)}, u32[]{:S(2)}) collective-permute-start(bf16[48,1920]{1,0:T(8,128)(2,1)S(1)} %slice.32), channel_id=1, source_target_pairs={{24,0},{0,8},{8,16},{16,24},{25,1},{1,9},{9,17},{17,25},{26,2},{2,... | collective-permute-start | bytes 552968 | tf_op jit(solution)/shard_map/ppermute | solution.py:22
  111.2 4.1 %collective-permute-start.25 = (bf16[32,768]{1,0:T(8,128)(2,1)S(1)}, bf16[32,768]{1,0:T(8,128)(2,1)S(1)}, u32[]{:S(2)}, u32[]{:S(2)}) collective-permute-start(bf16[32,768]{1,0:T(8,128)(2,1)S(1)} %slice.31), channel_id=1, source_target_pairs={{2,0},{4,2},{6,4},{0,6},{3,1},{5,3},{7,5},{1,7},{10,8},{12,10},{14... | collective-permute-start | bytes 147464 | tf_op jit(solution)/shard_map/ppermute | solution.py:22
  115.4 5.6 %collective-permute-start.27 = (bf16[80,768]{1,0:T(8,128)(2,1)S(1)}, bf16[80,768]{1,0:T(8,128)(2,1)S(1)}, u32[]{:S(2)}, u32[]{:S(2)}) collective-permute-start(bf16[80,768]{1,0:T(8,128)(2,1)S(1)} %shard_map.58.own4), channel_id=1, source_target_pairs={{8,0},{16,8},{24,16},{0,24},{9,1},{17,9},{25,17},{1,25},{10,2},{18... | collective-permute-start | bytes 368648 | tf_op jit(solution)/shard_map/ppermute | solution.py:22
  118.2 6.3 %collective-permute-start.26 = (bf16[80,768]{1,0:T(8,128)(2,1)S(1)}, bf16[80,768]{1,0:T(8,128)(2,1)S(1)}, u32[]{:S(2)}, u32[]{:S(2)}) collective-permute-start(bf16[80,768]{1,0:T(8,128)(2,1)S(1)} %shard_map.58.own4), channel_id=1, source_target_pairs={{24,0},{0,8},{8,16},{16,24},{25,1},{1,9},{9,17},{17,25},{26,2},{2,... | collective-permute-start | bytes 368648 | tf_op jit(solution)/shard_map/ppermute | solution.py:22
  118.2 12.3 %collective-permute-start.30 = (bf16[80,768]{1,0:T(8,128)(2,1)S(1)}, bf16[80,768]{1,0:T(8,128)(2,1)S(1)}, u32[]{:S(2)}, u32[]{:S(2)}) collective-permute-start(bf16[80,768]{1,0:T(8,128)(2,1)S(1)} %shard_map.58.own4), channel_id=1, source_target_pairs={{16,0},{24,8},{0,16},{8,24},{17,1},{25,9},{1,17},{9,25},{18,2},{26... | collective-permute-start | bytes 368648 | tf_op jit(solution)/shard_map/ppermute | solution.py:22
  119.5 11.0 %collective-permute-start.29 = (bf16[32,1920]{1,0:T(8,128)(2,1)S(1)}, bf16[32,1920]{1,0:T(8,128)(2,1)S(1)}, u32[]{:S(2)}, u32[]{:S(2)}) collective-permute-start(bf16[32,1920]{1,0:T(8,128)(2,1)S(1)} %slice.33), channel_id=1, source_target_pairs={{8,0},{16,8},{24,16},{0,24},{9,1},{17,9},{25,17},{1,25},{10,2},{18... | collective-permute-start | bytes 368648 | tf_op jit(solution)/shard_map/ppermute | solution.py:22
  126.2 11.1 %collective-permute-start.31 = (f32[240,512]{1,0:T(8,128)S(1)}, f32[240,512]{1,0:T(8,128)S(1)}, u32[]{:S(2)}, u32[]{:S(2)}) collective-permute-start(f32[240,512]{1,0:T(8,128)S(1)} %get-tuple-element.60), channel_id=1, source_target_pairs={{1,0},{0,1},{3,2},{2,3},{5,4},{4,5},{7,6},{6,7},{9,8},{8,9},{11,10... | collective-permute-start | bytes 1474568 | tf_op jit(solution)/shard_map/ppermute | solution.py:26
  132.3 10.7 %all-to-all-start = ((f32[16,8,512]{2,1,0:T(8,128)}), f32[16,8,512]{2,1,0:T(8,128)S(1)}, u32[]{:S(2)}, u32[]{:S(2)}) async-start(f32[16,8,512]{2,1,0:T(8,128)} %get-tuple-element.64), calls=%async_computation | async-start | bytes 524288 | tf_op jit(solution)/shard_map/all_to_all | solution.py:387
  135.9 1.4 collective-permute-start.32

commit v4 on v3

--- a/solution.py
+++ b/solution.py
@@ -365,9 +365,11 @@
     z1, z3 = from_axis(pay, "zh", 3), from_axis(pay, "zh", 1)
     z2 = from_axis(z1[:low], "zh", 3), from_axis(z3[low:], "zh", 1)
     (early,) = call(first_join_kernel, [like((rx, 3 * cw), bf16)], pay, z1, z3)
-    r1, r3, r2lo, r2hi = ring(early, "x")
+    r1, r3 = from_axis(early, "x", 3), from_axis(early, "x", 1)
     (late,) = call(last_join_kernel, [like((rx, cw + 128), bf16)], pay, z1, z3, *z2)
     r24, r14, r34 = (from_axis(late, "x", k) for k in (2, 3, 1))
+    f1, f3, _ = lax.optimization_barrier((r1, r3, late))
+    r2lo, r2hi = from_axis(f1[:low], "x", 3), from_axis(f3[low:], "x", 1)
     wide, three, quarter = like((rows, width), f32), like((3 * rx, width), f32), like((rx, width), f32)
     my3, send3, acc = call(
         first_product_kernel,

time: 145 us -> 144 us (level)
  waiting for transfers between devices: 70 us -> 67.8 us
    ppermute x24, waiting for transfers between devices: 50.9 us -> 48.7 us  [from_axis(): return lax.ppermute(v, axis, [((i + k) % 4, i) for i in range(4)])]
  transfers between devices with their start and end apart: 34 -> 34, of which waited for: 19 -> 20; matrix products, arithmetic and copies ran while one was open for 0% -> 0% of each run, Pallas kernels for 6% -> 6%
where the time goes in v4:
time: 144 us
  waiting for transfers between devices  67.8 us (47%)
  starting transfers between devices  57.6 us (40%)
  Pallas kernels  15.9 us (11%)
    ppermute x24, waiting for transfers between devices, from_axis(): return lax.ppermute(v, axis, [((i + k) % 4, i) for i in range(4)])  48.7 us
    ppermute x24, starting transfers between devices, from_axis(): return lax.ppermute(v, axis, [((i + k) % 4, i) for i in range(4)])  38.3 us
    pallas_call x13, Pallas kernels, call(): pl.pallas_call(kernel, out_shape=outs, in_specs=[pl.BlockSpec(memory_spac...  15.9 us
    ppermute x9, starting transfers between devices, from_pair(): return lax.ppermute(v, axis, [(1, 0), (0, 1)])  15.8 us
    ppermute x9, waiting for transfers between devices, from_pair(): return lax.ppermute(v, axis, [(1, 0), (0, 1)])  13.4 us
    all_to_all x1, waiting for transfers between devices, per_device(): lax.all_to_all(sums, batch + ('core',), split_axis=0, concat_axis=0, tile...  5.72 us
    all_to_all x1, starting transfers between devices, per_device(): lax.all_to_all(sums, batch + ('core',), split_axis=0, concat_axis=0, tile...  3.54 us
  transfers between devices with their start and end apart: 34, of which 20 were waited for; matrix products, arithmetic and copies ran while one was open for 0% of the time, Pallas kernels for 6%

profile of v4, /device:TPU:1, one launch (start us, length us, event | category | flops | bytes accessed | tf_op | source)
XLA Modules:
  0.0 143.6 jit_solution(15866205471077172315)
XLA Ops:
  0.6 1.1 broadcast_select_fusion.1
  1.8 3.3 %collective-permute-start = (bf16[320,512]{1,0:T(8,128)(2,1)S(1)}, bf16[320,512]{1,0:T(8,128)(2,1)S(1)}, u32[]{:S(2)}, u32[]{:S(2)}) collective-permute-start(bf16[320,512]{1,0:T(8,128)(2,1)S(1)} %get-tuple-element.74), channel_id=1, source_target_pairs={{1,0},{0,1},{3,2},{2,3},{5,4},{4,5},{7,6},{6,7},{9,8},{8,9},{11,10... | collective-permute-start | bytes 983048 | tf_op jit(solution)/shard_map/ppermute | solution.py:26
  5.1 1.3 collective-permute-done
  6.3 0.1 pad_maximum_fusion.own
  6.4 0.1 collective-permute-start.3
  6.5 2.7 %collective-permute-start.2 = (bf16[320,1024]{1,0:T(8,128)(2,1)S(1)}, bf16[320,1024]{1,0:T(8,128)(2,1)S(1)}, u32[]{:S(2)}, u32[]{:S(2)}) collective-permute-start(bf16[320,1024]{1,0:T(8,128)(2,1)S(1)} %pad_maximum_fusion.own), channel_id=1, source_target_pairs={{64,0},{128,64},{192,128},{0,192},{65,1},{129,65},{193,129},{1,193... | collective-permute-start | bytes 1966088 | tf_op jit(solution)/shard_map/ppermute | solution.py:22
  9.2 0.0 collective-permute-start.1
  9.2 14.4 %collective-permute-done.3.refs_2_ = bf16[320,1024]{1,0:T(8,128)(2,1)S(1)} collective-permute-done((bf16[320,1024]{1,0:T(8,128)(2,1)S(1)}, bf16[320,1024]{1,0:T(8,128)(2,1)S(1)}, u32[]{:S(2)}, u32[]{:S(2)}) %collective-permute-start.3) | collective-permute-done | bytes 655392 | tf_op jit(solution)/shard_map/ppermute | solution.py:22
  23.7 0.1 collective-permute-start.5
  23.8 2.7 %collective-permute-start.4 = (bf16[160,1024]{1,0:T(8,128)(2,1)S(1)}, bf16[160,1024]{1,0:T(8,128)(2,1)S(1)}, u32[]{:S(2)}, u32[]{:S(2)}) collective-permute-start(bf16[160,1024]{1,0:T(8,128)(2,1)S(1)} %slice.28), channel_id=1, source_target_pairs={{64,0},{128,64},{192,128},{0,192},{65,1},{129,65},{193,129},{1,193... | collective-permute-start | bytes 983048 | tf_op jit(solution)/shard_map/ppermute | solution.py:22
  26.6 2.7 %collective-permute-start.6 = (bf16[320,1024]{1,0:T(8,128)(2,1)S(1)}, bf16[320,1024]{1,0:T(8,128)(2,1)S(1)}, u32[]{:S(2)}, u32[]{:S(2)}) collective-permute-start(bf16[320,1024]{1,0:T(8,128)(2,1)S(1)} %collective-permute-done.1.refs_0_), channel_id=1, source_target_pairs={{64,0},{128,64},{192,128},{0,192},{65,1},{129,65},{193,129},{1,193... | collective-permute-start | bytes 1966088 | tf_op jit(solution)/shard_map/ppermute | solution.py:22
  29.2 3.7 %collective-permute-done.5.refs_4_ = bf16[160,1024]{1,0:T(8,128)(2,1)S(1)} collective-permute-done((bf16[160,1024]{1,0:T(8,128)(2,1)S(1)}, bf16[160,1024]{1,0:T(8,128)(2,1)S(1)}, u32[]{:S(2)}, u32[]{:S(2)}) %collective-permute-start.5) | collective-permute-done | bytes 327712 | tf_op jit(solution)/shard_map/ppermute | solution.py:22
  33.0 0.1 collective-permute-start.9
  33.1 1.4 collective-permute-start.8
  34.4 1.8 %shard_map.49 = (f32[24,1024]{1,0:T(8,128)S(1)}, bf16[1600,1024]{1,0:T(8,128)(2,1)S(1)}) custom-call(bf16[320,1024]{1,0:T(8,128)(2,1)S(1)} %pad_maximum_fusion.own, bf16[320,1024]{1,0:T(8,128)(2,1)S(1)} %collective-permute-done.1.refs_0_, bf16[320,1024]{1,0:T(8,128)(2,1)S(1)} %collective-permute-done.2.refs_1_, ...), custom_call_target="tpu_custom_call" | custom-call | tf_op jit(solution)/shard_map/pallas_call | solution.py:298
  36.3 2.9 %collective-permute-done.9.refs_3_ = bf16[160,1024]{1,0:T(8,128)(2,1)S(1)} collective-permute-done((bf16[160,1024]{1,0:T(8,128)(2,1)S(1)}, bf16[160,1024]{1,0:T(8,128)(2,1)S(1)}, u32[]{:S(2)}, u32[]{:S(2)}) %collective-permute-start.9) | collective-permute-done | bytes 327712 | tf_op jit(solution)/shard_map/ppermute | solution.py:26
  39.2 6.2 %collective-permute-done.8.refs_2_ = bf16[160,1024]{1,0:T(8,128)(2,1)S(1)} collective-permute-done((bf16[160,1024]{1,0:T(8,128)(2,1)S(1)}, bf16[160,1024]{1,0:T(8,128)(2,1)S(1)}, u32[]{:S(2)}, u32[]{:S(2)}) %collective-permute-start.8) | collective-permute-done | bytes 327712 | tf_op jit(solution)/shard_map/ppermute | solution.py:26
  45.4 1.7 %collective-permute-done.7.refs_1_ = bf16[320,1024]{1,0:T(8,128)(2,1)S(1)} collective-permute-done((bf16[320,1024]{1,0:T(8,128)(2,1)S(1)}, bf16[320,1024]{1,0:T(8,128)(2,1)S(1)}, u32[]{:S(2)}, u32[]{:S(2)}) %collective-permute-start.7) | collective-permute-done | bytes 655392 | tf_op jit(solution)/shard_map/ppermute | solution.py:22
  47.0 4.6 %shard_map.50 = (bf16[2560,1024]{1,0:T(8,128)(2,1)S(1)}, bf16[2560,512]{1,0:T(8,128)(2,1)S(1)}, f32[8,1024]{1,0:T(8,128)S(1)}, bf16[48,2560]{1,0:T(8,128)(2,1)S(1)}, bf16[32,2560]{1,0:T(8,128)(2,1)S(1)}) custom-call(f32[24,1024]{1,0:T(8,128)S(1)} %get-tuple-element.38.st, bf16[1600,1024]{1,0:T(8,128)(2,1)S(1)} %get-tuple-element.39.known, ...), custom_call_target="tpu_custom_call" | custom-call | tf_op jit(solution)/shard_map/pallas_call | solution.py:298
  51.6 0.1 collective-permute-start.10
  51.7 2.7 %collective-permute-start.11 = (bf16[32,2560]{1,0:T(8,128)(2,1)S(1)}, bf16[32,2560]{1,0:T(8,128)(2,1)S(1)}, u32[]{:S(2)}, u32[]{:S(2)}) collective-permute-start(bf16[32,2560]{1,0:T(8,128)(2,1)S(1)} %get-tuple-element.45), channel_id=1, source_target_pairs={{8,0},{16,8},{24,16},{0,24},{9,1},{17,9},{25,17},{1,25},{10,2},{18... | collective-permute-start | bytes 491528 | tf_op jit(solution)/shard_map/ppermute | solution.py:22
  54.4 2.4 %shard_map.51 = (bf16[80,2560]{1,0:T(8,128)(2,1)S(1)}, bf16[80,2560]{1,0:T(8,128)(2,1)S(1)}, bf16[80,2560]{1,0:T(8,128)(2,1)S(1)}) custom-call(bf16[2560,1024]{1,0:T(8,128)(2,1)S(1)} %get-tuple-element.40.n), custom_call_target="tpu_custom_call" | custom-call | tf_op jit(solution)/shard_map/pallas_call | solution.py:298
  56.8 1.2 collective-permute-done.10.a
  58.0 0.1 shard_map.52
  58.1 0.1 collective-permute-start.12
  58.2 2.7 %collective-permute-start.13 = (bf16[80,2560]{1,0:T(8,128)(2,1)S(1)}, bf16[80,2560]{1,0:T(8,128)(2,1)S(1)}, u32[]{:S(2)}, u32[]{:S(2)}) collective-permute-start(bf16[80,2560]{1,0:T(8,128)(2,1)S(1)} %get-tuple-element.47), channel_id=1, source_target_pairs={{8,0},{16,8},{24,16},{0,24},{9,1},{17,9},{25,17},{1,25},{10,2},{18... | collective-permute-start | bytes 1228808 | tf_op jit(solution)/shard_map/ppermute | solution.py:22
  60.8 5.3 %collective-permute-done.12.e = bf16[80,2560]{1,0:T(8,128)(2,1)S(1)} collective-permute-done((bf16[80,2560]{1,0:T(8,128)(2,1)S(1)}, bf16[80,2560]{1,0:T(8,128)(2,1)S(1)}, u32[]{:S(2)}, u32[]{:S(2)}) %collective-permute-start.12) | collective-permute-done | bytes 409632 | tf_op jit(solution)/shard_map/ppermute | solution.py:22
  66.2 0.2 shard_map.53
  66.4 5.5 %collective-permute-start.14 = (bf16[2560,512]{1,0:T(8,128)(2,1)S(1)}, bf16[2560,512]{1,0:T(8,128)(2,1)S(1)}, u32[]{:S(2)}, u32[]{:S(2)}) collective-permute-start(bf16[2560,512]{1,0:T(8,128)(2,1)S(1)} %get-tuple-element.52), channel_id=1, source_target_pairs={{1,0},{0,1},{3,2},{2,3},{5,4},{4,5},{7,6},{6,7},{9,8},{8,9},{11,10... | collective-permute-start | bytes 7864328 | tf_op jit(solution)/shard_map/ppermute | solution.py:26
  71.9 1.8 %collective-permute-start.17 = (bf16[80,640]{1,0:T(8,128)(2,1)S(1)}, bf16[80,640]{1,0:T(8,128)(2,1)S(1)}, u32[]{:S(2)}, u32[]{:S(2)}) collective-permute-start(bf16[80,640]{1,0:T(8,128)(2,1)S(1)} %get-tuple-element.57), channel_id=1, source_target_pairs={{6,0},{0,2},{2,4},{4,6},{7,1},{1,3},{3,5},{5,7},{14,8},{8,10},{10,... | collective-permute-start | bytes 307208 | tf_op jit(solution)/shard_map/ppermute | solution.py:22
  73.7 4.8 %collective-permute-start.16 = (bf16[80,640]{1,0:T(8,128)(2,1)S(1)}, bf16[80,640]{1,0:T(8,128)(2,1)S(1)}, u32[]{:S(2)}, u32[]{:S(2)}) collective-permute-start(bf16[80,640]{1,0:T(8,128)(2,1)S(1)} %get-tuple-element.56), channel_id=1, source_target_pairs={{4,0},{6,2},{0,4},{2,6},{5,1},{7,3},{1,5},{3,7},{12,8},{14,10},{8,... | collective-permute-start | bytes 307208 | tf_op jit(solution)/shard_map/ppermute | solution.py:22
  78.5 2.4 %collective-permute-start.18 = (bf16[80,640]{1,0:T(8,128)(2,1)S(1)}, bf16[80,640]{1,0:T(8,128)(2,1)S(1)}, u32[]{:S(2)}, u32[]{:S(2)}) collective-permute-start(bf16[80,640]{1,0:T(8,128)(2,1)S(1)} %get-tuple-element.58), channel_id=1, source_target_pairs={{2,0},{4,2},{6,4},{0,6},{3,1},{5,3},{7,5},{1,7},{10,8},{12,10},{14... | collective-permute-start | bytes 307208 | tf_op jit(solution)/shard_map/ppermute | solution.py:22
  80.9 0.9 collective-permute-start.15
  81.8 0.8 collective-permute-done.15.inv_o
  82.6 1.1 shard_map.54
  83.7 2.1 %collective-permute-done.16.r1 = bf16[80,640]{1,0:T(8,128)(2,1)S(1)} collective-permute-done((bf16[80,640]{1,0:T(8,128)(2,1)S(1)}, bf16[80,640]{1,0:T(8,128)(2,1)S(1)}, u32[]{:S(2)}, u32[]{:S(2)}) %collective-permute-start.16) | collective-permute-done | bytes 102432 | tf_op jit(solution)/shard_map/ppermute | solution.py:22
  85.9 3.0 %collective-permute-done.18.r3 = bf16[80,640]{1,0:T(8,128)(2,1)S(1)} collective-permute-done((bf16[80,640]{1,0:T(8,128)(2,1)S(1)}, bf16[80,640]{1,0:T(8,128)(2,1)S(1)}, u32[]{:S(2)}, u32[]{:S(2)}) %collective-permute-start.18) | collective-permute-done | bytes 102432 | tf_op jit(solution)/shard_map/ppermute | solution.py:22
  88.8 0.1 shard_map.55.mine
  88.9 0.6 collective-permute-start.19
  89.5 0.9 collective-permute-done.19.theirs
  90.4 0.1 shard_map.56.own
  90.6 3.4 %collective-permute-start.21 = (bf16[80,768]{1,0:T(8,128)(2,1)S(1)}, bf16[80,768]{1,0:T(8,128)(2,1)S(1)}, u32[]{:S(2)}, u32[]{:S(2)}) collective-permute-start(bf16[80,768]{1,0:T(8,128)(2,1)S(1)} %shard_map.56.own), channel_id=1, source_target_pairs={{2,0},{4,2},{6,4},{0,6},{3,1},{5,3},{7,5},{1,7},{10,8},{12,10},{14... | collective-permute-start | bytes 368648 | tf_op jit(solution)/shard_map/ppermute | solution.py:22
  94.0 4.7 %collective-permute-done.21.r3 = bf16[80,768]{1,0:T(8,128)(2,1)S(1)} collective-permute-done((bf16[80,768]{1,0:T(8,128)(2,1)S(1)}, bf16[80,768]{1,0:T(8,128)(2,1)S(1)}, u32[]{:S(2)}, u32[]{:S(2)}) %collective-permute-start.21) | collective-permute-done | bytes 122912 | tf_op jit(solution)/shard_map/ppermute | solution.py:22
  98.6 2.6 %collective-permute-done.20.r1 = bf16[80,768]{1,0:T(8,128)(2,1)S(1)} collective-permute-done((bf16[80,768]{1,0:T(8,128)(2,1)S(1)}, bf16[80,768]{1,0:T(8,128)(2,1)S(1)}, u32[]{:S(2)}, u32[]{:S(2)}) %collective-permute-start.20) | collective-permute-done | bytes 122912 | tf_op jit(solution)/shard_map/ppermute | solution.py:22
  101.2 3.0 %collective-permute-start.23 = (bf16[80,1920]{1,0:T(8,128)(2,1)S(1)}, bf16[80,1920]{1,0:T(8,128)(2,1)S(1)}, u32[]{:S(2)}, u32[]{:S(2)}) collective-permute-start(bf16[80,1920]{1,0:T(8,128)(2,1)S(1)} %shard_map.57.own), channel_id=1, source_target_pairs={{8,0},{16,8},{24,16},{0,24},{9,1},{17,9},{25,17},{1,25},{10,2},{18... | collective-permute-start | bytes 921608 | tf_op jit(solution)/shard_map/ppermute | solution.py:22
  104.3 0.9 collective-permute-start.24
  105.2 2.7 %collective-permute-start.25 = (bf16[32,768]{1,0:T(8,128)(2,1)S(1)}, bf16[32,768]{1,0:T(8,128)(2,1)S(1)}, u32[]{:S(2)}, u32[]{:S(2)}) collective-permute-start(bf16[32,768]{1,0:T(8,128)(2,1)S(1)} %slice.31), channel_id=1, source_target_pairs={{2,0},{4,2},{6,4},{0,6},{3,1},{5,3},{7,5},{1,7},{10,8},{12,10},{14... | collective-permute-start | bytes 147464 | tf_op jit(solution)/shard_map/ppermute | solution.py:22
  107.9 1.6 %collective-permute-done.25.r2hi = bf16[32,768]{1,0:T(8,128)(2,1)S(1)} collective-permute-done((bf16[32,768]{1,0:T(8,128)(2,1)S(1)}, bf16[32,768]{1,0:T(8,128)(2,1)S(1)}, u32[]{:S(2)}, u32[]{:S(2)}) %collective-permute-start.25) | collective-permute-done | bytes 49184 | tf_op jit(solution)/shard_map/ppermute | solution.py:22
  109.6 0.7 collective-permute-done.24.r2lo
  110.2 0.1 shard_map.58.own4
  110.3 2.6 %collective-permute-done.22.r1 = bf16[80,1920]{1,0:T(8,128)(2,1)S(1)} collective-permute-done((bf16[80,1920]{1,0:T(8,128)(2,1)S(1)}, bf16[80,1920]{1,0:T(8,128)(2,1)S(1)}, u32[]{:S(2)}, u32[]{:S(2)}) %collective-permute-start.22) | collective-permute-done | bytes 307232 | tf_op jit(solution)/shard_map/ppermute | solution.py:22
  112.9 0.1 collective-permute-start.28
  113.0 2.7 %collective-permute-start.27 = (bf16[80,768]{1,0:T(8,128)(2,1)S(1)}, bf16[80,768]{1,0:T(8,128)(2,1)S(1)}, u32[]{:S(2)}, u32[]{:S(2)}) collective-permute-start(bf16[80,768]{1,0:T(8,128)(2,1)S(1)} %shard_map.58.own4), channel_id=1, source_target_pairs={{8,0},{16,8},{24,16},{0,24},{9,1},{17,9},{25,17},{1,25},{10,2},{18... | collective-permute-start | bytes 368648 | tf_op jit(solution)/shard_map/ppermute | solution.py:22
  115.7 1.2 collective-permute-start.30
  116.9 1.6 %collective-permute-start.29 = (bf16[32,1920]{1,0:T(8,128)(2,1)S(1)}, bf16[32,1920]{1,0:T(8,128)(2,1)S(1)}, u32[]{:S(2)}, u32[]{:S(2)}) collective-permute-start(bf16[32,1920]{1,0:T(8,128)(2,1)S(1)} %slice.27), channel_id=1, source_target_pairs={{8,0},{16,8},{24,16},{0,24},{9,1},{17,9},{25,17},{1,25},{10,2},{18... | collective-permute-start | bytes 368648 | tf_op jit(solution)/shard_map/ppermute | solution.py:22
  118.5 5.1 %collective-permute-done.26.r14 = bf16[80,768]{1,0:T(8,128)(2,1)S(1)} collective-permute-done((bf16[80,768]{1,0:T(8,128)(2,1)S(1)}, bf16[80,768]{1,0:T(8,128)(2,1)S(1)}, u32[]{:S(2)}, u32[]{:S(2)}) %collective-permute-start.26) | collective-permute-done | bytes 122912 | tf_op jit(solution)/shard_map/ppermute | solution.py:22
  123.5 1.8 %shard_map.59 = (f32[240,512]{1,0:T(8,128)S(1)}, f32[240,512]{1,0:T(8,128)S(1)}, f32[8,1024]{1,0:T(8,128)S(1)}) custom-call(bf16[80,1920]{1,0:T(8,128)(2,1)S(1)} %shard_map.57.own, bf16[80,1920]{1,0:T(8,128)(2,1)S(1)} %collective-permute-done.22.r1, bf16[80,1920]{1,0:T(8,128)(2,1)S(1)} %collective-permute-done.23.r3, bf16[80,768]{1,0:T(8,128)(2,1)S(1)} %shard_map.58.own4, ...), custom_call_target="tpu_custom_call" | custom-call | tf_op jit(solution)/shard_map/pallas_call | solution.py:298
  125.3 3.8 %collective-permute-start.31 = (f32[240,512]{1,0:T(8,128)S(1)}, f32[240,512]{1,0:T(8,128)S(1)}, u32[]{:S(2)}, u32[]{:S(2)}) collective-permute-start(f32[240,512]{1,0:T(8,128)S(1)} %get-tuple-element.64), channel_id=1, source_target_pairs={{1,0},{0,1},{3,2},{2,3},{5,4},{4,5},{7,6},{6,7},{9,8},{8,9},{11,10... | collective-permute-start | bytes 1474568 | tf_op jit(solution)/shard_map/ppermute | solution.py:26
  129.1 1.8 %shard_map.60 = (f32[80,512]{1,0:T(8,128)S(1)}, f32[80,512]{1,0:T(8,128)S(1)}, f32[16,8,512]{2,1,0:T(8,128)}) custom-call(bf16[48,1920]{1,0:T(8,128)(2,1)S(1)} %collective-permute-done.28.r2lo, bf16[32,1920]{1,0:T(8,128)(2,1)S(1)} %collective-permute-done.29.r2hi, bf16[80,768]{1,0:T(8,128)(2,1)S(1)} %collective-permute-done.30.r24, ...), custom_call_target="tpu_custom_call" | custom-call | tf_op jit(solution)/shard_map/pallas_call | solution.py:298
  131.0 3.5 %all-to-all-start = ((f32[16,8,512]{2,1,0:T(8,128)}), f32[16,8,512]{2,1,0:T(8,128)S(1)}, u32[]{:S(2)}, u32[]{:S(2)}) async-start(f32[16,8,512]{2,1,0:T(8,128)} %get-tuple-element.68), calls=%async_computation | async-start | bytes 524288 | tf_op jit(solution)/shard_map/all_to_all | solution.py:389
  134.5 0.2 collective-permute-start.32
  134.7 1.3 collective-permute-done.32.other1
  136.0 5.7 %all-to-all-done.sums = f32[16,8,512]{2,1,0:T(8,128)S(1)} async-done(((f32[16,8,512]{2,1,0:T(8,128)}), f32[16,8,512]{2,1,0:T(8,128)S(1)}, u32[]{:S(2)}, u32[]{:S(2)}) %all-to-all-start) | async-done | bytes 262176 | tf_op jit(solution)/shard_map/all_to_all | solution.py:389
  141.7 1.7 %shard_map.61 = (f32[1,1]{1,0:T(1,128)}, f32[320,512]{1,0:T(8,128)}, f32[320,512]{1,0:T(8,128)}) custom-call(f32[240,512]{1,0:T(8,128)S(1)} %get-tuple-element.59.my3, f32[80,512]{1,0:T(8,128)S(1)} %get-tuple-element.63.my1, f32[240,512]{1,0:T(8,128)S(1)} %collective-permute-done.31.other3, f32[80,512]{1,0:T(8,128)S(1)} %collective-permute-done.32.other1, ...), custom_call_target="tpu_custom_call" | custom-call | tf_op jit(solution)/shard_map/pallas_call | solution.py:298
  (26 shorter events, 0.2 us)
Async XLA Ops:
  1.8 4.6 %collective-permute-start = (bf16[320,512]{1,0:T(8,128)(2,1)S(1)}, bf16[320,512]{1,0:T(8,128)(2,1)S(1)}, u32[]{:S(2)}, u32[]{:S(2)}) collective-permute-start(bf16[320,512]{1,0:T(8,128)(2,1)S(1)} %get-tuple-element.74), channel_id=1, source_target_pairs={{1,0},{0,1},{3,2},{2,3},{5,4},{4,5},{7,6},{6,7},{9,8},{8,9},{11,10... | collective-permute-start | bytes 983048 | tf_op jit(solution)/shard_map/ppermute | solution.py:26
  6.4 17.2 %collective-permute-start.3 = (bf16[320,1024]{1,0:T(8,128)(2,1)S(1)}, bf16[320,1024]{1,0:T(8,128)(2,1)S(1)}, u32[]{:S(2)}, u32[]{:S(2)}) collective-permute-start(bf16[320,1024]{1,0:T(8,128)(2,1)S(1)} %pad_maximum_fusion.own), channel_id=1, source_target_pairs={{192,0},{0,64},{64,128},{128,192},{193,1},{1,65},{65,129},{129,193... | collective-permute-start | bytes 1966088 | tf_op jit(solution)/shard_map/ppermute | solution.py:22
  6.5 17.3 %collective-permute-start.2 = (bf16[320,1024]{1,0:T(8,128)(2,1)S(1)}, bf16[320,1024]{1,0:T(8,128)(2,1)S(1)}, u32[]{:S(2)}, u32[]{:S(2)}) collective-permute-start(bf16[320,1024]{1,0:T(8,128)(2,1)S(1)} %pad_maximum_fusion.own), channel_id=1, source_target_pairs={{64,0},{128,64},{192,128},{0,192},{65,1},{129,65},{193,129},{1,193... | collective-permute-start | bytes 1966088 | tf_op jit(solution)/shard_map/ppermute | solution.py:22
  9.2 17.4 %collective-permute-start.1 = (bf16[320,1024]{1,0:T(8,128)(2,1)S(1)}, bf16[320,1024]{1,0:T(8,128)(2,1)S(1)}, u32[]{:S(2)}, u32[]{:S(2)}) collective-permute-start(bf16[320,1024]{1,0:T(8,128)(2,1)S(1)} %pad_maximum_fusion.own), channel_id=1, source_target_pairs={{32,0},{0,32},{33,1},{1,33},{34,2},{2,34},{35,3},{3,35},{36,4},{4,... | collective-permute-start | bytes 1966088 | tf_op jit(solution)/shard_map/ppermute | solution.py:26
  23.7 9.3 %collective-permute-start.5 = (bf16[160,1024]{1,0:T(8,128)(2,1)S(1)}, bf16[160,1024]{1,0:T(8,128)(2,1)S(1)}, u32[]{:S(2)}, u32[]{:S(2)}) collective-permute-start(bf16[160,1024]{1,0:T(8,128)(2,1)S(1)} %slice.29), channel_id=1, source_target_pairs={{192,0},{0,64},{64,128},{128,192},{193,1},{1,65},{65,129},{129,193... | collective-permute-start | bytes 983048 | tf_op jit(solution)/shard_map/ppermute | solution.py:22
  23.8 9.3 %collective-permute-start.4 = (bf16[160,1024]{1,0:T(8,128)(2,1)S(1)}, bf16[160,1024]{1,0:T(8,128)(2,1)S(1)}, u32[]{:S(2)}, u32[]{:S(2)}) collective-permute-start(bf16[160,1024]{1,0:T(8,128)(2,1)S(1)} %slice.28), channel_id=1, source_target_pairs={{64,0},{128,64},{192,128},{0,192},{65,1},{129,65},{193,129},{1,193... | collective-permute-start | bytes 983048 | tf_op jit(solution)/shard_map/ppermute | solution.py:22
  26.5 20.5 %collective-permute-start.7 = (bf16[320,1024]{1,0:T(8,128)(2,1)S(1)}, bf16[320,1024]{1,0:T(8,128)(2,1)S(1)}, u32[]{:S(2)}, u32[]{:S(2)}) collective-permute-start(bf16[320,1024]{1,0:T(8,128)(2,1)S(1)} %collective-permute-done.1.refs_0_), channel_id=1, source_target_pairs={{192,0},{0,64},{64,128},{128,192},{193,1},{1,65},{65,129},{129,193... | collective-permute-start | bytes 1966088 | tf_op jit(solution)/shard_map/ppermute | solution.py:22
  26.6 20.5 %collective-permute-start.6 = (bf16[320,1024]{1,0:T(8,128)(2,1)S(1)}, bf16[320,1024]{1,0:T(8,128)(2,1)S(1)}, u32[]{:S(2)}, u32[]{:S(2)}) collective-permute-start(bf16[320,1024]{1,0:T(8,128)(2,1)S(1)} %collective-permute-done.1.refs_0_), channel_id=1, source_target_pairs={{64,0},{128,64},{192,128},{0,192},{65,1},{129,65},{193,129},{1,193... | collective-permute-start | bytes 1966088 | tf_op jit(solution)/shard_map/ppermute | solution.py:22
  33.0 6.2 %collective-permute-start.9 = (bf16[160,1024]{1,0:T(8,128)(2,1)S(1)}, bf16[160,1024]{1,0:T(8,128)(2,1)S(1)}, u32[]{:S(2)}, u32[]{:S(2)}) collective-permute-start(bf16[160,1024]{1,0:T(8,128)(2,1)S(1)} %collective-permute-done.5.refs_4_), channel_id=1, source_target_pairs={{32,0},{0,32},{33,1},{1,33},{34,2},{2,34},{35,3},{3,35},{36,4},{4,... | collective-permute-start | bytes 983048 | tf_op jit(solution)/shard_map/ppermute | solution.py:26
  33.1 12.3 %collective-permute-start.8 = (bf16[160,1024]{1,0:T(8,128)(2,1)S(1)}, bf16[160,1024]{1,0:T(8,128)(2,1)S(1)}, u32[]{:S(2)}, u32[]{:S(2)}) collective-permute-start(bf16[160,1024]{1,0:T(8,128)(2,1)S(1)} %collective-permute-done.4.refs_3_), channel_id=1, source_target_pairs={{32,0},{0,32},{33,1},{1,33},{34,2},{2,34},{35,3},{3,35},{36,4},{4,... | collective-permute-start | bytes 983048 | tf_op jit(solution)/shard_map/ppermute | solution.py:26
  51.6 6.3 %collective-permute-start.10 = (bf16[48,2560]{1,0:T(8,128)(2,1)S(1)}, bf16[48,2560]{1,0:T(8,128)(2,1)S(1)}, u32[]{:S(2)}, u32[]{:S(2)}) collective-permute-start(bf16[48,2560]{1,0:T(8,128)(2,1)S(1)} %get-tuple-element.43), channel_id=1, source_target_pairs={{24,0},{0,8},{8,16},{16,24},{25,1},{1,9},{9,17},{17,25},{26,2},{2,... | collective-permute-start | bytes 737288 | tf_op jit(solution)/shard_map/ppermute | solution.py:22
  51.7 5.0 %collective-permute-start.11 = (bf16[32,2560]{1,0:T(8,128)(2,1)S(1)}, bf16[32,2560]{1,0:T(8,128)(2,1)S(1)}, u32[]{:S(2)}, u32[]{:S(2)}) collective-permute-start(bf16[32,2560]{1,0:T(8,128)(2,1)S(1)} %get-tuple-element.45), channel_id=1, source_target_pairs={{8,0},{16,8},{24,16},{0,24},{9,1},{17,9},{25,17},{1,25},{10,2},{18... | collective-permute-start | bytes 491528 | tf_op jit(solution)/shard_map/ppermute | solution.py:22
  58.1 8.1 %collective-permute-start.12 = (bf16[80,2560]{1,0:T(8,128)(2,1)S(1)}, bf16[80,2560]{1,0:T(8,128)(2,1)S(1)}, u32[]{:S(2)}, u32[]{:S(2)}) collective-permute-start(bf16[80,2560]{1,0:T(8,128)(2,1)S(1)} %get-tuple-element.46), channel_id=1, source_target_pairs={{24,0},{0,8},{8,16},{16,24},{25,1},{1,9},{9,17},{17,25},{26,2},{2,... | collective-permute-start | bytes 1228808 | tf_op jit(solution)/shard_map/ppermute | solution.py:22
  58.2 8.0 %collective-permute-start.13 = (bf16[80,2560]{1,0:T(8,128)(2,1)S(1)}, bf16[80,2560]{1,0:T(8,128)(2,1)S(1)}, u32[]{:S(2)}, u32[]{:S(2)}) collective-permute-start(bf16[80,2560]{1,0:T(8,128)(2,1)S(1)} %get-tuple-element.47), channel_id=1, source_target_pairs={{8,0},{16,8},{24,16},{0,24},{9,1},{17,9},{25,17},{1,25},{10,2},{18... | collective-permute-start | bytes 1228808 | tf_op jit(solution)/shard_map/ppermute | solution.py:22
  66.4 16.2 %collective-permute-start.14 = (bf16[2560,512]{1,0:T(8,128)(2,1)S(1)}, bf16[2560,512]{1,0:T(8,128)(2,1)S(1)}, u32[]{:S(2)}, u32[]{:S(2)}) collective-permute-start(bf16[2560,512]{1,0:T(8,128)(2,1)S(1)} %get-tuple-element.52), channel_id=1, source_target_pairs={{1,0},{0,1},{3,2},{2,3},{5,4},{4,5},{7,6},{6,7},{9,8},{8,9},{11,10... | collective-permute-start | bytes 7864328 | tf_op jit(solution)/shard_map/ppermute | solution.py:26
  71.9 11.8 %collective-permute-start.17 = (bf16[80,640]{1,0:T(8,128)(2,1)S(1)}, bf16[80,640]{1,0:T(8,128)(2,1)S(1)}, u32[]{:S(2)}, u32[]{:S(2)}) collective-permute-start(bf16[80,640]{1,0:T(8,128)(2,1)S(1)} %get-tuple-element.57), channel_id=1, source_target_pairs={{6,0},{0,2},{2,4},{4,6},{7,1},{1,3},{3,5},{5,7},{14,8},{8,10},{10,... | collective-permute-start | bytes 307208 | tf_op jit(solution)/shard_map/ppermute | solution.py:22
  73.7 12.2 %collective-permute-start.16 = (bf16[80,640]{1,0:T(8,128)(2,1)S(1)}, bf16[80,640]{1,0:T(8,128)(2,1)S(1)}, u32[]{:S(2)}, u32[]{:S(2)}) collective-permute-start(bf16[80,640]{1,0:T(8,128)(2,1)S(1)} %get-tuple-element.56), channel_id=1, source_target_pairs={{4,0},{6,2},{0,4},{2,6},{5,1},{7,3},{1,5},{3,7},{12,8},{14,10},{8,... | collective-permute-start | bytes 307208 | tf_op jit(solution)/shard_map/ppermute | solution.py:22
  78.5 10.4 %collective-permute-start.18 = (bf16[80,640]{1,0:T(8,128)(2,1)S(1)}, bf16[80,640]{1,0:T(8,128)(2,1)S(1)}, u32[]{:S(2)}, u32[]{:S(2)}) collective-permute-start(bf16[80,640]{1,0:T(8,128)(2,1)S(1)} %get-tuple-element.58), channel_id=1, source_target_pairs={{2,0},{4,2},{6,4},{0,6},{3,1},{5,3},{7,5},{1,7},{10,8},{12,10},{14... | collective-permute-start | bytes 307208 | tf_op jit(solution)/shard_map/ppermute | solution.py:22
  80.9 1.8 %collective-permute-start.15 = (f32[8,512]{1,0:T(8,128)S(1)}, f32[8,512]{1,0:T(8,128)S(1)}, u32[]{:S(2)}, u32[]{:S(2)}) collective-permute-start(f32[8,512]{1,0:T(8,128)S(1)} %slice.23), channel_id=1, source_target_pairs={{1,0},{0,1},{3,2},{2,3},{5,4},{4,5},{7,6},{6,7},{9,8},{8,9},{11,10... | collective-permute-start | bytes 49160 | tf_op jit(solution)/shard_map/ppermute | solution.py:26
  88.9 1.5 %collective-permute-start.19 = (bf16[80,640]{1,0:T(8,128)(2,1)S(1)}, bf16[80,640]{1,0:T(8,128)(2,1)S(1)}, u32[]{:S(2)}, u32[]{:S(2)}) collective-permute-start(bf16[80,640]{1,0:T(8,128)(2,1)S(1)} %shard_map.55.mine), channel_id=1, source_target_pairs={{1,0},{0,1},{3,2},{2,3},{5,4},{4,5},{7,6},{6,7},{9,8},{8,9},{11,10... | collective-permute-start | bytes 307208 | tf_op jit(solution)/shard_map/ppermute | solution.py:26
  90.6 8.1 %collective-permute-start.21 = (bf16[80,768]{1,0:T(8,128)(2,1)S(1)}, bf16[80,768]{1,0:T(8,128)(2,1)S(1)}, u32[]{:S(2)}, u32[]{:S(2)}) collective-permute-start(bf16[80,768]{1,0:T(8,128)(2,1)S(1)} %shard_map.56.own), channel_id=1, source_target_pairs={{2,0},{4,2},{6,4},{0,6},{3,1},{5,3},{7,5},{1,7},{10,8},{12,10},{14... | collective-permute-start | bytes 368648 | tf_op jit(solution)/shard_map/ppermute | solution.py:22
  93.9 7.3 %collective-permute-start.20 = (bf16[80,768]{1,0:T(8,128)(2,1)S(1)}, bf16[80,768]{1,0:T(8,128)(2,1)S(1)}, u32[]{:S(2)}, u32[]{:S(2)}) collective-permute-start(bf16[80,768]{1,0:T(8,128)(2,1)S(1)} %shard_map.56.own), channel_id=1, source_target_pairs={{6,0},{0,2},{2,4},{4,6},{7,1},{1,3},{3,5},{5,7},{14,8},{8,10},{10,... | collective-permute-start | bytes 368648 | tf_op jit(solution)/shard_map/ppermute | solution.py:22
  101.2 9.1 %collective-permute-start.23 = (bf16[80,1920]{1,0:T(8,128)(2,1)S(1)}, bf16[80,1920]{1,0:T(8,128)(2,1)S(1)}, u32[]{:S(2)}, u32[]{:S(2)}) collective-permute-start(bf16[80,1920]{1,0:T(8,128)(2,1)S(1)} %shard_map.57.own), channel_id=1, source_target_pairs={{8,0},{16,8},{24,16},{0,24},{9,1},{17,9},{25,17},{1,25},{10,2},{18... | collective-permute-start | bytes 921608 | tf_op jit(solution)/shard_map/ppermute | solution.py:22
  104.3 8.6 %collective-permute-start.22 = (bf16[80,1920]{1,0:T(8,128)(2,1)S(1)}, bf16[80,1920]{1,0:T(8,128)(2,1)S(1)}, u32[]{:S(2)}, u32[]{:S(2)}) collective-permute-start(bf16[80,1920]{1,0:T(8,128)(2,1)S(1)} %shard_map.57.own), channel_id=1, source_target_pairs={{24,0},{0,8},{8,16},{16,24},{25,1},{1,9},{9,17},{17,25},{26,2},{2,... | collective-permute-start | bytes 921608 | tf_op jit(solution)/shard_map/ppermute | solution.py:22
  104.3 5.9 %collective-permute-start.24 = (bf16[48,768]{1,0:T(8,128)(2,1)S(1)}, bf16[48,768]{1,0:T(8,128)(2,1)S(1)}, u32[]{:S(2)}, u32[]{:S(2)}) collective-permute-start(bf16[48,768]{1,0:T(8,128)(2,1)S(1)} %slice.30), channel_id=1, source_target_pairs={{6,0},{0,2},{2,4},{4,6},{7,1},{1,3},{3,5},{5,7},{14,8},{8,10},{10,... | collective-permute-start | bytes 221192 | tf_op jit(solution)/shard_map/ppermute | solution.py:22
  105.2 4.4 %collective-permute-start.25 = (bf16[32,768]{1,0:T(8,128)(2,1)S(1)}, bf16[32,768]{1,0:T(8,128)(2,1)S(1)}, u32[]{:S(2)}, u32[]{:S(2)}) collective-permute-start(bf16[32,768]{1,0:T(8,128)(2,1)S(1)} %slice.31), channel_id=1, source_target_pairs={{2,0},{4,2},{6,4},{0,6},{3,1},{5,3},{7,5},{1,7},{10,8},{12,10},{14... | collective-permute-start | bytes 147464 | tf_op jit(solution)/shard_map/ppermute | solution.py:22
  112.9 16.2 %collective-permute-start.28 = (bf16[48,1920]{1,0:T(8,128)(2,1)S(1)}, bf16[48,1920]{1,0:T(8,128)(2,1)S(1)}, u32[]{:S(2)}, u32[]{:S(2)}) collective-permute-start(bf16[48,1920]{1,0:T(8,128)(2,1)S(1)} %slice.26), channel_id=1, source_target_pairs={{24,0},{0,8},{8,16},{16,24},{25,1},{1,9},{9,17},{17,25},{26,2},{2,... | collective-permute-start | bytes 552968 | tf_op jit(solution)/shard_map/ppermute | solution.py:22
  113.0 5.4 %collective-permute-start.27 = (bf16[80,768]{1,0:T(8,128)(2,1)S(1)}, bf16[80,768]{1,0:T(8,128)(2,1)S(1)}, u32[]{:S(2)}, u32[]{:S(2)}) collective-permute-start(bf16[80,768]{1,0:T(8,128)(2,1)S(1)} %shard_map.58.own4), channel_id=1, source_target_pairs={{8,0},{16,8},{24,16},{0,24},{9,1},{17,9},{25,17},{1,25},{10,2},{18... | collective-permute-start | bytes 368648 | tf_op jit(solution)/shard_map/ppermute | solution.py:22
  115.7 7.8 %collective-permute-start.26 = (bf16[80,768]{1,0:T(8,128)(2,1)S(1)}, bf16[80,768]{1,0:T(8,128)(2,1)S(1)}, u32[]{:S(2)}, u32[]{:S(2)}) collective-permute-start(bf16[80,768]{1,0:T(8,128)(2,1)S(1)} %shard_map.58.own4), channel_id=1, source_target_pairs={{24,0},{0,8},{8,16},{16,24},{25,1},{1,9},{9,17},{17,25},{26,2},{2,... | collective-permute-start | bytes 368648 | tf_op jit(solution)/shard_map/ppermute | solution.py:22
  115.7 13.4 %collective-permute-start.30 = (bf16[80,768]{1,0:T(8,128)(2,1)S(1)}, bf16[80,768]{1,0:T(8,128)(2,1)S(1)}, u32[]{:S(2)}, u32[]{:S(2)}) collective-permute-start(bf16[80,768]{1,0:T(8,128)(2,1)S(1)} %shard_map.58.own4), channel_id=1, source_target_pairs={{16,0},{24,8},{0,16},{8,24},{17,1},{25,9},{1,17},{9,25},{18,2},{26... | collective-permute-start | bytes 368648 | tf_op jit(solution)/shard_map/ppermute | solution.py:22
  116.9 12.2 %collective-permute-start.29 = (bf16[32,1920]{1,0:T(8,128)(2,1)S(1)}, bf16[32,1920]{1,0:T(8,128)(2,1)S(1)}, u32[]{:S(2)}, u32[]{:S(2)}) collective-permute-start(bf16[32,1920]{1,0:T(8,128)(2,1)S(1)} %slice.27), channel_id=1, source_target_pairs={{8,0},{16,8},{24,16},{0,24},{9,1},{17,9},{25,17},{1,25},{10,2},{18... | collective-permute-start | bytes 368648 | tf_op jit(solution)/shard_map/ppermute | solution.py:22
  125.3 10.7 %collective-permute-start.31 = (f32[240,512]{1,0:T(8,128)S(1)}, f32[240,512]{1,0:T(8,128)S(1)}, u32[]{:S(2)}, u32[]{:S(2)}) collective-permute-start(f32[240,512]{1,0:T(8,128)S(1)} %get-tuple-element.64), channel_id=1, source_target_pairs={{1,0},{0,1},{3,2},{2,3},{5,4},{4,5},{7,6},{6,7},{9,8},{8,9},{11,10... | collective-permute-start | bytes 1474568 | tf_op jit(solution)/shard_map/ppermute | solution.py:26
  131.0 10.7 %all-to-all-start = ((f32[16,8,512]{2,1,0:T(8,128)}), f32[16,8,512]{2,1,0:T(8,128)S(1)}, u32[]{:S(2)}, u32[]{:S(2)}) async-start(f32[16,8,512]{2,1,0:T(8,128)} %get-tuple-element.68), calls=%async_computation | async-start | bytes 524288 | tf_op jit(solution)/shard_map/all_to_all | solution.py:389
  134.5 1.5 %collective-permute-start.32 = (f32[80,512]{1,0:T(8,128)S(1)}, f32[80,512]{1,0:T(8,128)S(1)}, u32[]{:S(2)}, u32[]{:S(2)}) collective-permute-start(f32[80,512]{1,0:T(8,128)S(1)} %get-tuple-element.65), channel_id=1, source_target_pairs={{1,0},{0,1},{3,2},{2,3},{5,4},{4,5},{7,6},{6,7},{9,8},{8,9},{11,10... | collective-permute-start | bytes 491528 | tf_op jit(solution)/shard_map/ppermute | solution.py:26

commit v5 on v1

--- a/solution.py
+++ b/solution.py
@@ -220,13 +220,13 @@
     gram[0:low, :] = r2lo[:, :images]
     gram[low:, :] = r2hi[:, :images]
     part = lane_sum(r2lo, images)
-    zero = jnp.zeros((1, width), f32)
     got = []
     for out, cols in ((send, slice(width, 2 * width)), (my, slice(0, width))):
         v = jnp.dot(gram[...], n[:, cols], preferred_element_type=f32)
         out[...] = v
         more = column_sums(v, n[pl.ds(at, rx), cols])
-        got.append(acc[:, cols] + jnp.concatenate(more + [zero + part] + [zero] * 5, 0))
+        lanes = jnp.broadcast_to(part, (1, 128)) + acc[2:3, 0:128]
+        got.append(jnp.concatenate([acc[0:1, cols] + more[0], acc[1:2, cols] + more[1], lanes], 1))
     to_even = jnp.where(lax.axis_index("core") == 0, got[1], got[0])
     to_odd = jnp.where(lax.axis_index("core") == 0, got[0], got[1])
     for i in range(0, sums.shape[0], 2):
@@ -242,13 +242,13 @@
     even, odd = sums[0], sums[1]
     for i in range(2, sums.shape[0], 2):
         even, odd = even + sums[i], odd + sums[i + 1]
-    loss[...] = even[2:3, 0:1] + odd[2:3, 0:1]
+    loss[...] = even[:, 2 * width : 2 * width + 1] + odd[:, 2 * width : 2 * width + 1]
     mine = jnp.where(lax.axis_index("core") == 0, even, odd)
     theirs = jnp.where(lax.axis_index("core") == 0, odd, even)
-    my_mean = (scale * mine[0:1, :] + coef * diag[2:3, :]) / images
-    my_dot = scale * mine[1:2, :] / images + coef * c
-    other_mean = (scale * theirs[0:1, :] + coef * diag[1:2, :]) / images
-    other_dot = scale * theirs[1:2, :] / images + coef * c
+    my_mean = (scale * mine[:, :width] + coef * diag[2:3, :]) / images
+    my_dot = scale * mine[:, width : 2 * width] / images + coef * c
+    other_mean = (scale * theirs[:, :width] + coef * diag[1:2, :]) / images
+    other_dot = scale * theirs[:, width : 2 * width] / images + coef * c
     starts = row_starts(rx)
 
     def write(my_ref, other_ref):
@@ -291,6 +291,10 @@
     )(*args, *fetch)
 
 
+def after(v, *others):
+    return lax.optimization_barrier((v,) + others)[0]
+
+
 def per_device(view_a, view_b):
     rows, width = view_a.shape
     images, full, rx, cw = rows * 8, width * 2, rows // 4, rows * 2
@@ -356,10 +360,10 @@
         scratch=[pltpu.VMEM((3 * rx, images), bf16)],
         limit=8,
     )
-    other3 = from_pair(send3, "core")
+    other3 = from_pair(after(send3, r2lo, r2hi), "core")
     my1, send1, sums = call(
         last_product_kernel,
-        [quarter, quarter, like((16, 8, width), f32)],
+        [quarter, quarter, like((16, 1, full + 128), f32)],
         *(r2lo, r2hi, n, acc),
         scratch=[pltpu.VMEM((rx, images), bf16)],
     )

time: 142 us -> 140 us (0.986)
  blocking collectives: 0 us -> 9.55 us
  starting transfers between devices: 56.6 us -> 51 us
  waiting for transfers between devices: 66.7 us -> 61.8 us
    all_to_all x0 -> x1, blocking collectives: none -> 9.55 us  [per_device(): lax.all_to_all(sums, batch + ('core',), split_axis=0, concat_axis=0, tile...]
    all_to_all x1 -> x0, starting transfers between devices: 6.01 us -> none  [per_device(): lax.all_to_all(sums, batch + ('core',), split_axis=0, concat_axis=0, tile...]
    all_to_all x1 -> x0, waiting for transfers between devices: 5.77 us -> none  [per_device(): lax.all_to_all(sums, batch + ('core',), split_axis=0, concat_axis=0, tile...]
    ppermute x21, waiting for transfers between devices: 47.6 us -> 49.6 us  [from_axis(): return lax.ppermute(v, axis, [((i + k) % 4, i) for i in range(4)])]
  transfers between devices with their start and end apart: 31 -> 30, of which waited for: 19 -> 19; matrix products, arithmetic and copies ran while one was open for 0% -> 0% of each run, Pallas kernels for 6% -> 6%
where the time goes in v5:
time: 140 us; the launch traced here: 139 us
  waiting for transfers between devices  61.8 us (44%)
  starting transfers between devices  51 us (36%)
  Pallas kernels  14.9 us (11%)
  blocking collectives  9.55 us (7%)
    ppermute x21, waiting for transfers between devices, from_axis(): return lax.ppermute(v, axis, [((i + k) % 4, i) for i in range(4)])  49.6 us
    ppermute x21, starting transfers between devices, from_axis(): return lax.ppermute(v, axis, [((i + k) % 4, i) for i in range(4)])  35.4 us
    ppermute x9, starting transfers between devices, from_pair(): return lax.ppermute(v, axis, [(1, 0), (0, 1)])  15.6 us
    pallas_call x12, Pallas kernels, call(): pl.pallas_call(kernel, out_shape=outs, in_specs=[pl.BlockSpec(memory_spac...  14.9 us
    ppermute x9, waiting for transfers between devices, from_pair(): return lax.ppermute(v, axis, [(1, 0), (0, 1)])  12.1 us
    all_to_all x1, blocking collectives, per_device(): lax.all_to_all(sums, batch + ('core',), split_axis=0, concat_axis=0, tile...  9.55 us
  transfers between devices with their start and end apart: 30, of which 19 were waited for; matrix products, arithmetic and copies ran while one was open for 0% of the time, Pallas kernels for 6%

profile of v5, /device:TPU:1, one launch (start us, length us, event | category | flops | bytes accessed | tf_op | source)
XLA Modules:
  0.0 139.5 jit_solution(14199775224828360262)
XLA Ops:
  0.6 1.1 broadcast_select_fusion.1
  1.8 3.3 %collective-permute-start = (bf16[320,512]{1,0:T(8,128)(2,1)S(1)}, bf16[320,512]{1,0:T(8,128)(2,1)S(1)}, u32[]{:S(2)}, u32[]{:S(2)}) collective-permute-start(bf16[320,512]{1,0:T(8,128)(2,1)S(1)} %get-tuple-element.72), channel_id=1, source_target_pairs={{1,0},{0,1},{3,2},{2,3},{5,4},{4,5},{7,6},{6,7},{9,8},{8,9},{11,10... | collective-permute-start | bytes 983048 | tf_op jit(solution)/shard_map/ppermute | solution.py:26
  5.1 1.3 collective-permute-done
  6.3 0.1 pad_maximum_fusion.own
  6.4 0.1 collective-permute-start.3
  6.5 2.7 %collective-permute-start.2 = (bf16[320,1024]{1,0:T(8,128)(2,1)S(1)}, bf16[320,1024]{1,0:T(8,128)(2,1)S(1)}, u32[]{:S(2)}, u32[]{:S(2)}) collective-permute-start(bf16[320,1024]{1,0:T(8,128)(2,1)S(1)} %pad_maximum_fusion.own), channel_id=1, source_target_pairs={{64,0},{128,64},{192,128},{0,192},{65,1},{129,65},{193,129},{1,193... | collective-permute-start | bytes 1966088 | tf_op jit(solution)/shard_map/ppermute | solution.py:22
  9.2 0.0 collective-permute-start.1
  9.2 14.4 %collective-permute-done.3.refs_2_ = bf16[320,1024]{1,0:T(8,128)(2,1)S(1)} collective-permute-done((bf16[320,1024]{1,0:T(8,128)(2,1)S(1)}, bf16[320,1024]{1,0:T(8,128)(2,1)S(1)}, u32[]{:S(2)}, u32[]{:S(2)}) %collective-permute-start.3) | collective-permute-done | bytes 655392 | tf_op jit(solution)/shard_map/ppermute | solution.py:22
  23.7 0.1 collective-permute-start.5
  23.8 0.0 collective-permute-done.2.refs_1_
  23.8 2.7 %collective-permute-start.4 = (bf16[160,1024]{1,0:T(8,128)(2,1)S(1)}, bf16[160,1024]{1,0:T(8,128)(2,1)S(1)}, u32[]{:S(2)}, u32[]{:S(2)}) collective-permute-start(bf16[160,1024]{1,0:T(8,128)(2,1)S(1)} %slice.28), channel_id=1, source_target_pairs={{64,0},{128,64},{192,128},{0,192},{65,1},{129,65},{193,129},{1,193... | collective-permute-start | bytes 983048 | tf_op jit(solution)/shard_map/ppermute | solution.py:22
  26.6 2.7 %collective-permute-start.6 = (bf16[320,1024]{1,0:T(8,128)(2,1)S(1)}, bf16[320,1024]{1,0:T(8,128)(2,1)S(1)}, u32[]{:S(2)}, u32[]{:S(2)}) collective-permute-start(bf16[320,1024]{1,0:T(8,128)(2,1)S(1)} %collective-permute-done.1.refs_0_), channel_id=1, source_target_pairs={{64,0},{128,64},{192,128},{0,192},{65,1},{129,65},{193,129},{1,193... | collective-permute-start | bytes 1966088 | tf_op jit(solution)/shard_map/ppermute | solution.py:22
  29.2 3.7 %collective-permute-done.5.refs_4_ = bf16[160,1024]{1,0:T(8,128)(2,1)S(1)} collective-permute-done((bf16[160,1024]{1,0:T(8,128)(2,1)S(1)}, bf16[160,1024]{1,0:T(8,128)(2,1)S(1)}, u32[]{:S(2)}, u32[]{:S(2)}) %collective-permute-start.5) | collective-permute-done | bytes 327712 | tf_op jit(solution)/shard_map/ppermute | solution.py:22
  33.0 0.1 collective-permute-start.9
  33.1 1.4 collective-permute-start.8
  34.4 1.8 %shard_map.49 = (f32[24,1024]{1,0:T(8,128)S(1)}, bf16[1600,1024]{1,0:T(8,128)(2,1)S(1)}) custom-call(bf16[320,1024]{1,0:T(8,128)(2,1)S(1)} %pad_maximum_fusion.own, bf16[320,1024]{1,0:T(8,128)(2,1)S(1)} %collective-permute-done.1.refs_0_, bf16[320,1024]{1,0:T(8,128)(2,1)S(1)} %collective-permute-done.2.refs_1_, ...), custom_call_target="tpu_custom_call" | custom-call | tf_op jit(solution)/shard_map/pallas_call | solution.py:282
  36.3 2.9 %collective-permute-done.9.refs_3_ = bf16[160,1024]{1,0:T(8,128)(2,1)S(1)} collective-permute-done((bf16[160,1024]{1,0:T(8,128)(2,1)S(1)}, bf16[160,1024]{1,0:T(8,128)(2,1)S(1)}, u32[]{:S(2)}, u32[]{:S(2)}) %collective-permute-start.9) | collective-permute-done | bytes 327712 | tf_op jit(solution)/shard_map/ppermute | solution.py:26
  39.2 6.2 %collective-permute-done.8.refs_2_ = bf16[160,1024]{1,0:T(8,128)(2,1)S(1)} collective-permute-done((bf16[160,1024]{1,0:T(8,128)(2,1)S(1)}, bf16[160,1024]{1,0:T(8,128)(2,1)S(1)}, u32[]{:S(2)}, u32[]{:S(2)}) %collective-permute-start.8) | collective-permute-done | bytes 327712 | tf_op jit(solution)/shard_map/ppermute | solution.py:26
  45.4 1.7 %collective-permute-done.7.refs_1_ = bf16[320,1024]{1,0:T(8,128)(2,1)S(1)} collective-permute-done((bf16[320,1024]{1,0:T(8,128)(2,1)S(1)}, bf16[320,1024]{1,0:T(8,128)(2,1)S(1)}, u32[]{:S(2)}, u32[]{:S(2)}) %collective-permute-start.7) | collective-permute-done | bytes 655392 | tf_op jit(solution)/shard_map/ppermute | solution.py:22
  47.0 4.6 %shard_map.50 = (bf16[2560,1024]{1,0:T(8,128)(2,1)S(1)}, bf16[2560,512]{1,0:T(8,128)(2,1)S(1)}, f32[8,1024]{1,0:T(8,128)S(1)}, bf16[48,2560]{1,0:T(8,128)(2,1)S(1)}, bf16[32,2560]{1,0:T(8,128)(2,1)S(1)}) custom-call(f32[24,1024]{1,0:T(8,128)S(1)} %get-tuple-element.37.st, bf16[1600,1024]{1,0:T(8,128)(2,1)S(1)} %get-tuple-element.38.known, ...), custom_call_target="tpu_custom_call" | custom-call | tf_op jit(solution)/shard_map/pallas_call | solution.py:282
  51.6 0.1 collective-permute-start.10
  51.7 2.7 %collective-permute-start.11 = (bf16[32,2560]{1,0:T(8,128)(2,1)S(1)}, bf16[32,2560]{1,0:T(8,128)(2,1)S(1)}, u32[]{:S(2)}, u32[]{:S(2)}) collective-permute-start(bf16[32,2560]{1,0:T(8,128)(2,1)S(1)} %get-tuple-element.44), channel_id=1, source_target_pairs={{8,0},{16,8},{24,16},{0,24},{9,1},{17,9},{25,17},{1,25},{10,2},{18... | collective-permute-start | bytes 491528 | tf_op jit(solution)/shard_map/ppermute | solution.py:22
  54.4 2.4 %shard_map.51 = (bf16[80,2560]{1,0:T(8,128)(2,1)S(1)}, bf16[80,2560]{1,0:T(8,128)(2,1)S(1)}, bf16[80,2560]{1,0:T(8,128)(2,1)S(1)}) custom-call(bf16[2560,1024]{1,0:T(8,128)(2,1)S(1)} %get-tuple-element.39.n), custom_call_target="tpu_custom_call" | custom-call | tf_op jit(solution)/shard_map/pallas_call | solution.py:282
  56.8 1.2 collective-permute-done.10.a
  58.0 0.1 shard_map.52
  58.1 0.1 collective-permute-start.12
  58.2 2.7 %collective-permute-start.13 = (bf16[80,2560]{1,0:T(8,128)(2,1)S(1)}, bf16[80,2560]{1,0:T(8,128)(2,1)S(1)}, u32[]{:S(2)}, u32[]{:S(2)}) collective-permute-start(bf16[80,2560]{1,0:T(8,128)(2,1)S(1)} %get-tuple-element.46), channel_id=1, source_target_pairs={{8,0},{16,8},{24,16},{0,24},{9,1},{17,9},{25,17},{1,25},{10,2},{18... | collective-permute-start | bytes 1228808 | tf_op jit(solution)/shard_map/ppermute | solution.py:22
  60.8 5.3 %collective-permute-done.12.e = bf16[80,2560]{1,0:T(8,128)(2,1)S(1)} collective-permute-done((bf16[80,2560]{1,0:T(8,128)(2,1)S(1)}, bf16[80,2560]{1,0:T(8,128)(2,1)S(1)}, u32[]{:S(2)}, u32[]{:S(2)}) %collective-permute-start.12) | collective-permute-done | bytes 409632 | tf_op jit(solution)/shard_map/ppermute | solution.py:22
  66.2 0.2 shard_map.53
  66.4 5.5 %collective-permute-start.14 = (bf16[2560,512]{1,0:T(8,128)(2,1)S(1)}, bf16[2560,512]{1,0:T(8,128)(2,1)S(1)}, u32[]{:S(2)}, u32[]{:S(2)}) collective-permute-start(bf16[2560,512]{1,0:T(8,128)(2,1)S(1)} %get-tuple-element.51), channel_id=1, source_target_pairs={{1,0},{0,1},{3,2},{2,3},{5,4},{4,5},{7,6},{6,7},{9,8},{8,9},{11,10... | collective-permute-start | bytes 7864328 | tf_op jit(solution)/shard_map/ppermute | solution.py:26
  71.9 1.8 %collective-permute-start.17 = (bf16[80,640]{1,0:T(8,128)(2,1)S(1)}, bf16[80,640]{1,0:T(8,128)(2,1)S(1)}, u32[]{:S(2)}, u32[]{:S(2)}) collective-permute-start(bf16[80,640]{1,0:T(8,128)(2,1)S(1)} %get-tuple-element.56), channel_id=1, source_target_pairs={{6,0},{0,2},{2,4},{4,6},{7,1},{1,3},{3,5},{5,7},{14,8},{8,10},{10,... | collective-permute-start | bytes 307208 | tf_op jit(solution)/shard_map/ppermute | solution.py:22
  73.7 4.8 %collective-permute-start.16 = (bf16[80,640]{1,0:T(8,128)(2,1)S(1)}, bf16[80,640]{1,0:T(8,128)(2,1)S(1)}, u32[]{:S(2)}, u32[]{:S(2)}) collective-permute-start(bf16[80,640]{1,0:T(8,128)(2,1)S(1)} %get-tuple-element.55), channel_id=1, source_target_pairs={{4,0},{6,2},{0,4},{2,6},{5,1},{7,3},{1,5},{3,7},{12,8},{14,10},{8,... | collective-permute-start | bytes 307208 | tf_op jit(solution)/shard_map/ppermute | solution.py:22
  78.5 2.4 %collective-permute-start.18 = (bf16[80,640]{1,0:T(8,128)(2,1)S(1)}, bf16[80,640]{1,0:T(8,128)(2,1)S(1)}, u32[]{:S(2)}, u32[]{:S(2)}) collective-permute-start(bf16[80,640]{1,0:T(8,128)(2,1)S(1)} %get-tuple-element.57), channel_id=1, source_target_pairs={{2,0},{4,2},{6,4},{0,6},{3,1},{5,3},{7,5},{1,7},{10,8},{12,10},{14... | collective-permute-start | bytes 307208 | tf_op jit(solution)/shard_map/ppermute | solution.py:22
  80.9 0.9 collective-permute-start.15
  81.8 0.8 collective-permute-done.15.inv_o
  82.6 1.1 shard_map.54
  83.7 2.1 %collective-permute-done.16.r1 = bf16[80,640]{1,0:T(8,128)(2,1)S(1)} collective-permute-done((bf16[80,640]{1,0:T(8,128)(2,1)S(1)}, bf16[80,640]{1,0:T(8,128)(2,1)S(1)}, u32[]{:S(2)}, u32[]{:S(2)}) %collective-permute-start.16) | collective-permute-done | bytes 102432 | tf_op jit(solution)/shard_map/ppermute | solution.py:22
  85.9 3.0 %collective-permute-done.18.r3 = bf16[80,640]{1,0:T(8,128)(2,1)S(1)} collective-permute-done((bf16[80,640]{1,0:T(8,128)(2,1)S(1)}, bf16[80,640]{1,0:T(8,128)(2,1)S(1)}, u32[]{:S(2)}, u32[]{:S(2)}) %collective-permute-start.18) | collective-permute-done | bytes 102432 | tf_op jit(solution)/shard_map/ppermute | solution.py:22
  88.8 0.1 shard_map.55.mine
  88.9 0.6 collective-permute-start.19
  89.5 0.9 collective-permute-done.19.theirs
  90.4 0.1 shard_map.56.own
  90.6 1.5 %collective-permute-start.20 = (bf16[80,768]{1,0:T(8,128)(2,1)S(1)}, bf16[80,768]{1,0:T(8,128)(2,1)S(1)}, u32[]{:S(2)}, u32[]{:S(2)}) collective-permute-start(bf16[80,768]{1,0:T(8,128)(2,1)S(1)} %shard_map.56.own), channel_id=1, source_target_pairs={{6,0},{0,2},{2,4},{4,6},{7,1},{1,3},{3,5},{5,7},{14,8},{8,10},{10,... | collective-permute-start | bytes 368648 | tf_op jit(solution)/shard_map/ppermute | solution.py:22
  92.0 2.2 %collective-permute-start.21 = (bf16[80,768]{1,0:T(8,128)(2,1)S(1)}, bf16[80,768]{1,0:T(8,128)(2,1)S(1)}, u32[]{:S(2)}, u32[]{:S(2)}) collective-permute-start(bf16[80,768]{1,0:T(8,128)(2,1)S(1)} %shard_map.56.own), channel_id=1, source_target_pairs={{2,0},{4,2},{6,4},{0,6},{3,1},{5,3},{7,5},{1,7},{10,8},{12,10},{14... | collective-permute-start | bytes 368648 | tf_op jit(solution)/shard_map/ppermute | solution.py:22
  94.2 5.7 %collective-permute-done.20.r1 = bf16[80,768]{1,0:T(8,128)(2,1)S(1)} collective-permute-done((bf16[80,768]{1,0:T(8,128)(2,1)S(1)}, bf16[80,768]{1,0:T(8,128)(2,1)S(1)}, u32[]{:S(2)}, u32[]{:S(2)}) %collective-permute-start.20) | collective-permute-done | bytes 122912 | tf_op jit(solution)/shard_map/ppermute | solution.py:22
  99.9 0.3 collective-permute-start.22
  100.2 0.7 collective-permute-done.21.r3
  100.9 2.6 %collective-permute-start.23 = (bf16[32,768]{1,0:T(8,128)(2,1)S(1)}, bf16[32,768]{1,0:T(8,128)(2,1)S(1)}, u32[]{:S(2)}, u32[]{:S(2)}) collective-permute-start(bf16[32,768]{1,0:T(8,128)(2,1)S(1)} %slice.31), channel_id=1, source_target_pairs={{2,0},{4,2},{6,4},{0,6},{3,1},{5,3},{7,5},{1,7},{10,8},{12,10},{14... | collective-permute-start | bytes 147464 | tf_op jit(solution)/shard_map/ppermute | solution.py:22
  103.6 1.4 %collective-permute-done.23.r2hi = bf16[32,768]{1,0:T(8,128)(2,1)S(1)} collective-permute-done((bf16[32,768]{1,0:T(8,128)(2,1)S(1)}, bf16[32,768]{1,0:T(8,128)(2,1)S(1)}, u32[]{:S(2)}, u32[]{:S(2)}) %collective-permute-start.23) | collective-permute-done | bytes 49184 | tf_op jit(solution)/shard_map/ppermute | solution.py:22
  105.0 0.3 collective-permute-done.22.r2lo
  105.2 0.1 shard_map.57.own
  105.3 1.2 collective-permute-start.24
  106.5 2.1 %collective-permute-start.25 = (bf16[80,2688]{1,0:T(8,128)(2,1)S(1)}, bf16[80,2688]{1,0:T(8,128)(2,1)S(1)}, u32[]{:S(2)}, u32[]{:S(2)}) collective-permute-start(bf16[80,2688]{1,0:T(8,128)(2,1)S(1)} %shard_map.57.own), channel_id=1, source_target_pairs={{8,0},{16,8},{24,16},{0,24},{9,1},{17,9},{25,17},{1,25},{10,2},{18... | collective-permute-start | bytes 1290248 | tf_op jit(solution)/shard_map/ppermute | solution.py:22
  108.7 8.0 %collective-permute-done.24.r1 = bf16[80,2688]{1,0:T(8,128)(2,1)S(1)} collective-permute-done((bf16[80,2688]{1,0:T(8,128)(2,1)S(1)}, bf16[80,2688]{1,0:T(8,128)(2,1)S(1)}, u32[]{:S(2)}, u32[]{:S(2)}) %collective-permute-start.24) | collective-permute-done | bytes 430112 | tf_op jit(solution)/shard_map/ppermute | solution.py:22
  116.7 0.1 collective-permute-start.26
  116.8 2.7 %collective-permute-start.27 = (bf16[32,2688]{1,0:T(8,128)(2,1)S(1)}, bf16[32,2688]{1,0:T(8,128)(2,1)S(1)}, u32[]{:S(2)}, u32[]{:S(2)}) collective-permute-start(bf16[32,2688]{1,0:T(8,128)(2,1)S(1)} %slice.33), channel_id=1, source_target_pairs={{8,0},{16,8},{24,16},{0,24},{9,1},{17,9},{25,17},{1,25},{10,2},{18... | collective-permute-start | bytes 516104 | tf_op jit(solution)/shard_map/ppermute | solution.py:22
  119.5 1.5 %shard_map.58 = (f32[240,512]{1,0:T(8,128)S(1)}, f32[240,512]{1,0:T(8,128)S(1)}, f32[8,1024]{1,0:T(8,128)S(1)}) custom-call(bf16[80,2688]{1,0:T(8,128)(2,1)S(1)} %shard_map.57.own, bf16[80,2688]{1,0:T(8,128)(2,1)S(1)} %collective-permute-done.24.r1, bf16[80,2688]{1,0:T(8,128)(2,1)S(1)} %collective-permute-done.25.r3, bf16[2560,1024]{1,0:T(8,128)(2,1)S(1)} %get-tuple-element.39.n), custom_call_target="tpu_custom_call" | custom-call | tf_op jit(solution)/shard_map/pallas_call | solution.py:282
  121.1 0.8 collective-permute-done.27.r2hi
  121.9 1.3 collective-permute-done.26.r2lo
  123.1 3.7 %collective-permute-start.28 = (f32[240,512]{1,0:T(8,128)S(1)}, f32[240,512]{1,0:T(8,128)S(1)}, u32[]{:S(2)}, u32[]{:S(2)}) collective-permute-start(f32[240,512]{1,0:T(8,128)S(1)} %get-tuple-element.62), channel_id=1, source_target_pairs={{1,0},{0,1},{3,2},{2,3},{5,4},{4,5},{7,6},{6,7},{9,8},{8,9},{11,10... | collective-permute-start | bytes 1474568 | tf_op jit(solution)/shard_map/ppermute | solution.py:26
  126.8 1.1 shard_map.59
  127.9 0.1 collective-permute-start.29
  128.0 9.6 %all_to_all.5.sums = f32[16,1,1152]{2,1,0:T(1,128)S(1)} all-to-all(f32[16,1,1152]{2,1,0:T(1,128)S(1)} %get-tuple-element.66), channel_id=1, replica_groups=mesh['y'=4,'zl'=2,'x'=4,'zh'=4,'core'=2] {'y','zl','core'}, dimensions={0} | all-to-all | bytes 147456 | tf_op jit(solution)/shard_map/all_to_all | solution.py:371
  137.6 1.7 %shard_map.60 = (f32[1,1]{1,0:T(1,128)}, f32[320,512]{1,0:T(8,128)}, f32[320,512]{1,0:T(8,128)}) custom-call(f32[240,512]{1,0:T(8,128)S(1)} %get-tuple-element.58.my3, f32[80,512]{1,0:T(8,128)S(1)} %get-tuple-element.60.my1, f32[240,512]{1,0:T(8,128)S(1)} %collective-permute-done.28.other3, f32[80,512]{1,0:T(8,128)S(1)} %collective-permute-done.29.other1, ...), custom_call_target="tpu_custom_call" | custom-call | tf_op jit(solution)/shard_map/pallas_call | solution.py:282
  (18 shorter events, 0.1 us)
Async XLA Ops:
  1.8 4.6 %collective-permute-start = (bf16[320,512]{1,0:T(8,128)(2,1)S(1)}, bf16[320,512]{1,0:T(8,128)(2,1)S(1)}, u32[]{:S(2)}, u32[]{:S(2)}) collective-permute-start(bf16[320,512]{1,0:T(8,128)(2,1)S(1)} %get-tuple-element.72), channel_id=1, source_target_pairs={{1,0},{0,1},{3,2},{2,3},{5,4},{4,5},{7,6},{6,7},{9,8},{8,9},{11,10... | collective-permute-start | bytes 983048 | tf_op jit(solution)/shard_map/ppermute | solution.py:26
  6.4 17.2 %collective-permute-start.3 = (bf16[320,1024]{1,0:T(8,128)(2,1)S(1)}, bf16[320,1024]{1,0:T(8,128)(2,1)S(1)}, u32[]{:S(2)}, u32[]{:S(2)}) collective-permute-start(bf16[320,1024]{1,0:T(8,128)(2,1)S(1)} %pad_maximum_fusion.own), channel_id=1, source_target_pairs={{192,0},{0,64},{64,128},{128,192},{193,1},{1,65},{65,129},{129,193... | collective-permute-start | bytes 1966088 | tf_op jit(solution)/shard_map/ppermute | solution.py:22
  6.5 17.3 %collective-permute-start.2 = (bf16[320,1024]{1,0:T(8,128)(2,1)S(1)}, bf16[320,1024]{1,0:T(8,128)(2,1)S(1)}, u32[]{:S(2)}, u32[]{:S(2)}) collective-permute-start(bf16[320,1024]{1,0:T(8,128)(2,1)S(1)} %pad_maximum_fusion.own), channel_id=1, source_target_pairs={{64,0},{128,64},{192,128},{0,192},{65,1},{129,65},{193,129},{1,193... | collective-permute-start | bytes 1966088 | tf_op jit(solution)/shard_map/ppermute | solution.py:22
  9.2 17.4 %collective-permute-start.1 = (bf16[320,1024]{1,0:T(8,128)(2,1)S(1)}, bf16[320,1024]{1,0:T(8,128)(2,1)S(1)}, u32[]{:S(2)}, u32[]{:S(2)}) collective-permute-start(bf16[320,1024]{1,0:T(8,128)(2,1)S(1)} %pad_maximum_fusion.own), channel_id=1, source_target_pairs={{32,0},{0,32},{33,1},{1,33},{34,2},{2,34},{35,3},{3,35},{36,4},{4,... | collective-permute-start | bytes 1966088 | tf_op jit(solution)/shard_map/ppermute | solution.py:26
  23.7 9.3 %collective-permute-start.5 = (bf16[160,1024]{1,0:T(8,128)(2,1)S(1)}, bf16[160,1024]{1,0:T(8,128)(2,1)S(1)}, u32[]{:S(2)}, u32[]{:S(2)}) collective-permute-start(bf16[160,1024]{1,0:T(8,128)(2,1)S(1)} %slice.29), channel_id=1, source_target_pairs={{192,0},{0,64},{64,128},{128,192},{193,1},{1,65},{65,129},{129,193... | collective-permute-start | bytes 983048 | tf_op jit(solution)/shard_map/ppermute | solution.py:22
  23.8 9.3 %collective-permute-start.4 = (bf16[160,1024]{1,0:T(8,128)(2,1)S(1)}, bf16[160,1024]{1,0:T(8,128)(2,1)S(1)}, u32[]{:S(2)}, u32[]{:S(2)}) collective-permute-start(bf16[160,1024]{1,0:T(8,128)(2,1)S(1)} %slice.28), channel_id=1, source_target_pairs={{64,0},{128,64},{192,128},{0,192},{65,1},{129,65},{193,129},{1,193... | collective-permute-start | bytes 983048 | tf_op jit(solution)/shard_map/ppermute | solution.py:22
  26.5 20.5 %collective-permute-start.7 = (bf16[320,1024]{1,0:T(8,128)(2,1)S(1)}, bf16[320,1024]{1,0:T(8,128)(2,1)S(1)}, u32[]{:S(2)}, u32[]{:S(2)}) collective-permute-start(bf16[320,1024]{1,0:T(8,128)(2,1)S(1)} %collective-permute-done.1.refs_0_), channel_id=1, source_target_pairs={{192,0},{0,64},{64,128},{128,192},{193,1},{1,65},{65,129},{129,193... | collective-permute-start | bytes 1966088 | tf_op jit(solution)/shard_map/ppermute | solution.py:22
  26.6 20.5 %collective-permute-start.6 = (bf16[320,1024]{1,0:T(8,128)(2,1)S(1)}, bf16[320,1024]{1,0:T(8,128)(2,1)S(1)}, u32[]{:S(2)}, u32[]{:S(2)}) collective-permute-start(bf16[320,1024]{1,0:T(8,128)(2,1)S(1)} %collective-permute-done.1.refs_0_), channel_id=1, source_target_pairs={{64,0},{128,64},{192,128},{0,192},{65,1},{129,65},{193,129},{1,193... | collective-permute-start | bytes 1966088 | tf_op jit(solution)/shard_map/ppermute | solution.py:22
  33.0 6.2 %collective-permute-start.9 = (bf16[160,1024]{1,0:T(8,128)(2,1)S(1)}, bf16[160,1024]{1,0:T(8,128)(2,1)S(1)}, u32[]{:S(2)}, u32[]{:S(2)}) collective-permute-start(bf16[160,1024]{1,0:T(8,128)(2,1)S(1)} %collective-permute-done.5.refs_4_), channel_id=1, source_target_pairs={{32,0},{0,32},{33,1},{1,33},{34,2},{2,34},{35,3},{3,35},{36,4},{4,... | collective-permute-start | bytes 983048 | tf_op jit(solution)/shard_map/ppermute | solution.py:26
  33.1 12.3 %collective-permute-start.8 = (bf16[160,1024]{1,0:T(8,128)(2,1)S(1)}, bf16[160,1024]{1,0:T(8,128)(2,1)S(1)}, u32[]{:S(2)}, u32[]{:S(2)}) collective-permute-start(bf16[160,1024]{1,0:T(8,128)(2,1)S(1)} %collective-permute-done.4.refs_3_), channel_id=1, source_target_pairs={{32,0},{0,32},{33,1},{1,33},{34,2},{2,34},{35,3},{3,35},{36,4},{4,... | collective-permute-start | bytes 983048 | tf_op jit(solution)/shard_map/ppermute | solution.py:26
  51.6 6.3 %collective-permute-start.10 = (bf16[48,2560]{1,0:T(8,128)(2,1)S(1)}, bf16[48,2560]{1,0:T(8,128)(2,1)S(1)}, u32[]{:S(2)}, u32[]{:S(2)}) collective-permute-start(bf16[48,2560]{1,0:T(8,128)(2,1)S(1)} %get-tuple-element.42), channel_id=1, source_target_pairs={{24,0},{0,8},{8,16},{16,24},{25,1},{1,9},{9,17},{17,25},{26,2},{2,... | collective-permute-start | bytes 737288 | tf_op jit(solution)/shard_map/ppermute | solution.py:22
  51.7 5.0 %collective-permute-start.11 = (bf16[32,2560]{1,0:T(8,128)(2,1)S(1)}, bf16[32,2560]{1,0:T(8,128)(2,1)S(1)}, u32[]{:S(2)}, u32[]{:S(2)}) collective-permute-start(bf16[32,2560]{1,0:T(8,128)(2,1)S(1)} %get-tuple-element.44), channel_id=1, source_target_pairs={{8,0},{16,8},{24,16},{0,24},{9,1},{17,9},{25,17},{1,25},{10,2},{18... | collective-permute-start | bytes 491528 | tf_op jit(solution)/shard_map/ppermute | solution.py:22
  58.1 8.1 %collective-permute-start.12 = (bf16[80,2560]{1,0:T(8,128)(2,1)S(1)}, bf16[80,2560]{1,0:T(8,128)(2,1)S(1)}, u32[]{:S(2)}, u32[]{:S(2)}) collective-permute-start(bf16[80,2560]{1,0:T(8,128)(2,1)S(1)} %get-tuple-element.45), channel_id=1, source_target_pairs={{24,0},{0,8},{8,16},{16,24},{25,1},{1,9},{9,17},{17,25},{26,2},{2,... | collective-permute-start | bytes 1228808 | tf_op jit(solution)/shard_map/ppermute | solution.py:22
  58.2 8.0 %collective-permute-start.13 = (bf16[80,2560]{1,0:T(8,128)(2,1)S(1)}, bf16[80,2560]{1,0:T(8,128)(2,1)S(1)}, u32[]{:S(2)}, u32[]{:S(2)}) collective-permute-start(bf16[80,2560]{1,0:T(8,128)(2,1)S(1)} %get-tuple-element.46), channel_id=1, source_target_pairs={{8,0},{16,8},{24,16},{0,24},{9,1},{17,9},{25,17},{1,25},{10,2},{18... | collective-permute-start | bytes 1228808 | tf_op jit(solution)/shard_map/ppermute | solution.py:22
  66.4 16.2 %collective-permute-start.14 = (bf16[2560,512]{1,0:T(8,128)(2,1)S(1)}, bf16[2560,512]{1,0:T(8,128)(2,1)S(1)}, u32[]{:S(2)}, u32[]{:S(2)}) collective-permute-start(bf16[2560,512]{1,0:T(8,128)(2,1)S(1)} %get-tuple-element.51), channel_id=1, source_target_pairs={{1,0},{0,1},{3,2},{2,3},{5,4},{4,5},{7,6},{6,7},{9,8},{8,9},{11,10... | collective-permute-start | bytes 7864328 | tf_op jit(solution)/shard_map/ppermute | solution.py:26
  71.9 11.8 %collective-permute-start.17 = (bf16[80,640]{1,0:T(8,128)(2,1)S(1)}, bf16[80,640]{1,0:T(8,128)(2,1)S(1)}, u32[]{:S(2)}, u32[]{:S(2)}) collective-permute-start(bf16[80,640]{1,0:T(8,128)(2,1)S(1)} %get-tuple-element.56), channel_id=1, source_target_pairs={{6,0},{0,2},{2,4},{4,6},{7,1},{1,3},{3,5},{5,7},{14,8},{8,10},{10,... | collective-permute-start | bytes 307208 | tf_op jit(solution)/shard_map/ppermute | solution.py:22
  73.7 12.2 %collective-permute-start.16 = (bf16[80,640]{1,0:T(8,128)(2,1)S(1)}, bf16[80,640]{1,0:T(8,128)(2,1)S(1)}, u32[]{:S(2)}, u32[]{:S(2)}) collective-permute-start(bf16[80,640]{1,0:T(8,128)(2,1)S(1)} %get-tuple-element.55), channel_id=1, source_target_pairs={{4,0},{6,2},{0,4},{2,6},{5,1},{7,3},{1,5},{3,7},{12,8},{14,10},{8,... | collective-permute-start | bytes 307208 | tf_op jit(solution)/shard_map/ppermute | solution.py:22
  78.5 10.4 %collective-permute-start.18 = (bf16[80,640]{1,0:T(8,128)(2,1)S(1)}, bf16[80,640]{1,0:T(8,128)(2,1)S(1)}, u32[]{:S(2)}, u32[]{:S(2)}) collective-permute-start(bf16[80,640]{1,0:T(8,128)(2,1)S(1)} %get-tuple-element.57), channel_id=1, source_target_pairs={{2,0},{4,2},{6,4},{0,6},{3,1},{5,3},{7,5},{1,7},{10,8},{12,10},{14... | collective-permute-start | bytes 307208 | tf_op jit(solution)/shard_map/ppermute | solution.py:22
  80.9 1.8 %collective-permute-start.15 = (f32[8,512]{1,0:T(8,128)S(1)}, f32[8,512]{1,0:T(8,128)S(1)}, u32[]{:S(2)}, u32[]{:S(2)}) collective-permute-start(f32[8,512]{1,0:T(8,128)S(1)} %slice.23), channel_id=1, source_target_pairs={{1,0},{0,1},{3,2},{2,3},{5,4},{4,5},{7,6},{6,7},{9,8},{8,9},{11,10... | collective-permute-start | bytes 49160 | tf_op jit(solution)/shard_map/ppermute | solution.py:26
  88.9 1.5 %collective-permute-start.19 = (bf16[80,640]{1,0:T(8,128)(2,1)S(1)}, bf16[80,640]{1,0:T(8,128)(2,1)S(1)}, u32[]{:S(2)}, u32[]{:S(2)}) collective-permute-start(bf16[80,640]{1,0:T(8,128)(2,1)S(1)} %shard_map.55.mine), channel_id=1, source_target_pairs={{1,0},{0,1},{3,2},{2,3},{5,4},{4,5},{7,6},{6,7},{9,8},{8,9},{11,10... | collective-permute-start | bytes 307208 | tf_op jit(solution)/shard_map/ppermute | solution.py:26
  90.6 9.3 %collective-permute-start.20 = (bf16[80,768]{1,0:T(8,128)(2,1)S(1)}, bf16[80,768]{1,0:T(8,128)(2,1)S(1)}, u32[]{:S(2)}, u32[]{:S(2)}) collective-permute-start(bf16[80,768]{1,0:T(8,128)(2,1)S(1)} %shard_map.56.own), channel_id=1, source_target_pairs={{6,0},{0,2},{2,4},{4,6},{7,1},{1,3},{3,5},{5,7},{14,8},{8,10},{10,... | collective-permute-start | bytes 368648 | tf_op jit(solution)/shard_map/ppermute | solution.py:22
  92.0 8.9 %collective-permute-start.21 = (bf16[80,768]{1,0:T(8,128)(2,1)S(1)}, bf16[80,768]{1,0:T(8,128)(2,1)S(1)}, u32[]{:S(2)}, u32[]{:S(2)}) collective-permute-start(bf16[80,768]{1,0:T(8,128)(2,1)S(1)} %shard_map.56.own), channel_id=1, source_target_pairs={{2,0},{4,2},{6,4},{0,6},{3,1},{5,3},{7,5},{1,7},{10,8},{12,10},{14... | collective-permute-start | bytes 368648 | tf_op jit(solution)/shard_map/ppermute | solution.py:22
  99.9 5.3 %collective-permute-start.22 = (bf16[48,768]{1,0:T(8,128)(2,1)S(1)}, bf16[48,768]{1,0:T(8,128)(2,1)S(1)}, u32[]{:S(2)}, u32[]{:S(2)}) collective-permute-start(bf16[48,768]{1,0:T(8,128)(2,1)S(1)} %slice.30), channel_id=1, source_target_pairs={{6,0},{0,2},{2,4},{4,6},{7,1},{1,3},{3,5},{5,7},{14,8},{8,10},{10,... | collective-permute-start | bytes 221192 | tf_op jit(solution)/shard_map/ppermute | solution.py:22
  100.9 4.0 %collective-permute-start.23 = (bf16[32,768]{1,0:T(8,128)(2,1)S(1)}, bf16[32,768]{1,0:T(8,128)(2,1)S(1)}, u32[]{:S(2)}, u32[]{:S(2)}) collective-permute-start(bf16[32,768]{1,0:T(8,128)(2,1)S(1)} %slice.31), channel_id=1, source_target_pairs={{2,0},{4,2},{6,4},{0,6},{3,1},{5,3},{7,5},{1,7},{10,8},{12,10},{14... | collective-permute-start | bytes 147464 | tf_op jit(solution)/shard_map/ppermute | solution.py:22
  105.3 11.3 %collective-permute-start.24 = (bf16[80,2688]{1,0:T(8,128)(2,1)S(1)}, bf16[80,2688]{1,0:T(8,128)(2,1)S(1)}, u32[]{:S(2)}, u32[]{:S(2)}) collective-permute-start(bf16[80,2688]{1,0:T(8,128)(2,1)S(1)} %shard_map.57.own), channel_id=1, source_target_pairs={{24,0},{0,8},{8,16},{16,24},{25,1},{1,9},{9,17},{17,25},{26,2},{2,... | collective-permute-start | bytes 1290248 | tf_op jit(solution)/shard_map/ppermute | solution.py:22
  106.5 10.3 %collective-permute-start.25 = (bf16[80,2688]{1,0:T(8,128)(2,1)S(1)}, bf16[80,2688]{1,0:T(8,128)(2,1)S(1)}, u32[]{:S(2)}, u32[]{:S(2)}) collective-permute-start(bf16[80,2688]{1,0:T(8,128)(2,1)S(1)} %shard_map.57.own), channel_id=1, source_target_pairs={{8,0},{16,8},{24,16},{0,24},{9,1},{17,9},{25,17},{1,25},{10,2},{18... | collective-permute-start | bytes 1290248 | tf_op jit(solution)/shard_map/ppermute | solution.py:22
  116.7 6.5 %collective-permute-start.26 = (bf16[48,2688]{1,0:T(8,128)(2,1)S(1)}, bf16[48,2688]{1,0:T(8,128)(2,1)S(1)}, u32[]{:S(2)}, u32[]{:S(2)}) collective-permute-start(bf16[48,2688]{1,0:T(8,128)(2,1)S(1)} %slice.32), channel_id=1, source_target_pairs={{24,0},{0,8},{8,16},{16,24},{25,1},{1,9},{9,17},{17,25},{26,2},{2,... | collective-permute-start | bytes 774152 | tf_op jit(solution)/shard_map/ppermute | solution.py:22
  116.8 5.1 %collective-permute-start.27 = (bf16[32,2688]{1,0:T(8,128)(2,1)S(1)}, bf16[32,2688]{1,0:T(8,128)(2,1)S(1)}, u32[]{:S(2)}, u32[]{:S(2)}) collective-permute-start(bf16[32,2688]{1,0:T(8,128)(2,1)S(1)} %slice.33), channel_id=1, source_target_pairs={{8,0},{16,8},{24,16},{0,24},{9,1},{17,9},{25,17},{1,25},{10,2},{18... | collective-permute-start | bytes 516104 | tf_op jit(solution)/shard_map/ppermute | solution.py:22
  123.1 14.5 %collective-permute-start.28 = (f32[240,512]{1,0:T(8,128)S(1)}, f32[240,512]{1,0:T(8,128)S(1)}, u32[]{:S(2)}, u32[]{:S(2)}) collective-permute-start(f32[240,512]{1,0:T(8,128)S(1)} %get-tuple-element.62), channel_id=1, source_target_pairs={{1,0},{0,1},{3,2},{2,3},{5,4},{4,5},{7,6},{6,7},{9,8},{8,9},{11,10... | collective-permute-start | bytes 1474568 | tf_op jit(solution)/shard_map/ppermute | solution.py:26
  127.9 9.7 %collective-permute-start.29 = (f32[80,512]{1,0:T(8,128)S(1)}, f32[80,512]{1,0:T(8,128)S(1)}, u32[]{:S(2)}, u32[]{:S(2)}) collective-permute-start(f32[80,512]{1,0:T(8,128)S(1)} %get-tuple-element.63), channel_id=1, source_target_pairs={{1,0},{0,1},{3,2},{2,3},{5,4},{4,5},{7,6},{6,7},{9,8},{8,9},{11,10... | collective-permute-start | bytes 491528 | tf_op jit(solution)/shard_map/ppermute | solution.py:26

commit v6 on v5

--- a/solution.py
+++ b/solution.py
@@ -213,17 +213,18 @@
         acc[:, cols] = jnp.concatenate(got + [zero + part] + [zero] * 5, 0)
 
 
-def last_product_kernel(r2lo, r2hi, n, acc, my, send, sums, gram):
+def last_product_kernel(r2lo, r2hi, n, send3, acc, my, send, sums, gram):
     (low, rx), images = (r2lo.shape[0], gram.shape[0]), gram.shape[1]
     width = my.shape[1]
     at = row_starts(rx)[2]
     gram[0:low, :] = r2lo[:, :images]
     gram[low:, :] = r2hi[:, :images]
     part = lane_sum(r2lo, images)
+    send[0 : send3.shape[0], :] = send3[...]
     got = []
     for out, cols in ((send, slice(width, 2 * width)), (my, slice(0, width))):
         v = jnp.dot(gram[...], n[:, cols], preferred_element_type=f32)
-        out[...] = v
+        out[out.shape[0] - v.shape[0] :, :] = v
         more = column_sums(v, n[pl.ds(at, rx), cols])
         lanes = jnp.broadcast_to(part, (1, 128)) + acc[2:3, 0:128]
         got.append(jnp.concatenate([acc[0:1, cols] + more[0], acc[1:2, cols] + more[1], lanes], 1))
@@ -234,7 +235,7 @@
         sums[i + 1] = to_odd
 
 
-def grad_kernel(images, my3, my1, other3, other1, my_own, o_own, diag, sums, inv_my, inv_other, loss, *refs):
+def grad_kernel(images, my3, my1, swapped, my_own, o_own, diag, sums, inv_my, inv_other, loss, *refs):
     grad_a, grad_b, out_my, out_other, sems = refs
     rx, width = my1.shape
     c = diag[0:1, :]
@@ -258,7 +259,7 @@
             rel = slice(i * rx, i * rx + rx)
             my, other = my_own[at, :].astype(f32), o_own[at, :].astype(f32)
             d_my = scale * (my3[rel, :] if i < 3 else my1[...]) + coef * other
-            d_other = scale * (other3[rel, :] if i < 3 else other1[...]) + coef * my
+            d_other = scale * swapped[rel, :] + coef * my
             out_my[rel, :] = (d_my - my_mean - my * my_dot) * inv_my[0:1, :width]
             copies.append(pltpu.make_async_copy(out_my.at[rel, :], my_ref.at[at, :], sems.at[2 * i]))
             copies[-1].start()
@@ -360,19 +361,18 @@
         scratch=[pltpu.VMEM((3 * rx, images), bf16)],
         limit=8,
     )
-    other3 = from_pair(after(send3, r2lo, r2hi), "core")
-    my1, send1, sums = call(
+    my1, send, sums = call(
         last_product_kernel,
-        [quarter, quarter, like((16, 1, full + 128), f32)],
-        *(r2lo, r2hi, n, acc),
+        [quarter, wide, like((16, 1, full + 128), f32)],
+        *(r2lo, r2hi, n, send3, acc),
         scratch=[pltpu.VMEM((rx, images), bf16)],
     )
-    other1 = from_pair(send1, "core")
+    other = from_pair(send, "core")
     sums = lax.all_to_all(sums, batch + ("core",), split_axis=0, concat_axis=0, tiled=True)
     loss, grad_a, grad_b = call(
         functools.partial(grad_kernel, images),
         [like((1, 1), f32), wide, wide],
-        *(my3, my1, other3, other1, my_own, o_own, diag, sums, inv, inv_other),
+        *(my3, my1, other, my_own, o_own, diag, sums, inv, inv_other),
         scratch=[pltpu.VMEM((rows, width), f32), pltpu.VMEM((rows, width), f32), pltpu.SemaphoreType.DMA((8,))],
         outside=2,
     )

time: 140 us -> 139 us (level)
    ppermute x9 -> x8, starting transfers between devices: 15.6 us -> 15.6 us  [from_pair(): return lax.ppermute(v, axis, [(1, 0), (0, 1)])]
    ppermute x9 -> x8, waiting for transfers between devices: 12.1 us -> 12.1 us  [from_pair(): return lax.ppermute(v, axis, [(1, 0), (0, 1)])]
  transfers between devices with their start and end apart: 30 -> 29, of which waited for: 19 -> 19; matrix products, arithmetic and copies ran while one was open for 0% -> 0% of each run, Pallas kernels for 6% -> 5%
where the time goes in v6:
time: 139 us
  waiting for transfers between devices  61.8 us (44%)
  starting transfers between devices  51 us (37%)
  Pallas kernels  14.9 us (11%)
  blocking collectives  9.17 us (7%)
    ppermute x21, waiting for transfers between devices, from_axis(): return lax.ppermute(v, axis, [((i + k) % 4, i) for i in range(4)])  49.6 us
    ppermute x21, starting transfers between devices, from_axis(): return lax.ppermute(v, axis, [((i + k) % 4, i) for i in range(4)])  35.4 us
    ppermute x8, starting transfers between devices, from_pair(): return lax.ppermute(v, axis, [(1, 0), (0, 1)])  15.6 us
    pallas_call x12, Pallas kernels, call(): pl.pallas_call(kernel, out_shape=outs, in_specs=[pl.BlockSpec(memory_spac...  14.9 us
    ppermute x8, waiting for transfers between devices, from_pair(): return lax.ppermute(v, axis, [(1, 0), (0, 1)])  12.1 us
    all_to_all x1, blocking collectives, per_device(): lax.all_to_all(sums, batch + ('core',), split_axis=0, concat_axis=0, tile...  9.17 us
  transfers between devices with their start and end apart: 29, of which 19 were waited for; matrix products, arithmetic and copies ran while one was open for 0% of the time, Pallas kernels for 5%

profile of v6, /device:TPU:1, one launch (start us, length us, event | category | flops | bytes accessed | tf_op | source)
XLA Modules:
  0.0 139.1 jit_solution(11006578668721602579)
XLA Ops:
  0.6 1.1 broadcast_select_fusion.1
  1.8 3.3 %collective-permute-start = (bf16[320,512]{1,0:T(8,128)(2,1)S(1)}, bf16[320,512]{1,0:T(8,128)(2,1)S(1)}, u32[]{:S(2)}, u32[]{:S(2)}) collective-permute-start(bf16[320,512]{1,0:T(8,128)(2,1)S(1)} %get-tuple-element.70), channel_id=1, source_target_pairs={{1,0},{0,1},{3,2},{2,3},{5,4},{4,5},{7,6},{6,7},{9,8},{8,9},{11,10... | collective-permute-start | bytes 983048 | tf_op jit(solution)/shard_map/ppermute | solution.py:26
  5.1 1.3 collective-permute-done
  6.3 0.1 pad_maximum_fusion.own
  6.4 0.1 collective-permute-start.3
  6.5 2.7 %collective-permute-start.2 = (bf16[320,1024]{1,0:T(8,128)(2,1)S(1)}, bf16[320,1024]{1,0:T(8,128)(2,1)S(1)}, u32[]{:S(2)}, u32[]{:S(2)}) collective-permute-start(bf16[320,1024]{1,0:T(8,128)(2,1)S(1)} %pad_maximum_fusion.own), channel_id=1, source_target_pairs={{64,0},{128,64},{192,128},{0,192},{65,1},{129,65},{193,129},{1,193... | collective-permute-start | bytes 1966088 | tf_op jit(solution)/shard_map/ppermute | solution.py:22
  9.2 0.0 collective-permute-start.1
  9.2 14.4 %collective-permute-done.3.refs_2_ = bf16[320,1024]{1,0:T(8,128)(2,1)S(1)} collective-permute-done((bf16[320,1024]{1,0:T(8,128)(2,1)S(1)}, bf16[320,1024]{1,0:T(8,128)(2,1)S(1)}, u32[]{:S(2)}, u32[]{:S(2)}) %collective-permute-start.3) | collective-permute-done | bytes 655392 | tf_op jit(solution)/shard_map/ppermute | solution.py:22
  23.7 0.1 collective-permute-start.5
  23.8 2.7 %collective-permute-start.4 = (bf16[160,1024]{1,0:T(8,128)(2,1)S(1)}, bf16[160,1024]{1,0:T(8,128)(2,1)S(1)}, u32[]{:S(2)}, u32[]{:S(2)}) collective-permute-start(bf16[160,1024]{1,0:T(8,128)(2,1)S(1)} %slice.28), channel_id=1, source_target_pairs={{64,0},{128,64},{192,128},{0,192},{65,1},{129,65},{193,129},{1,193... | collective-permute-start | bytes 983048 | tf_op jit(solution)/shard_map/ppermute | solution.py:22
  26.5 0.0 collective-permute-done.1.refs_0_
  26.5 0.0 collective-permute-start.7
  26.6 2.7 %collective-permute-start.6 = (bf16[320,1024]{1,0:T(8,128)(2,1)S(1)}, bf16[320,1024]{1,0:T(8,128)(2,1)S(1)}, u32[]{:S(2)}, u32[]{:S(2)}) collective-permute-start(bf16[320,1024]{1,0:T(8,128)(2,1)S(1)} %collective-permute-done.1.refs_0_), channel_id=1, source_target_pairs={{64,0},{128,64},{192,128},{0,192},{65,1},{129,65},{193,129},{1,193... | collective-permute-start | bytes 1966088 | tf_op jit(solution)/shard_map/ppermute | solution.py:22
  29.2 3.7 %collective-permute-done.5.refs_4_ = bf16[160,1024]{1,0:T(8,128)(2,1)S(1)} collective-permute-done((bf16[160,1024]{1,0:T(8,128)(2,1)S(1)}, bf16[160,1024]{1,0:T(8,128)(2,1)S(1)}, u32[]{:S(2)}, u32[]{:S(2)}) %collective-permute-start.5) | collective-permute-done | bytes 327712 | tf_op jit(solution)/shard_map/ppermute | solution.py:22
  33.0 0.1 collective-permute-start.9
  33.1 1.4 collective-permute-start.8
  34.4 1.8 %shard_map.49 = (f32[24,1024]{1,0:T(8,128)S(1)}, bf16[1600,1024]{1,0:T(8,128)(2,1)S(1)}) custom-call(bf16[320,1024]{1,0:T(8,128)(2,1)S(1)} %pad_maximum_fusion.own, bf16[320,1024]{1,0:T(8,128)(2,1)S(1)} %collective-permute-done.1.refs_0_, bf16[320,1024]{1,0:T(8,128)(2,1)S(1)} %collective-permute-done.2.refs_1_, ...), custom_call_target="tpu_custom_call" | custom-call | tf_op jit(solution)/shard_map/pallas_call | solution.py:283
  36.3 2.9 %collective-permute-done.9.refs_3_ = bf16[160,1024]{1,0:T(8,128)(2,1)S(1)} collective-permute-done((bf16[160,1024]{1,0:T(8,128)(2,1)S(1)}, bf16[160,1024]{1,0:T(8,128)(2,1)S(1)}, u32[]{:S(2)}, u32[]{:S(2)}) %collective-permute-start.9) | collective-permute-done | bytes 327712 | tf_op jit(solution)/shard_map/ppermute | solution.py:26
  39.2 6.2 %collective-permute-done.8.refs_2_ = bf16[160,1024]{1,0:T(8,128)(2,1)S(1)} collective-permute-done((bf16[160,1024]{1,0:T(8,128)(2,1)S(1)}, bf16[160,1024]{1,0:T(8,128)(2,1)S(1)}, u32[]{:S(2)}, u32[]{:S(2)}) %collective-permute-start.8) | collective-permute-done | bytes 327712 | tf_op jit(solution)/shard_map/ppermute | solution.py:26
  45.4 1.7 %collective-permute-done.7.refs_1_ = bf16[320,1024]{1,0:T(8,128)(2,1)S(1)} collective-permute-done((bf16[320,1024]{1,0:T(8,128)(2,1)S(1)}, bf16[320,1024]{1,0:T(8,128)(2,1)S(1)}, u32[]{:S(2)}, u32[]{:S(2)}) %collective-permute-start.7) | collective-permute-done | bytes 655392 | tf_op jit(solution)/shard_map/ppermute | solution.py:22
  47.0 4.6 %shard_map.50 = (bf16[2560,1024]{1,0:T(8,128)(2,1)S(1)}, bf16[2560,512]{1,0:T(8,128)(2,1)S(1)}, f32[8,1024]{1,0:T(8,128)S(1)}, bf16[48,2560]{1,0:T(8,128)(2,1)S(1)}, bf16[32,2560]{1,0:T(8,128)(2,1)S(1)}) custom-call(f32[24,1024]{1,0:T(8,128)S(1)} %get-tuple-element.36.st, bf16[1600,1024]{1,0:T(8,128)(2,1)S(1)} %get-tuple-element.37.known, ...), custom_call_target="tpu_custom_call" | custom-call | tf_op jit(solution)/shard_map/pallas_call | solution.py:283
  51.6 0.1 collective-permute-start.10
  51.7 2.7 %collective-permute-start.11 = (bf16[32,2560]{1,0:T(8,128)(2,1)S(1)}, bf16[32,2560]{1,0:T(8,128)(2,1)S(1)}, u32[]{:S(2)}, u32[]{:S(2)}) collective-permute-start(bf16[32,2560]{1,0:T(8,128)(2,1)S(1)} %get-tuple-element.43), channel_id=1, source_target_pairs={{8,0},{16,8},{24,16},{0,24},{9,1},{17,9},{25,17},{1,25},{10,2},{18... | collective-permute-start | bytes 491528 | tf_op jit(solution)/shard_map/ppermute | solution.py:22
  54.4 2.4 %shard_map.51 = (bf16[80,2560]{1,0:T(8,128)(2,1)S(1)}, bf16[80,2560]{1,0:T(8,128)(2,1)S(1)}, bf16[80,2560]{1,0:T(8,128)(2,1)S(1)}) custom-call(bf16[2560,1024]{1,0:T(8,128)(2,1)S(1)} %get-tuple-element.38.n), custom_call_target="tpu_custom_call" | custom-call | tf_op jit(solution)/shard_map/pallas_call | solution.py:283
  56.8 1.2 collective-permute-done.10.a
  58.0 0.1 shard_map.52
  58.1 0.1 collective-permute-start.12
  58.2 2.7 %collective-permute-start.13 = (bf16[80,2560]{1,0:T(8,128)(2,1)S(1)}, bf16[80,2560]{1,0:T(8,128)(2,1)S(1)}, u32[]{:S(2)}, u32[]{:S(2)}) collective-permute-start(bf16[80,2560]{1,0:T(8,128)(2,1)S(1)} %get-tuple-element.45), channel_id=1, source_target_pairs={{8,0},{16,8},{24,16},{0,24},{9,1},{17,9},{25,17},{1,25},{10,2},{18... | collective-permute-start | bytes 1228808 | tf_op jit(solution)/shard_map/ppermute | solution.py:22
  60.8 5.3 %collective-permute-done.12.e = bf16[80,2560]{1,0:T(8,128)(2,1)S(1)} collective-permute-done((bf16[80,2560]{1,0:T(8,128)(2,1)S(1)}, bf16[80,2560]{1,0:T(8,128)(2,1)S(1)}, u32[]{:S(2)}, u32[]{:S(2)}) %collective-permute-start.12) | collective-permute-done | bytes 409632 | tf_op jit(solution)/shard_map/ppermute | solution.py:22
  66.2 0.2 shard_map.53
  66.4 5.5 %collective-permute-start.14 = (bf16[2560,512]{1,0:T(8,128)(2,1)S(1)}, bf16[2560,512]{1,0:T(8,128)(2,1)S(1)}, u32[]{:S(2)}, u32[]{:S(2)}) collective-permute-start(bf16[2560,512]{1,0:T(8,128)(2,1)S(1)} %get-tuple-element.50), channel_id=1, source_target_pairs={{1,0},{0,1},{3,2},{2,3},{5,4},{4,5},{7,6},{6,7},{9,8},{8,9},{11,10... | collective-permute-start | bytes 7864328 | tf_op jit(solution)/shard_map/ppermute | solution.py:26
  71.9 1.8 %collective-permute-start.17 = (bf16[80,640]{1,0:T(8,128)(2,1)S(1)}, bf16[80,640]{1,0:T(8,128)(2,1)S(1)}, u32[]{:S(2)}, u32[]{:S(2)}) collective-permute-start(bf16[80,640]{1,0:T(8,128)(2,1)S(1)} %get-tuple-element.55), channel_id=1, source_target_pairs={{6,0},{0,2},{2,4},{4,6},{7,1},{1,3},{3,5},{5,7},{14,8},{8,10},{10,... | collective-permute-start | bytes 307208 | tf_op jit(solution)/shard_map/ppermute | solution.py:22
  73.7 4.8 %collective-permute-start.16 = (bf16[80,640]{1,0:T(8,128)(2,1)S(1)}, bf16[80,640]{1,0:T(8,128)(2,1)S(1)}, u32[]{:S(2)}, u32[]{:S(2)}) collective-permute-start(bf16[80,640]{1,0:T(8,128)(2,1)S(1)} %get-tuple-element.54), channel_id=1, source_target_pairs={{4,0},{6,2},{0,4},{2,6},{5,1},{7,3},{1,5},{3,7},{12,8},{14,10},{8,... | collective-permute-start | bytes 307208 | tf_op jit(solution)/shard_map/ppermute | solution.py:22
  78.5 2.4 %collective-permute-start.18 = (bf16[80,640]{1,0:T(8,128)(2,1)S(1)}, bf16[80,640]{1,0:T(8,128)(2,1)S(1)}, u32[]{:S(2)}, u32[]{:S(2)}) collective-permute-start(bf16[80,640]{1,0:T(8,128)(2,1)S(1)} %get-tuple-element.56), channel_id=1, source_target_pairs={{2,0},{4,2},{6,4},{0,6},{3,1},{5,3},{7,5},{1,7},{10,8},{12,10},{14... | collective-permute-start | bytes 307208 | tf_op jit(solution)/shard_map/ppermute | solution.py:22
  80.9 0.9 collective-permute-start.15
  81.8 0.8 collective-permute-done.15.inv_o
  82.6 1.1 shard_map.54
  83.7 2.1 %collective-permute-done.16.r1 = bf16[80,640]{1,0:T(8,128)(2,1)S(1)} collective-permute-done((bf16[80,640]{1,0:T(8,128)(2,1)S(1)}, bf16[80,640]{1,0:T(8,128)(2,1)S(1)}, u32[]{:S(2)}, u32[]{:S(2)}) %collective-permute-start.16) | collective-permute-done | bytes 102432 | tf_op jit(solution)/shard_map/ppermute | solution.py:22
  85.9 3.0 %collective-permute-done.18.r3 = bf16[80,640]{1,0:T(8,128)(2,1)S(1)} collective-permute-done((bf16[80,640]{1,0:T(8,128)(2,1)S(1)}, bf16[80,640]{1,0:T(8,128)(2,1)S(1)}, u32[]{:S(2)}, u32[]{:S(2)}) %collective-permute-start.18) | collective-permute-done | bytes 102432 | tf_op jit(solution)/shard_map/ppermute | solution.py:22
  88.8 0.1 shard_map.55.mine
  88.9 0.6 collective-permute-start.19
  89.5 0.9 collective-permute-done.19.theirs
  90.4 0.1 shard_map.56.own
  90.6 1.5 %collective-permute-start.20 = (bf16[80,768]{1,0:T(8,128)(2,1)S(1)}, bf16[80,768]{1,0:T(8,128)(2,1)S(1)}, u32[]{:S(2)}, u32[]{:S(2)}) collective-permute-start(bf16[80,768]{1,0:T(8,128)(2,1)S(1)} %shard_map.56.own), channel_id=1, source_target_pairs={{6,0},{0,2},{2,4},{4,6},{7,1},{1,3},{3,5},{5,7},{14,8},{8,10},{10,... | collective-permute-start | bytes 368648 | tf_op jit(solution)/shard_map/ppermute | solution.py:22
  92.0 2.2 %collective-permute-start.21 = (bf16[80,768]{1,0:T(8,128)(2,1)S(1)}, bf16[80,768]{1,0:T(8,128)(2,1)S(1)}, u32[]{:S(2)}, u32[]{:S(2)}) collective-permute-start(bf16[80,768]{1,0:T(8,128)(2,1)S(1)} %shard_map.56.own), channel_id=1, source_target_pairs={{2,0},{4,2},{6,4},{0,6},{3,1},{5,3},{7,5},{1,7},{10,8},{12,10},{14... | collective-permute-start | bytes 368648 | tf_op jit(solution)/shard_map/ppermute | solution.py:22
  94.2 5.7 %collective-permute-done.20.r1 = bf16[80,768]{1,0:T(8,128)(2,1)S(1)} collective-permute-done((bf16[80,768]{1,0:T(8,128)(2,1)S(1)}, bf16[80,768]{1,0:T(8,128)(2,1)S(1)}, u32[]{:S(2)}, u32[]{:S(2)}) %collective-permute-start.20) | collective-permute-done | bytes 122912 | tf_op jit(solution)/shard_map/ppermute | solution.py:22
  99.9 0.3 collective-permute-start.22
  100.2 0.7 collective-permute-done.21.r3
  100.9 2.6 %collective-permute-start.23 = (bf16[32,768]{1,0:T(8,128)(2,1)S(1)}, bf16[32,768]{1,0:T(8,128)(2,1)S(1)}, u32[]{:S(2)}, u32[]{:S(2)}) collective-permute-start(bf16[32,768]{1,0:T(8,128)(2,1)S(1)} %slice.31), channel_id=1, source_target_pairs={{2,0},{4,2},{6,4},{0,6},{3,1},{5,3},{7,5},{1,7},{10,8},{12,10},{14... | collective-permute-start | bytes 147464 | tf_op jit(solution)/shard_map/ppermute | solution.py:22
  103.6 1.4 %collective-permute-done.23.r2hi = bf16[32,768]{1,0:T(8,128)(2,1)S(1)} collective-permute-done((bf16[32,768]{1,0:T(8,128)(2,1)S(1)}, bf16[32,768]{1,0:T(8,128)(2,1)S(1)}, u32[]{:S(2)}, u32[]{:S(2)}) %collective-permute-start.23) | collective-permute-done | bytes 49184 | tf_op jit(solution)/shard_map/ppermute | solution.py:22
  105.0 0.3 collective-permute-done.22.r2lo
  105.2 0.1 shard_map.57.own
  105.3 1.2 collective-permute-start.24
  106.5 2.1 %collective-permute-start.25 = (bf16[80,2688]{1,0:T(8,128)(2,1)S(1)}, bf16[80,2688]{1,0:T(8,128)(2,1)S(1)}, u32[]{:S(2)}, u32[]{:S(2)}) collective-permute-start(bf16[80,2688]{1,0:T(8,128)(2,1)S(1)} %shard_map.57.own), channel_id=1, source_target_pairs={{8,0},{16,8},{24,16},{0,24},{9,1},{17,9},{25,17},{1,25},{10,2},{18... | collective-permute-start | bytes 1290248 | tf_op jit(solution)/shard_map/ppermute | solution.py:22
  108.7 8.0 %collective-permute-done.24.r1 = bf16[80,2688]{1,0:T(8,128)(2,1)S(1)} collective-permute-done((bf16[80,2688]{1,0:T(8,128)(2,1)S(1)}, bf16[80,2688]{1,0:T(8,128)(2,1)S(1)}, u32[]{:S(2)}, u32[]{:S(2)}) %collective-permute-start.24) | collective-permute-done | bytes 430112 | tf_op jit(solution)/shard_map/ppermute | solution.py:22
  116.7 0.1 collective-permute-start.26
  116.8 2.7 %collective-permute-start.27 = (bf16[32,2688]{1,0:T(8,128)(2,1)S(1)}, bf16[32,2688]{1,0:T(8,128)(2,1)S(1)}, u32[]{:S(2)}, u32[]{:S(2)}) collective-permute-start(bf16[32,2688]{1,0:T(8,128)(2,1)S(1)} %slice.33), channel_id=1, source_target_pairs={{8,0},{16,8},{24,16},{0,24},{9,1},{17,9},{25,17},{1,25},{10,2},{18... | collective-permute-start | bytes 516104 | tf_op jit(solution)/shard_map/ppermute | solution.py:22
  119.5 1.5 %shard_map.58 = (f32[240,512]{1,0:T(8,128)S(1)}, f32[240,512]{1,0:T(8,128)S(1)}, f32[8,1024]{1,0:T(8,128)S(1)}) custom-call(bf16[80,2688]{1,0:T(8,128)(2,1)S(1)} %shard_map.57.own, bf16[80,2688]{1,0:T(8,128)(2,1)S(1)} %collective-permute-done.24.r1, bf16[80,2688]{1,0:T(8,128)(2,1)S(1)} %collective-permute-done.25.r3, bf16[2560,1024]{1,0:T(8,128)(2,1)S(1)} %get-tuple-element.38.n), custom_call_target="tpu_custom_call" | custom-call | tf_op jit(solution)/shard_map/pallas_call | solution.py:283
  121.1 0.8 collective-permute-done.27.r2hi
  121.9 1.3 collective-permute-done.26.r2lo
  123.1 1.1 shard_map.59
  124.3 3.8 %collective-permute-start.28 = (f32[320,512]{1,0:T(8,128)S(1)}, f32[320,512]{1,0:T(8,128)S(1)}, u32[]{:S(2)}, u32[]{:S(2)}) collective-permute-start(f32[320,512]{1,0:T(8,128)S(1)} %get-tuple-element.61), channel_id=1, source_target_pairs={{1,0},{0,1},{3,2},{2,3},{5,4},{4,5},{7,6},{6,7},{9,8},{8,9},{11,10... | collective-permute-start | bytes 1966088 | tf_op jit(solution)/shard_map/ppermute | solution.py:26
  128.0 9.2 %all_to_all.5.sums = f32[16,1,1152]{2,1,0:T(1,128)S(1)} all-to-all(f32[16,1,1152]{2,1,0:T(1,128)S(1)} %get-tuple-element.64), channel_id=1, replica_groups=mesh['y'=4,'zl'=2,'x'=4,'zh'=4,'core'=2] {'y','zl','core'}, dimensions={0} | all-to-all | bytes 147456 | tf_op jit(solution)/shard_map/all_to_all | solution.py:371
  137.2 1.7 %shard_map.60 = (f32[1,1]{1,0:T(1,128)}, f32[320,512]{1,0:T(8,128)}, f32[320,512]{1,0:T(8,128)}) custom-call(f32[240,512]{1,0:T(8,128)S(1)} %get-tuple-element.57.my3, f32[80,512]{1,0:T(8,128)S(1)} %get-tuple-element.60.my1, f32[320,512]{1,0:T(8,128)S(1)} %collective-permute-done.28.swapped, bf16[320,512]{1,0:T(8,128)(2,1)S(1)} %get-tuple-element.62.my_own, ...), custom_call_target="tpu_custom_call" | custom-call | tf_op jit(solution)/shard_map/pallas_call | solution.py:283
  (16 shorter events, 0.1 us)
Async XLA Ops:
  1.8 4.6 %collective-permute-start = (bf16[320,512]{1,0:T(8,128)(2,1)S(1)}, bf16[320,512]{1,0:T(8,128)(2,1)S(1)}, u32[]{:S(2)}, u32[]{:S(2)}) collective-permute-start(bf16[320,512]{1,0:T(8,128)(2,1)S(1)} %get-tuple-element.70), channel_id=1, source_target_pairs={{1,0},{0,1},{3,2},{2,3},{5,4},{4,5},{7,6},{6,7},{9,8},{8,9},{11,10... | collective-permute-start | bytes 983048 | tf_op jit(solution)/shard_map/ppermute | solution.py:26
  6.4 17.2 %collective-permute-start.3 = (bf16[320,1024]{1,0:T(8,128)(2,1)S(1)}, bf16[320,1024]{1,0:T(8,128)(2,1)S(1)}, u32[]{:S(2)}, u32[]{:S(2)}) collective-permute-start(bf16[320,1024]{1,0:T(8,128)(2,1)S(1)} %pad_maximum_fusion.own), channel_id=1, source_target_pairs={{192,0},{0,64},{64,128},{128,192},{193,1},{1,65},{65,129},{129,193... | collective-permute-start | bytes 1966088 | tf_op jit(solution)/shard_map/ppermute | solution.py:22
  6.5 17.3 %collective-permute-start.2 = (bf16[320,1024]{1,0:T(8,128)(2,1)S(1)}, bf16[320,1024]{1,0:T(8,128)(2,1)S(1)}, u32[]{:S(2)}, u32[]{:S(2)}) collective-permute-start(bf16[320,1024]{1,0:T(8,128)(2,1)S(1)} %pad_maximum_fusion.own), channel_id=1, source_target_pairs={{64,0},{128,64},{192,128},{0,192},{65,1},{129,65},{193,129},{1,193... | collective-permute-start | bytes 1966088 | tf_op jit(solution)/shard_map/ppermute | solution.py:22
  9.2 17.4 %collective-permute-start.1 = (bf16[320,1024]{1,0:T(8,128)(2,1)S(1)}, bf16[320,1024]{1,0:T(8,128)(2,1)S(1)}, u32[]{:S(2)}, u32[]{:S(2)}) collective-permute-start(bf16[320,1024]{1,0:T(8,128)(2,1)S(1)} %pad_maximum_fusion.own), channel_id=1, source_target_pairs={{32,0},{0,32},{33,1},{1,33},{34,2},{2,34},{35,3},{3,35},{36,4},{4,... | collective-permute-start | bytes 1966088 | tf_op jit(solution)/shard_map/ppermute | solution.py:26
  23.7 9.3 %collective-permute-start.5 = (bf16[160,1024]{1,0:T(8,128)(2,1)S(1)}, bf16[160,1024]{1,0:T(8,128)(2,1)S(1)}, u32[]{:S(2)}, u32[]{:S(2)}) collective-permute-start(bf16[160,1024]{1,0:T(8,128)(2,1)S(1)} %slice.29), channel_id=1, source_target_pairs={{192,0},{0,64},{64,128},{128,192},{193,1},{1,65},{65,129},{129,193... | collective-permute-start | bytes 983048 | tf_op jit(solution)/shard_map/ppermute | solution.py:22
  23.8 9.3 %collective-permute-start.4 = (bf16[160,1024]{1,0:T(8,128)(2,1)S(1)}, bf16[160,1024]{1,0:T(8,128)(2,1)S(1)}, u32[]{:S(2)}, u32[]{:S(2)}) collective-permute-start(bf16[160,1024]{1,0:T(8,128)(2,1)S(1)} %slice.28), channel_id=1, source_target_pairs={{64,0},{128,64},{192,128},{0,192},{65,1},{129,65},{193,129},{1,193... | collective-permute-start | bytes 983048 | tf_op jit(solution)/shard_map/ppermute | solution.py:22
  26.5 20.5 %collective-permute-start.7 = (bf16[320,1024]{1,0:T(8,128)(2,1)S(1)}, bf16[320,1024]{1,0:T(8,128)(2,1)S(1)}, u32[]{:S(2)}, u32[]{:S(2)}) collective-permute-start(bf16[320,1024]{1,0:T(8,128)(2,1)S(1)} %collective-permute-done.1.refs_0_), channel_id=1, source_target_pairs={{192,0},{0,64},{64,128},{128,192},{193,1},{1,65},{65,129},{129,193... | collective-permute-start | bytes 1966088 | tf_op jit(solution)/shard_map/ppermute | solution.py:22
  26.6 20.5 %collective-permute-start.6 = (bf16[320,1024]{1,0:T(8,128)(2,1)S(1)}, bf16[320,1024]{1,0:T(8,128)(2,1)S(1)}, u32[]{:S(2)}, u32[]{:S(2)}) collective-permute-start(bf16[320,1024]{1,0:T(8,128)(2,1)S(1)} %collective-permute-done.1.refs_0_), channel_id=1, source_target_pairs={{64,0},{128,64},{192,128},{0,192},{65,1},{129,65},{193,129},{1,193... | collective-permute-start | bytes 1966088 | tf_op jit(solution)/shard_map/ppermute | solution.py:22
  33.0 6.2 %collective-permute-start.9 = (bf16[160,1024]{1,0:T(8,128)(2,1)S(1)}, bf16[160,1024]{1,0:T(8,128)(2,1)S(1)}, u32[]{:S(2)}, u32[]{:S(2)}) collective-permute-start(bf16[160,1024]{1,0:T(8,128)(2,1)S(1)} %collective-permute-done.5.refs_4_), channel_id=1, source_target_pairs={{32,0},{0,32},{33,1},{1,33},{34,2},{2,34},{35,3},{3,35},{36,4},{4,... | collective-permute-start | bytes 983048 | tf_op jit(solution)/shard_map/ppermute | solution.py:26
  33.1 12.3 %collective-permute-start.8 = (bf16[160,1024]{1,0:T(8,128)(2,1)S(1)}, bf16[160,1024]{1,0:T(8,128)(2,1)S(1)}, u32[]{:S(2)}, u32[]{:S(2)}) collective-permute-start(bf16[160,1024]{1,0:T(8,128)(2,1)S(1)} %collective-permute-done.4.refs_3_), channel_id=1, source_target_pairs={{32,0},{0,32},{33,1},{1,33},{34,2},{2,34},{35,3},{3,35},{36,4},{4,... | collective-permute-start | bytes 983048 | tf_op jit(solution)/shard_map/ppermute | solution.py:26
  51.6 6.3 %collective-permute-start.10 = (bf16[48,2560]{1,0:T(8,128)(2,1)S(1)}, bf16[48,2560]{1,0:T(8,128)(2,1)S(1)}, u32[]{:S(2)}, u32[]{:S(2)}) collective-permute-start(bf16[48,2560]{1,0:T(8,128)(2,1)S(1)} %get-tuple-element.41), channel_id=1, source_target_pairs={{24,0},{0,8},{8,16},{16,24},{25,1},{1,9},{9,17},{17,25},{26,2},{2,... | collective-permute-start | bytes 737288 | tf_op jit(solution)/shard_map/ppermute | solution.py:22
  51.7 5.0 %collective-permute-start.11 = (bf16[32,2560]{1,0:T(8,128)(2,1)S(1)}, bf16[32,2560]{1,0:T(8,128)(2,1)S(1)}, u32[]{:S(2)}, u32[]{:S(2)}) collective-permute-start(bf16[32,2560]{1,0:T(8,128)(2,1)S(1)} %get-tuple-element.43), channel_id=1, source_target_pairs={{8,0},{16,8},{24,16},{0,24},{9,1},{17,9},{25,17},{1,25},{10,2},{18... | collective-permute-start | bytes 491528 | tf_op jit(solution)/shard_map/ppermute | solution.py:22
  58.1 8.1 %collective-permute-start.12 = (bf16[80,2560]{1,0:T(8,128)(2,1)S(1)}, bf16[80,2560]{1,0:T(8,128)(2,1)S(1)}, u32[]{:S(2)}, u32[]{:S(2)}) collective-permute-start(bf16[80,2560]{1,0:T(8,128)(2,1)S(1)} %get-tuple-element.44), channel_id=1, source_target_pairs={{24,0},{0,8},{8,16},{16,24},{25,1},{1,9},{9,17},{17,25},{26,2},{2,... | collective-permute-start | bytes 1228808 | tf_op jit(solution)/shard_map/ppermute | solution.py:22
  58.2 8.0 %collective-permute-start.13 = (bf16[80,2560]{1,0:T(8,128)(2,1)S(1)}, bf16[80,2560]{1,0:T(8,128)(2,1)S(1)}, u32[]{:S(2)}, u32[]{:S(2)}) collective-permute-start(bf16[80,2560]{1,0:T(8,128)(2,1)S(1)} %get-tuple-element.45), channel_id=1, source_target_pairs={{8,0},{16,8},{24,16},{0,24},{9,1},{17,9},{25,17},{1,25},{10,2},{18... | collective-permute-start | bytes 1228808 | tf_op jit(solution)/shard_map/ppermute | solution.py:22
  66.4 16.2 %collective-permute-start.14 = (bf16[2560,512]{1,0:T(8,128)(2,1)S(1)}, bf16[2560,512]{1,0:T(8,128)(2,1)S(1)}, u32[]{:S(2)}, u32[]{:S(2)}) collective-permute-start(bf16[2560,512]{1,0:T(8,128)(2,1)S(1)} %get-tuple-element.50), channel_id=1, source_target_pairs={{1,0},{0,1},{3,2},{2,3},{5,4},{4,5},{7,6},{6,7},{9,8},{8,9},{11,10... | collective-permute-start | bytes 7864328 | tf_op jit(solution)/shard_map/ppermute | solution.py:26
  71.9 11.8 %collective-permute-start.17 = (bf16[80,640]{1,0:T(8,128)(2,1)S(1)}, bf16[80,640]{1,0:T(8,128)(2,1)S(1)}, u32[]{:S(2)}, u32[]{:S(2)}) collective-permute-start(bf16[80,640]{1,0:T(8,128)(2,1)S(1)} %get-tuple-element.55), channel_id=1, source_target_pairs={{6,0},{0,2},{2,4},{4,6},{7,1},{1,3},{3,5},{5,7},{14,8},{8,10},{10,... | collective-permute-start | bytes 307208 | tf_op jit(solution)/shard_map/ppermute | solution.py:22
  73.7 12.2 %collective-permute-start.16 = (bf16[80,640]{1,0:T(8,128)(2,1)S(1)}, bf16[80,640]{1,0:T(8,128)(2,1)S(1)}, u32[]{:S(2)}, u32[]{:S(2)}) collective-permute-start(bf16[80,640]{1,0:T(8,128)(2,1)S(1)} %get-tuple-element.54), channel_id=1, source_target_pairs={{4,0},{6,2},{0,4},{2,6},{5,1},{7,3},{1,5},{3,7},{12,8},{14,10},{8,... | collective-permute-start | bytes 307208 | tf_op jit(solution)/shard_map/ppermute | solution.py:22
  78.5 10.4 %collective-permute-start.18 = (bf16[80,640]{1,0:T(8,128)(2,1)S(1)}, bf16[80,640]{1,0:T(8,128)(2,1)S(1)}, u32[]{:S(2)}, u32[]{:S(2)}) collective-permute-start(bf16[80,640]{1,0:T(8,128)(2,1)S(1)} %get-tuple-element.56), channel_id=1, source_target_pairs={{2,0},{4,2},{6,4},{0,6},{3,1},{5,3},{7,5},{1,7},{10,8},{12,10},{14... | collective-permute-start | bytes 307208 | tf_op jit(solution)/shard_map/ppermute | solution.py:22
  80.9 1.8 %collective-permute-start.15 = (f32[8,512]{1,0:T(8,128)S(1)}, f32[8,512]{1,0:T(8,128)S(1)}, u32[]{:S(2)}, u32[]{:S(2)}) collective-permute-start(f32[8,512]{1,0:T(8,128)S(1)} %slice.23), channel_id=1, source_target_pairs={{1,0},{0,1},{3,2},{2,3},{5,4},{4,5},{7,6},{6,7},{9,8},{8,9},{11,10... | collective-permute-start | bytes 49160 | tf_op jit(solution)/shard_map/ppermute | solution.py:26
  88.9 1.5 %collective-permute-start.19 = (bf16[80,640]{1,0:T(8,128)(2,1)S(1)}, bf16[80,640]{1,0:T(8,128)(2,1)S(1)}, u32[]{:S(2)}, u32[]{:S(2)}) collective-permute-start(bf16[80,640]{1,0:T(8,128)(2,1)S(1)} %shard_map.55.mine), channel_id=1, source_target_pairs={{1,0},{0,1},{3,2},{2,3},{5,4},{4,5},{7,6},{6,7},{9,8},{8,9},{11,10... | collective-permute-start | bytes 307208 | tf_op jit(solution)/shard_map/ppermute | solution.py:26
  90.6 9.3 %collective-permute-start.20 = (bf16[80,768]{1,0:T(8,128)(2,1)S(1)}, bf16[80,768]{1,0:T(8,128)(2,1)S(1)}, u32[]{:S(2)}, u32[]{:S(2)}) collective-permute-start(bf16[80,768]{1,0:T(8,128)(2,1)S(1)} %shard_map.56.own), channel_id=1, source_target_pairs={{6,0},{0,2},{2,4},{4,6},{7,1},{1,3},{3,5},{5,7},{14,8},{8,10},{10,... | collective-permute-start | bytes 368648 | tf_op jit(solution)/shard_map/ppermute | solution.py:22
  92.0 8.9 %collective-permute-start.21 = (bf16[80,768]{1,0:T(8,128)(2,1)S(1)}, bf16[80,768]{1,0:T(8,128)(2,1)S(1)}, u32[]{:S(2)}, u32[]{:S(2)}) collective-permute-start(bf16[80,768]{1,0:T(8,128)(2,1)S(1)} %shard_map.56.own), channel_id=1, source_target_pairs={{2,0},{4,2},{6,4},{0,6},{3,1},{5,3},{7,5},{1,7},{10,8},{12,10},{14... | collective-permute-start | bytes 368648 | tf_op jit(solution)/shard_map/ppermute | solution.py:22
  99.9 5.3 %collective-permute-start.22 = (bf16[48,768]{1,0:T(8,128)(2,1)S(1)}, bf16[48,768]{1,0:T(8,128)(2,1)S(1)}, u32[]{:S(2)}, u32[]{:S(2)}) collective-permute-start(bf16[48,768]{1,0:T(8,128)(2,1)S(1)} %slice.30), channel_id=1, source_target_pairs={{6,0},{0,2},{2,4},{4,6},{7,1},{1,3},{3,5},{5,7},{14,8},{8,10},{10,... | collective-permute-start | bytes 221192 | tf_op jit(solution)/shard_map/ppermute | solution.py:22
  100.9 4.0 %collective-permute-start.23 = (bf16[32,768]{1,0:T(8,128)(2,1)S(1)}, bf16[32,768]{1,0:T(8,128)(2,1)S(1)}, u32[]{:S(2)}, u32[]{:S(2)}) collective-permute-start(bf16[32,768]{1,0:T(8,128)(2,1)S(1)} %slice.31), channel_id=1, source_target_pairs={{2,0},{4,2},{6,4},{0,6},{3,1},{5,3},{7,5},{1,7},{10,8},{12,10},{14... | collective-permute-start | bytes 147464 | tf_op jit(solution)/shard_map/ppermute | solution.py:22
  105.3 11.3 %collective-permute-start.24 = (bf16[80,2688]{1,0:T(8,128)(2,1)S(1)}, bf16[80,2688]{1,0:T(8,128)(2,1)S(1)}, u32[]{:S(2)}, u32[]{:S(2)}) collective-permute-start(bf16[80,2688]{1,0:T(8,128)(2,1)S(1)} %shard_map.57.own), channel_id=1, source_target_pairs={{24,0},{0,8},{8,16},{16,24},{25,1},{1,9},{9,17},{17,25},{26,2},{2,... | collective-permute-start | bytes 1290248 | tf_op jit(solution)/shard_map/ppermute | solution.py:22
  106.5 10.3 %collective-permute-start.25 = (bf16[80,2688]{1,0:T(8,128)(2,1)S(1)}, bf16[80,2688]{1,0:T(8,128)(2,1)S(1)}, u32[]{:S(2)}, u32[]{:S(2)}) collective-permute-start(bf16[80,2688]{1,0:T(8,128)(2,1)S(1)} %shard_map.57.own), channel_id=1, source_target_pairs={{8,0},{16,8},{24,16},{0,24},{9,1},{17,9},{25,17},{1,25},{10,2},{18... | collective-permute-start | bytes 1290248 | tf_op jit(solution)/shard_map/ppermute | solution.py:22
  116.7 6.5 %collective-permute-start.26 = (bf16[48,2688]{1,0:T(8,128)(2,1)S(1)}, bf16[48,2688]{1,0:T(8,128)(2,1)S(1)}, u32[]{:S(2)}, u32[]{:S(2)}) collective-permute-start(bf16[48,2688]{1,0:T(8,128)(2,1)S(1)} %slice.32), channel_id=1, source_target_pairs={{24,0},{0,8},{8,16},{16,24},{25,1},{1,9},{9,17},{17,25},{26,2},{2,... | collective-permute-start | bytes 774152 | tf_op jit(solution)/shard_map/ppermute | solution.py:22
  116.8 5.1 %collective-permute-start.27 = (bf16[32,2688]{1,0:T(8,128)(2,1)S(1)}, bf16[32,2688]{1,0:T(8,128)(2,1)S(1)}, u32[]{:S(2)}, u32[]{:S(2)}) collective-permute-start(bf16[32,2688]{1,0:T(8,128)(2,1)S(1)} %slice.33), channel_id=1, source_target_pairs={{8,0},{16,8},{24,16},{0,24},{9,1},{17,9},{25,17},{1,25},{10,2},{18... | collective-permute-start | bytes 516104 | tf_op jit(solution)/shard_map/ppermute | solution.py:22
  124.3 13.0 %collective-permute-start.28 = (f32[320,512]{1,0:T(8,128)S(1)}, f32[320,512]{1,0:T(8,128)S(1)}, u32[]{:S(2)}, u32[]{:S(2)}) collective-permute-start(f32[320,512]{1,0:T(8,128)S(1)} %get-tuple-element.61), channel_id=1, source_target_pairs={{1,0},{0,1},{3,2},{2,3},{5,4},{4,5},{7,6},{6,7},{9,8},{8,9},{11,10... | collective-permute-start | bytes 1966088 | tf_op jit(solution)/shard_map/ppermute | solution.py:26
